TPU v7x, 32 devices: a whole 2x2x4 slice. The times are simulated.
32 devices in a mesh: ctx: 8 (over y, x, core), wt: 4 (over z).
Axes of the slice: x: 2, y: 2, z: 4, core: 2. Of those that a mesh axis runs over, the one named last changes fastest.
Arguments:
- tokens: bfloat16 [2048, 576], P('ctx'), may hold values from -6 to 6
- w_query: bfloat16 [576, 576], replicated, may hold values from -0.25 to 0.25
- w_key: bfloat16 [576, 192], replicated, may hold values from -0.25 to 0.25
- w_value: bfloat16 [576, 192], replicated, may hold values from -0.25 to 0.25
- w_out: bfloat16 [576, 576], replicated, may hold values from -1.5 to 1.5
- norm_attn: bfloat16 [576], replicated, may hold values from 0.5 to 1.5
- norm_mlp: bfloat16 [576], replicated, may hold values from 0.5 to 1.5
- w_gate: bfloat16 [576, 1536], P(None, 'wt'), may hold values from -0.25 to 0.25
- w_up: bfloat16 [576, 1536], P(None, 'wt'), may hold values from -0.25 to 0.25
- w_down: bfloat16 [1536, 576], P('wt'), may hold values from -0.15625 to 0.15625
- stretch_order: int32 [1, 16], replicated, may hold values from 0 to 15, as said below
- cotangent: bfloat16 [2048, 576], P('ctx'), may hold values from -6 to 6
Outputs:
- output: bfloat16 [2048, 576], P('ctx')
- grad_tokens: float32 [2048, 576], P('ctx')
- grad_query: float32 [576, 576], replicated
- grad_key: float32 [576, 192], replicated
- grad_value: float32 [576, 192], replicated
- grad_out: float32 [576, 576], replicated
- grad_norm_attn: float32 [576], replicated
- grad_norm_mlp: float32 [576], replicated
- grad_gate: float32 [576, 1536], P(None, 'wt')
- grad_up: float32 [576, 1536], P(None, 'wt')
- grad_down: float32 [1536, 576], P('wt')
Inputs may be any that keep to these rules, and one draw needn't show every extreme that they name: `stretch_order`: for every sequence, slots 2 j and 2 j + 1 hold stretches c and 15 - c with c < 8; every stretch stands once.
All inputs are finite; a program needn't handle non-finite values.
Results may differ from a plain program's by a relative error of at most 0.019.
Values may be sent and summed in bfloat16 or wider, within the bound.
No kernel may reach another device: no remote copies, remote signals or barrier semaphores. Data moves between devices by JAX's collectives and lax.ppermute only.
A program may use at most 128 MiB of HBM per device.

v0:
```python
import jax
import jax.numpy as jnp
from jax import lax
from jax.sharding import PartitionSpec as P

Q_HEADS = 9
KV_HEADS = 3
HEAD = 64


EPSILON = 1e-05
THETA = 100000.0
NEGATIVE = -1e30


def rms_norm(values, gain):
    return values * lax.rsqrt(jnp.mean(values * values, axis=-1, keepdims=True) + EPSILON) * gain


def rotate(values, places):
    half = values.shape[-1] // 2
    rates = THETA ** (-jnp.arange(half, dtype=jnp.float32) / half)
    angle = places.astype(jnp.float32)[:, None] * rates[None, :]
    cosine = jnp.cos(angle)[:, None, :]
    sine = jnp.sin(angle)[:, None, :]
    first = values[..., :half]
    second = values[..., half:]
    return jnp.concatenate(
        [first * cosine - second * sine, second * cosine + first * sine], axis=-1
    )


def matmul(left, right):
    return jnp.dot(left, right, preferred_element_type=jnp.float32)


def matmul_nt(left, right):
    return lax.dot_general(
        left, right, (((1,), (1,)), ((), ())), preferred_element_type=jnp.float32
    )


def matmul_tn(left, right):
    return lax.dot_general(
        left, right, (((0,), (0,)), ((), ())), preferred_element_type=jnp.float32
    )


def slot_places(stretch_order, device, stretch):
    pair = lax.dynamic_slice_in_dim(stretch_order, 2 * device, 2, 1)
    offsets = jnp.arange(stretch, dtype=jnp.int32)
    return (pair[:, :, None] * stretch + offsets[None, None, :]).reshape(pair.shape[0], 2 * stretch)


def to_groups(flat, seq_count, group):
    span = flat.shape[0] // seq_count
    split = flat.reshape(seq_count, span, KV_HEADS, group, HEAD)
    return split.transpose(0, 2, 1, 3, 4).reshape(seq_count, KV_HEADS, span * group, HEAD)


def from_groups(grouped, group):
    seq_count = grouped.shape[0]
    span = grouped.shape[2] // group
    split = grouped.reshape(seq_count, KV_HEADS, span, group, HEAD)
    return split.transpose(0, 2, 1, 3, 4).reshape(seq_count * span, KV_HEADS * group * HEAD)


def split_keys(block, seq_count):
    parts = block.reshape(seq_count, block.shape[0] // seq_count, 2, KV_HEADS, HEAD)
    return (parts[:, :, 0].transpose(0, 2, 1, 3), parts[:, :, 1].transpose(0, 2, 1, 3))


def join_keys(key_part, value_part):
    both = jnp.stack([key_part, value_part], axis=1)
    seq_count = both.shape[0]
    span = both.shape[3]
    return both.transpose(0, 3, 1, 2, 4).reshape(seq_count * span, 2 * KV_HEADS * HEAD)


def local(
    tokens,
    w_query,
    w_key,
    w_value,
    w_out,
    norm_attn,
    norm_mlp,
    w_gate,
    w_up,
    w_down,
    stretch_order,
    cotangent,
):
    row_count = tokens.shape[0]
    seq_count = stretch_order.shape[0]
    stretch = row_count // (2 * seq_count)
    group = Q_HEADS // KV_HEADS
    key_width = KV_HEADS * HEAD
    scale = HEAD ** (-0.5)
    device = lax.axis_index("ctx")
    own_places = slot_places(stretch_order, device, stretch)
    query_places = jnp.repeat(own_places, group, axis=1)
    flat_places = own_places.reshape(row_count)
    inputs = tokens.astype(jnp.float32)
    normed_f, norm_attn_back = jax.vjp(rms_norm, inputs, norm_attn.astype(jnp.float32))
    normed = normed_f.astype(jnp.bfloat16)

    def rope_query(values):
        return rotate(values.reshape(row_count, Q_HEADS, HEAD), flat_places).reshape(
            row_count, Q_HEADS * HEAD
        )

    def rope_key(values):
        return rotate(values.reshape(row_count, KV_HEADS, HEAD), flat_places).reshape(
            row_count, key_width
        )

    query_rot, rope_query_back = jax.vjp(rope_query, matmul(normed, w_query))
    key_rot, rope_key_back = jax.vjp(rope_key, matmul(normed, w_key))
    values = matmul(normed, w_value).astype(jnp.bfloat16)
    keys_values = jnp.concatenate([key_rot.astype(jnp.bfloat16), values], axis=1)
    query_groups = to_groups(query_rot.astype(jnp.bfloat16), seq_count, group)

    def masked_scores(key_part, places):
        score = (
            jnp.einsum(
                "sgqd,sgkd->sgqk", query_groups, key_part, preferred_element_type=jnp.float32
            )
            * scale
        )
        seen = places[:, None, None, :] <= query_places[:, None, :, None]
        return (score, seen)

    def attend_block(carry, block, index):
        top, total, running = carry
        key_part, value_part = split_keys(block, seq_count)
        score, seen = masked_scores(key_part, slot_places(stretch_order, index, stretch))
        score = jnp.where(seen, score, NEGATIVE)
        new_top = jnp.maximum(top, jnp.max(score, axis=-1))
        fade = jnp.exp(top - new_top)
        weight = jnp.where(seen, jnp.exp(score - new_top[..., None]), 0.0)
        total = total * fade + jnp.sum(weight, axis=-1)
        running = running * fade[..., None] + jnp.einsum(
            "sgqk,sgkd->sgqd",
            weight.astype(jnp.bfloat16),
            value_part,
            preferred_element_type=jnp.float32,
        )
        return (new_top, total, running)

    stat_shape = (seq_count, KV_HEADS, row_count // seq_count * group)
    initial = (
        jnp.full(stat_shape, NEGATIVE, jnp.float32),
        jnp.zeros(stat_shape, jnp.float32),
        jnp.zeros(stat_shape + (HEAD,), jnp.float32),
    )
    piece = lax.all_gather(keys_values, "ctx", axis=0, tiled=True)
    count = piece.shape[0] // row_count
    blocks = piece.reshape(count, row_count, piece.shape[1])

    def block_step(inner, item):
        return (attend_block(inner, item[0], item[1]), None)

    result, unused = lax.scan(block_step, initial, (blocks, jnp.arange(count, dtype=jnp.int32)))
    top, total, running = result
    attended = from_groups(running / total[..., None], group)
    log_total = top + jnp.log(total)
    attended_low = attended.astype(jnp.bfloat16)
    mixed = inputs + matmul(attended_low, w_out)
    normed_mlp_f, norm_mlp_back = jax.vjp(rms_norm, mixed, norm_mlp.astype(jnp.float32))
    normed_mlp = normed_mlp_f.astype(jnp.bfloat16)
    gate = matmul(normed_mlp, w_gate)
    up_proj = matmul(normed_mlp, w_up)
    hidden_f, act_back = jax.vjp(lambda left, right: jax.nn.silu(left) * right, gate, up_proj)
    hidden = hidden_f.astype(jnp.bfloat16)
    mlp_total = lax.psum(matmul(hidden, w_down).astype(jnp.bfloat16), "wt").astype(jnp.float32)
    output = (mixed + mlp_total).astype(jnp.bfloat16)
    grad_hidden = matmul_nt(cotangent, w_down)
    grad_w_down = matmul_tn(hidden, cotangent)
    grad_gate_f, grad_up_f = act_back(grad_hidden)
    gate_low = grad_gate_f.astype(jnp.bfloat16)
    up_low = grad_up_f.astype(jnp.bfloat16)
    grad_w_gate = matmul_tn(normed_mlp, gate_low)
    grad_w_up = matmul_tn(normed_mlp, up_low)
    partial_in = matmul_nt(gate_low, w_gate) + matmul_nt(up_low, w_up)
    grad_normed_mlp = lax.psum(partial_in.astype(jnp.bfloat16), "wt").astype(jnp.float32)
    grad_mixed_norm, grad_norm_mlp = norm_mlp_back(grad_normed_mlp)
    grad_mixed = cotangent.astype(jnp.float32) + grad_mixed_norm
    branch_low = grad_mixed.astype(jnp.bfloat16)
    grad_w_out = matmul_tn(attended_low, branch_low)
    grad_attended = matmul_nt(branch_low, w_out).astype(jnp.bfloat16)
    delta_rows = jnp.sum(
        (grad_attended.astype(jnp.float32) * attended).reshape(row_count, Q_HEADS, HEAD), axis=-1
    )
    span = row_count // seq_count
    delta_groups = (
        delta_rows.reshape(seq_count, span, KV_HEADS, group)
        .transpose(0, 2, 1, 3)
        .reshape(stat_shape)
    )
    out_groups = to_groups(grad_attended, seq_count, group)

    def block_terms(block, index):
        key_part, value_part = split_keys(block, seq_count)
        score, seen = masked_scores(key_part, slot_places(stretch_order, index, stretch))
        probs = jnp.where(seen, jnp.exp(score - log_total[..., None]), 0.0)
        prob_grad = jnp.einsum(
            "sgqd,sgkd->sgqk", out_groups, value_part, preferred_element_type=jnp.float32
        )
        score_grad = (probs * (prob_grad - delta_groups[..., None])).astype(jnp.bfloat16)
        query_part = jnp.einsum(
            "sgqk,sgkd->sgqd", score_grad, key_part, preferred_element_type=jnp.float32
        )
        grad_key_part = (
            jnp.einsum(
                "sgqk,sgqd->sgkd", score_grad, query_groups, preferred_element_type=jnp.float32
            )
            * scale
        )
        grad_value_part = jnp.einsum(
            "sgqk,sgqd->sgkd",
            probs.astype(jnp.bfloat16),
            out_groups,
            preferred_element_type=jnp.float32,
        )
        return (query_part, join_keys(grad_key_part, grad_value_part))

    query_zero = jnp.zeros(stat_shape + (HEAD,), jnp.float32)
    back_keys = lax.all_gather(keys_values, "ctx", axis=0, tiled=True)
    block_count = back_keys.shape[0] // row_count
    all_blocks = back_keys.reshape(block_count, row_count, back_keys.shape[1])

    def scatter_step(query_acc, item):
        query_part, term = block_terms(item[0], item[1])
        return (query_acc + query_part, term)

    grad_query_groups, terms = lax.scan(
        scatter_step, query_zero, (all_blocks, jnp.arange(block_count, dtype=jnp.int32))
    )
    key_grads = lax.psum_scatter(
        terms.reshape(block_count * row_count, 2 * key_width),
        "ctx",
        scatter_dimension=0,
        tiled=True,
    )
    grad_query_rot = from_groups(grad_query_groups * scale, group)
    grad_key_pre = rope_key_back(key_grads[:, :key_width])[0].astype(jnp.bfloat16)
    grad_value_low = key_grads[:, key_width:].astype(jnp.bfloat16)
    grad_query_pre = rope_query_back(grad_query_rot)[0].astype(jnp.bfloat16)
    grad_w_query = matmul_tn(normed, grad_query_pre)
    grad_w_key = matmul_tn(normed, grad_key_pre)
    grad_w_value = matmul_tn(normed, grad_value_low)
    grad_normed = (
        matmul_nt(grad_query_pre, w_query)
        + matmul_nt(grad_key_pre, w_key)
        + matmul_nt(grad_value_low, w_value)
    )
    grad_inputs_norm, grad_norm_attn = norm_attn_back(grad_normed)
    grad_tokens = grad_mixed + grad_inputs_norm
    (
        grad_w_query,
        grad_w_key,
        grad_w_value,
        grad_w_out,
        grad_norm_attn,
        grad_norm_mlp,
        grad_w_gate,
        grad_w_up,
        grad_w_down,
    ) = lax.psum(
        (
            grad_w_query,
            grad_w_key,
            grad_w_value,
            grad_w_out,
            grad_norm_attn,
            grad_norm_mlp,
            grad_w_gate,
            grad_w_up,
            grad_w_down,
        ),
        "ctx",
    )
    return (
        output,
        grad_tokens,
        grad_w_query,
        grad_w_key,
        grad_w_value,
        grad_w_out,
        grad_norm_attn,
        grad_norm_mlp,
        grad_w_gate,
        grad_w_up,
        grad_w_down,
    )


def solution(mesh):
    return jax.shard_map(
        local,
        mesh=mesh,
        in_specs=(
            P("ctx", None),
            P(),
            P(),
            P(),
            P(),
            P(),
            P(),
            P(None, "wt"),
            P(None, "wt"),
            P("wt", None),
            P(),
            P("ctx", None),
        ),
        out_specs=(
            P("ctx", None),
            P("ctx", None),
            P(),
            P(),
            P(),
            P(),
            P(),
            P(),
            P(None, "wt"),
            P(None, "wt"),
            P("wt", None),
        ),
        check_vma=False,
    )
```

profile of v0, /device:TPU:0, one launch (start us, length us, event | category | flops | bytes accessed | tf_op | source)
XLA Modules:
  0.0 440.2 jit_solution(17642471956729836026)
XLA Ops:
  16.1 26.5 %all-gather.2.cloned.1.call-done = bf16[2048,384]{0,1:T(8,128)(2,1)} async-done(((bf16[256,384]{0,1:T(8,128)(2,1)}), bf16[2048,384]{0,1:T(8,128)(2,1)}) %all-gather.2.cloned.1.call-update) | async-done | bytes 1572880 | tf_op jit(solution)/shard_map/all_gather | solution.py:157
  42.6 2.7 copy.87
  45.2 56.3 %while.29 = (s32[]{:T(128)}, f32[1,3,768]{2,1,0:T(4,128)S(1)}, f32[1,3,768]{2,1,0:T(4,128)S(1)}, f32[1,3,768,64]{2,3,1,0:T(8,128)}, s32[8]{0:T(128)S(1)}, /*inde...) while((s32[]{:T(128)}, f32[1,3,768]{2,1,0:T(4,128)S(1)}, ...), condition=%wide.region_4.5_spmd.clone, body=%wide.region_1.4_spmd.clone.sunk | while | flops 159315712 | bytes 17964436 | solution.py:164
  103.6 2.5 copy.58
  112.2 39.5 %all-reduce.12.cloned.1.call-done = (bf16[256,576]{0,1:T(8,128)(2,1)}, bf16[256,576]{0,1:T(8,128)(2,1)}) async-done(((bf16[256,576]{0,1:T(8,128)(2,1)}, bf16[256,576]{0,1:T(8,128)(2,1)}), (bf16[256,576]{0,1:T(8,128)(2,1)}, bf16[256,576]{0,1:T(8,128)(2,1)})) %all-reduce.12.cloned.1.call-update) | async-done | bytes 589840 | tf_op jit(solution)/shard_map/psum | solution.py:176
  153.6 2.1 fusion.47
  155.7 2.4 bitcast_multiply_fusion.1
  158.1 2.1 copy.59
  160.2 2.6 reshape.441
  162.8 2.0 copy.62
  165.9 98.7 %while.30 = (s32[]{:T(128)}, f32[1,3,768,64]{2,3,1,0:T(8,128)S(1)}, f32[8,256,384]{2,1,0:T(8,128)}, s32[8]{0:T(128)S(1)}, s32[1,16]{1,0:T(1,128)S(1)}, /*index=5...) while((s32[]{:T(128)}, f32[1,3,768,64]{2,3,1,0:T(8,128)S(1)}, ...), condition=%wide.wide.region_11.12_spmd.clone, body=%wide.wide.region_10.11_spmd.clone.sunk | while | flops 384024832 | bytes 26572032 | solution.py:237
  166.9 1.9 fusion.156
  170.8 2.6 fusion.158
  179.2 1.9 fusion.156
  183.2 2.6 fusion.158
  191.6 1.9 fusion.156
  195.5 2.6 fusion.158
  203.9 1.9 fusion.156
  207.8 2.6 fusion.158
  216.3 1.9 fusion.156
  220.2 2.6 fusion.158
  228.6 1.9 fusion.156
  232.5 2.6 fusion.158
  241.0 1.9 fusion.156
  244.9 2.6 fusion.158
  253.3 1.9 fusion.156
  257.2 2.6 fusion.158
  270.2 3.3 copy.64
  277.6 32.8 %reduce-scatter.2.cloned.1.call-done = f32[256,384]{1,0:T(8,128)} async-done(((f32[2048,384]{1,0:T(8,128)}), f32[256,384]{1,0:T(8,128)}) %reduce-scatter.2.cloned.1.call-update) | async-done | bytes 393232 | tf_op jit(solution)/shard_map/reduce_scatter | solution.py:240
  316.6 14.0 %all-reduce.4 = (f32[576]{0:T(1024)}, f32[576]{0:T(1024)}) all-reduce(f32[576]{0:T(1024)S(1)} %get-tuple-element.257, f32[576]{0:T(1024)S(1)} %copy-done.46), channel_id=1, replica_groups=mesh['ctx'=8,'wt'=4] {'ctx'}, use_global_device_ids=true, to_apply=%region_19.20 | all-reduce | flops 1152 | bytes 9216 | tf_op jit(solution)/shard_map/psum | solution.py:270
  331.6 94.0 %all-reduce.10.cloned.1.call-done = (f32[576,576]{1,0:T(8,128)}, f32[576,192]{0,1:T(8,128)}, f32[576,192]{0,1:T(8,128)}, f32[576,576]{1,0:T(8,128)}, f32[576,384...) async-done(((f32[576,576]{1,0:T(8,128)}, f32[576,192]{0,1:T(8,128)}, f32[576,192]{0,1:T(8,128)}, f32[576,576]{1,0:T(8,128)}, f32[576,384]{1,0:T(8,128)}, ...) | async-done | bytes 6193168 | tf_op jit(solution)/shard_map/psum | solution.py:270
  425.6 2.7 copy.122
  (628 shorter events, 147.8 us)
Async XLA Ops:
  7.2 100.0 %copy-start = (bf16[576,576]{1,0:T(8,128)(2,1)S(1)}, bf16[576,576]{1,0:T(8,128)(2,1)}, u32[]{:S(2)}) copy-start(bf16[576,576]{1,0:T(8,128)(2,1)} %param.20) | copy-start | bytes 1990660
  7.2 6.7 %copy-start.4 = (bf16[256,576]{0,1:T(8,128)(2,1)S(1)}, bf16[256,576]{0,1:T(8,128)(2,1)}, u32[]{:S(2)}) copy-start(bf16[256,576]{0,1:T(8,128)(2,1)} %param.16) | copy-start | bytes 884740
  7.2 6.7 %copy-start.12 = (bf16[576,576]{1,0:T(8,128)(2,1)S(1)}, bf16[576,576]{1,0:T(8,128)(2,1)}, u32[]{:S(2)}) copy-start(bf16[576,576]{1,0:T(8,128)(2,1)} %param.17) | copy-start | bytes 1990660
  7.2 35.4 %all-gather.2.cloned.1.call-start = ((), (), s32[]{:S(2)}) async-start(), calls=%async_computation.1 | async-start | bytes 1769472 | tf_op jit(solution)/shard_map/all_gather | solution.py:157
  8.1 6.5 %copy-start.40 = (f32[576]{0:T(1024)}, f32[576]{0:T(1024)S(1)}, u32[]{:S(2)}) copy-start(f32[576]{0:T(1024)S(1)} %convert_element_type.106) | copy-start | bytes 6916
  9.2 5.5 %copy-start.44 = (f32[256]{0:T(256)}, f32[256]{0:T(256)S(1)}, u32[]{:S(2)}) copy-start(f32[256]{0:T(256)S(1)} %fusion.59) | copy-start | bytes 3076
  13.9 137.9 %all-reduce.12.cloned.1.call-start = ((), (), s32[]{:S(2)}) async-start(), calls=%async_computation.4 | async-start | bytes 1179648 | tf_op jit(solution)/shard_map/psum | solution.py:176
  15.8 29.4 %copy-start.52 = (s32[1,16]{1,0:T(1,128)S(1)}, s32[1,16]{1,0:T(1,128)}, u32[]{:S(2)}) copy-start(s32[1,16]{1,0:T(1,128)} %param.26) | copy-start | bytes 196
  112.0 198.5 %reduce-scatter.2.cloned.1.call-start = ((), (), s32[]{:S(2)}) async-start(), calls=%async_computation.2 | async-start | bytes 3538944 | tf_op jit(solution)/shard_map/reduce_scatter | solution.py:240
  155.7 7.1 %copy-start.8 = (f32[256,576]{0,1:T(8,128)}, f32[256,576]{0,1:T(8,128)S(1)}, u32[]{:S(2)}) copy-start(f32[256,576]{0,1:T(8,128)S(1)} %get-tuple-element.321) | copy-start | bytes 1769476
  165.9 4.7 %copy-start.42 = (s32[256]{0:T(256)}, s32[256]{0:T(256)S(1)}, u32[]{:S(2)}) copy-start(s32[256]{0:T(256)S(1)} %get-tuple-element.597) | copy-start | bytes 3076 | tf_op jit(solution)/shard_map/while
  165.9 4.7 %copy-start.47 = (f32[1,3,768]{2,1,0:T(4,128)}, f32[1,3,768]{2,1,0:T(4,128)S(1)}, u32[]{:S(2)}) copy-start(f32[1,3,768]{2,1,0:T(4,128)S(1)} %get-tuple-element.594) | copy-start | bytes 27652 | tf_op jit(solution)/shard_map/while
  165.9 4.7 %copy-start.53 = (s32[1,16]{1,0:T(1,128)}, s32[1,16]{1,0:T(1,128)S(1)}, u32[]{:S(2)}) copy-start(s32[1,16]{1,0:T(1,128)S(1)} %get-tuple-element.591) | copy-start | bytes 196 | tf_op jit(solution)/shard_map/while
  178.2 4.7 %copy-start.42 = (s32[256]{0:T(256)}, s32[256]{0:T(256)S(1)}, u32[]{:S(2)}) copy-start(s32[256]{0:T(256)S(1)} %get-tuple-element.597) | copy-start | bytes 3076 | tf_op jit(solution)/shard_map/while
  178.3 4.7 %copy-start.47 = (f32[1,3,768]{2,1,0:T(4,128)}, f32[1,3,768]{2,1,0:T(4,128)S(1)}, u32[]{:S(2)}) copy-start(f32[1,3,768]{2,1,0:T(4,128)S(1)} %get-tuple-element.594) | copy-start | bytes 27652 | tf_op jit(solution)/shard_map/while
  178.3 4.7 %copy-start.53 = (s32[1,16]{1,0:T(1,128)}, s32[1,16]{1,0:T(1,128)S(1)}, u32[]{:S(2)}) copy-start(s32[1,16]{1,0:T(1,128)S(1)} %get-tuple-element.591) | copy-start | bytes 196 | tf_op jit(solution)/shard_map/while
  190.6 4.7 %copy-start.42 = (s32[256]{0:T(256)}, s32[256]{0:T(256)S(1)}, u32[]{:S(2)}) copy-start(s32[256]{0:T(256)S(1)} %get-tuple-element.597) | copy-start | bytes 3076 | tf_op jit(solution)/shard_map/while
  190.6 4.7 %copy-start.47 = (f32[1,3,768]{2,1,0:T(4,128)}, f32[1,3,768]{2,1,0:T(4,128)S(1)}, u32[]{:S(2)}) copy-start(f32[1,3,768]{2,1,0:T(4,128)S(1)} %get-tuple-element.594) | copy-start | bytes 27652 | tf_op jit(solution)/shard_map/while
  202.9 4.7 %copy-start.42 = (s32[256]{0:T(256)}, s32[256]{0:T(256)S(1)}, u32[]{:S(2)}) copy-start(s32[256]{0:T(256)S(1)} %get-tuple-element.597) | copy-start | bytes 3076 | tf_op jit(solution)/shard_map/while
  202.9 4.7 %copy-start.47 = (f32[1,3,768]{2,1,0:T(4,128)}, f32[1,3,768]{2,1,0:T(4,128)S(1)}, u32[]{:S(2)}) copy-start(f32[1,3,768]{2,1,0:T(4,128)S(1)} %get-tuple-element.594) | copy-start | bytes 27652 | tf_op jit(solution)/shard_map/while
  203.0 4.7 %copy-start.53 = (s32[1,16]{1,0:T(1,128)}, s32[1,16]{1,0:T(1,128)S(1)}, u32[]{:S(2)}) copy-start(s32[1,16]{1,0:T(1,128)S(1)} %get-tuple-element.591) | copy-start | bytes 196 | tf_op jit(solution)/shard_map/while
  215.3 4.7 %copy-start.42 = (s32[256]{0:T(256)}, s32[256]{0:T(256)S(1)}, u32[]{:S(2)}) copy-start(s32[256]{0:T(256)S(1)} %get-tuple-element.597) | copy-start | bytes 3076 | tf_op jit(solution)/shard_map/while
  215.3 4.7 %copy-start.47 = (f32[1,3,768]{2,1,0:T(4,128)}, f32[1,3,768]{2,1,0:T(4,128)S(1)}, u32[]{:S(2)}) copy-start(f32[1,3,768]{2,1,0:T(4,128)S(1)} %get-tuple-element.594) | copy-start | bytes 27652 | tf_op jit(solution)/shard_map/while
  227.6 4.7 %copy-start.42 = (s32[256]{0:T(256)}, s32[256]{0:T(256)S(1)}, u32[]{:S(2)}) copy-start(s32[256]{0:T(256)S(1)} %get-tuple-element.597) | copy-start | bytes 3076 | tf_op jit(solution)/shard_map/while
  227.6 4.7 %copy-start.47 = (f32[1,3,768]{2,1,0:T(4,128)}, f32[1,3,768]{2,1,0:T(4,128)S(1)}, u32[]{:S(2)}) copy-start(f32[1,3,768]{2,1,0:T(4,128)S(1)} %get-tuple-element.594) | copy-start | bytes 27652 | tf_op jit(solution)/shard_map/while
  240.0 4.7 %copy-start.42 = (s32[256]{0:T(256)}, s32[256]{0:T(256)S(1)}, u32[]{:S(2)}) copy-start(s32[256]{0:T(256)S(1)} %get-tuple-element.597) | copy-start | bytes 3076 | tf_op jit(solution)/shard_map/while
  240.0 4.7 %copy-start.47 = (f32[1,3,768]{2,1,0:T(4,128)}, f32[1,3,768]{2,1,0:T(4,128)S(1)}, u32[]{:S(2)}) copy-start(f32[1,3,768]{2,1,0:T(4,128)S(1)} %get-tuple-element.594) | copy-start | bytes 27652 | tf_op jit(solution)/shard_map/while
  252.3 4.7 %copy-start.42 = (s32[256]{0:T(256)}, s32[256]{0:T(256)S(1)}, u32[]{:S(2)}) copy-start(s32[256]{0:T(256)S(1)} %get-tuple-element.597) | copy-start | bytes 3076 | tf_op jit(solution)/shard_map/while
  252.3 4.7 %copy-start.47 = (f32[1,3,768]{2,1,0:T(4,128)}, f32[1,3,768]{2,1,0:T(4,128)S(1)}, u32[]{:S(2)}) copy-start(f32[1,3,768]{2,1,0:T(4,128)S(1)} %get-tuple-element.594) | copy-start | bytes 27652 | tf_op jit(solution)/shard_map/while
  252.3 4.7 %copy-start.53 = (s32[1,16]{1,0:T(1,128)}, s32[1,16]{1,0:T(1,128)S(1)}, u32[]{:S(2)}) copy-start(s32[1,16]{1,0:T(1,128)S(1)} %get-tuple-element.591) | copy-start | bytes 196 | tf_op jit(solution)/shard_map/while
  264.7 160.8 %all-reduce.10.cloned.1.call-start = ((), (), s32[]{:S(2)}) async-start(), calls=%async_computation.3 | async-start | bytes 13172736 | tf_op jit(solution)/shard_map/psum | solution.py:270
  314.9 15.7 %copy-start.50 = (f32[256]{0:T(256)S(1)}, f32[256]{0:T(256)}, u32[]{:S(2)}) copy-start(f32[256]{0:T(256)} %copy-done.49) | copy-start | bytes 3076
  (134 other events, 250.6 us)
Sparse Core Ops, SparseCore 0:
  14.0 28.5 all-gather.1
  112.1 39.6 all-reduce.11
  264.8 45.5 reduce-scatter.1
  316.3 109.2 all-reduce.9
where the time goes:
time: 442 us; the launch traced here: 440 us
  waiting for transfers between devices  193 us (44%)
  local copies, waits for them, and re-layouts  88 us (20%)
  matrix products  87.7 us (20%)
  other arithmetic  29.8 us (7%)
  between operations  14.5 us (3%)
  blocking collectives  14 us (3%)
  loops' own time  13.1 us (3%)
    psum x1, waiting for transfers between devices, local(): lax.psum((grad_w_query, grad_w_key, grad_w_value, grad_w_out, grad_norm_a...  94 us
    psum x1, waiting for transfers between devices, local(): lax.psum(matmul(hidden, w_down).astype(jnp.bfloat16), 'wt')  39.5 us
    reduce_scatter x1, waiting for transfers between devices, local(): lax.psum_scatter(terms.reshape(block_count * row_count, 2 * key_width), '...  32.8 us
    all_gather x1, waiting for transfers between devices, local(): piece = lax.all_gather(keys_values, 'ctx', axis=0, tiled=True)  26.5 us
    dynamic_slice x32, local copies, waits for them, and re-layouts, local(): lax.scan(block_step, initial, (blocks, jnp.arange(count, dtype=jnp.int32)))  25.6 us
    dot_general x8, matrix products, block_terms(): jnp.einsum('sgqd,sgkd->sgqk', out_groups, value_part, preferred_element_t...  20.5 us
    dot_general x16, matrix products, masked_scores(): jnp.einsum('sgqd,sgkd->sgqk', query_groups, key_part, preferred_element_t...  20.2 us
    while x248, local copies, waits for them, and re-layouts  17.7 us
  transfers between devices with their start and end apart: 4, of which 4 were waited for; matrix products, arithmetic and copies ran while one was open for 4% of the time, Pallas kernels for 0%

commit v1 on v0

v1 whole, which is shorter than its diff:
```python
import functools

import jax
import jax.numpy as jnp
from jax import lax
from jax.experimental import pallas as pl
from jax.experimental.pallas import tpu as pltpu
from jax.sharding import PartitionSpec as P

Q_HEADS = 9
KV_HEADS = 3
GROUP = 3
HEAD = 64
PAIR = 2 * HEAD
EPSILON = 1e-05
THETA = 100000.0
NEGATIVE = -1e30
BF = jnp.bfloat16
F32 = jnp.float32
MIB = 1 << 20

VM = pl.BlockSpec(memory_space=pltpu.VMEM)
SM = pl.BlockSpec(memory_space=pltpu.SMEM)
HB = pl.BlockSpec(memory_space=pl.ANY)


def dot(left, right):
    return jnp.dot(left, right, preferred_element_type=F32)


def dot_nt(left, right):
    return lax.dot_general(left, right, (((1,), (1,)), ((), ())), preferred_element_type=F32)


def dot_tn(left, right):
    return lax.dot_general(left, right, (((0,), (0,)), ((), ())), preferred_element_type=F32)


def swap_lanes(x):
    half = x.shape[-1] // 2
    return jnp.concatenate([x[:, half:], x[:, :half]], axis=1)


def call(body, out_shape, in_specs, vmem, scratch=(), out_specs=None, flops=0, **kw):
    return pl.pallas_call(
        body,
        out_shape=out_shape,
        in_specs=in_specs,
        out_specs=out_specs if out_specs is not None else jax.tree.map(lambda _: VM, out_shape),
        scratch_shapes=list(scratch),
        compiler_params=pltpu.CompilerParams(vmem_limit_bytes=vmem * MIB),
        cost_estimate=pl.CostEstimate(flops=flops, bytes_accessed=4 * MIB, transcendentals=0),
        **kw,
    )


def shape(dims, dtype):
    return jax.ShapeDtypeStruct(dims, dtype)


def key_kernel(tok, gain, wk, wv, cos, sin, normed_out, kv_out):
    x = tok[...].astype(F32)
    r = lax.rsqrt(jnp.mean(x * x, axis=-1, keepdims=True) + EPSILON)
    normed = (x * r * gain[...].astype(F32)).astype(BF)
    normed_out[...] = normed
    k = dot(normed, wk[...])
    v = dot(normed, wv[...])
    for g in range(KV_HEADS):
        kg = k[:, g * HEAD : (g + 1) * HEAD]
        kr = kg * cos[...] + swap_lanes(kg) * sin[...]
        vg = v[:, g * HEAD : (g + 1) * HEAD]
        kv_out[:, g * PAIR : (g + 1) * PAIR] = jnp.concatenate([kr, vg], axis=1).astype(BF)


def query_kernel(normed, wq, cos, sin, q_out):
    rows = normed.shape[0]
    stretch = rows // 2
    q = dot(normed[...], wq[...])
    zero = jnp.zeros((rows, HEAD), F32)
    for h in range(Q_HEADS):
        qh = q[:, h * HEAD : (h + 1) * HEAD]
        qr = (qh * cos[...] + swap_lanes(qh) * sin[...]) * HEAD**-0.5
        wide = jnp.concatenate([qr, zero], axis=1).astype(BF)
        g, hh = h // GROUP, h % GROUP
        for sel in range(2):
            at = (sel * GROUP + hh) * stretch
            q_out[g, at : at + stretch, :] = wide[sel * stretch : (sel + 1) * stretch]


def parts_of(n):
    low_group = min(n, 8)
    unit_group = max(d for d in range(1, 14) if (n + 1) % d == 0)
    return low_group, n // low_group, unit_group, (n + 1) // unit_group


def loop(count, body):
    if count == 1:
        body(0)
    else:
        lax.fori_loop(0, count, lambda i, c: (body(i), c)[1], 0)


def unit(u, c, n):
    is_low = u <= c
    sel = jnp.where(is_low, 0, 1)
    stretch_id = jnp.where(is_low, u, n - 1 + u - c)
    diagonal = jnp.logical_or(u == c, u == n)
    return is_low, sel, stretch_id, diagonal


def seen_mask(stretch, diagonal):
    keys = lax.broadcasted_iota(jnp.int32, (stretch, GROUP * stretch), 0)
    cols = lax.broadcasted_iota(jnp.int32, (stretch, GROUP * stretch), 1)
    queries = lax.bitwise_and(cols, stretch - 1)
    return jnp.logical_or(keys <= queries, jnp.logical_not(diagonal))


def forward_kernel(n, wt, *refs):
    evens = refs[: n // 2]
    (meta, order, odds, q_ref, tok, cot, w_out, gain, w_gate, w_up, w_down) = refs[n // 2 : n // 2 + 11]
    outs = refs[n // 2 + 11 :]
    (kv_all, att_t, att_low_out, lse_out, mixed_out, n2_out, hid_out, gl_out, ul_out, po_out) = outs[:10]
    pin_outs = outs[10 : 10 + wt]
    kvn, m_s, l_s, o_s, pin_s, sems, out_sem = outs[10 + wt :]
    rows = tok.shape[0]
    stretch = rows // 2
    wide = GROUP * stretch
    me = meta[0]
    copies = []
    for k in range(n):
        low = order[0, 2 * lax.bitwise_xor(me, k)]
        src = evens[k // 2] if k % 2 == 0 else odds.at[k // 2]
        for half in range(2):
            to = low if half == 0 else 2 * n - 1 - low
            copies.append(
                pltpu.make_async_copy(
                    src.at[half * stretch : (half + 1) * stretch],
                    kvn.at[pl.ds(pl.multiple_of(to * stretch, stretch), stretch)],
                    sems.at[2 * k + half],
                )
            )
    for copy in copies:
        copy.start()
    for copy in copies:
        copy.wait()
    keep = pltpu.make_async_copy(kvn, kv_all, out_sem)
    keep.start()
    c = order[0, 2 * me]
    low_group, low_steps, unit_group, unit_steps = parts_of(n)

    for g in range(KV_HEADS):
        lanes = slice(g * PAIR, (g + 1) * PAIR)
        for sel in range(2):
            m_s[2 * g + sel] = jnp.full((1, wide), NEGATIVE, F32)
            l_s[2 * g + sel] = jnp.zeros((1, wide), F32)
            o_s[2 * g + sel] = jnp.zeros((PAIR, wide), F32)

        def low_step(i, g=g, lanes=lanes):
            size = low_group * stretch
            keys = kvn[pl.ds(i * size, size), lanes]
            s = dot_nt(keys, q_ref[g, wide : 2 * wide, :])
            at = 2 * g + 1
            top = jnp.maximum(m_s[at], jnp.max(s, axis=0, keepdims=True))
            fade = jnp.exp(m_s[at] - top)
            p = jnp.exp(s - top)
            l_s[at] = l_s[at] * fade + jnp.sum(p, axis=0, keepdims=True)
            o_s[at] = o_s[at] * fade + dot_tn(keys, p.astype(BF))
            m_s[at] = top

        loop(low_steps, low_step)

        def unit_step(i, g=g, lanes=lanes):
            scores = []
            tops = [m_s[2 * g], m_s[2 * g + 1]]
            for j in range(unit_group):
                u = i * unit_group + j
                is_low, sel, st, diagonal = unit(u, c, n)
                keys = kvn[pl.ds(pl.multiple_of(st * stretch, stretch), stretch), lanes]
                q = q_ref[g, pl.ds(pl.multiple_of(sel * wide, wide), wide), :]
                s = jnp.where(seen_mask(stretch, diagonal), dot_nt(keys, q), NEGATIVE)
                peak = jnp.max(s, axis=0, keepdims=True)
                tops[0] = jnp.where(is_low, jnp.maximum(tops[0], peak), tops[0])
                tops[1] = jnp.where(is_low, tops[1], jnp.maximum(tops[1], peak))
                scores.append((s, keys, is_low, sel))
            sums = []
            for sel in range(2):
                at = 2 * g + sel
                fade = jnp.exp(m_s[at] - tops[sel])
                sums.append(l_s[at] * fade)
                o_s[at] = o_s[at] * fade
                m_s[at] = tops[sel]
            for s, keys, is_low, sel in scores:
                p = jnp.exp(s - jnp.where(is_low, tops[0], tops[1]))
                part = jnp.sum(p, axis=0, keepdims=True)
                sums[0] = sums[0] + jnp.where(is_low, part, 0.0)
                sums[1] = sums[1] + jnp.where(is_low, 0.0, part)
                o_s[2 * g + sel] += dot_tn(keys, p.astype(BF))
            for sel in range(2):
                l_s[2 * g + sel] = sums[sel]

        loop(unit_steps, unit_step)
        for sel in range(2):
            at = 2 * g + sel
            total = l_s[at]
            lse_out[at : at + 1, :] = m_s[at] + jnp.log(total)
            result = o_s[at][HEAD:, :] / total
            for hh in range(GROUP):
                h = g * GROUP + hh
                att_t[h * HEAD : (h + 1) * HEAD, sel * stretch : (sel + 1) * stretch] = result[
                    :, hh * stretch : (hh + 1) * stretch
                ]
    att_low = att_t[...].T.astype(BF)
    att_low_out[...] = att_low
    mixed = tok[...].astype(F32) + dot(att_low, w_out[...])
    mixed_out[...] = mixed
    r = lax.rsqrt(jnp.mean(mixed * mixed, axis=-1, keepdims=True) + EPSILON)
    n2 = (mixed * r * gain[...].astype(F32)).astype(BF)
    n2_out[...] = n2
    gate = dot(n2, w_gate[...])
    up = dot(n2, w_up[...])
    sig = 1.0 / (1.0 + jnp.exp(-gate))
    silu = gate * sig
    hidden = (silu * up).astype(BF)
    hid_out[...] = hidden
    grad_hidden = dot_nt(cot[...], w_down[...])
    gl = (grad_hidden * up * (sig * (1.0 + gate * (1.0 - sig)))).astype(BF)
    ul = (grad_hidden * silu).astype(BF)
    gl_out[...] = gl
    ul_out[...] = ul
    pin_s[...] = dot_nt(gl, w_gate[...]) + dot_nt(ul, w_up[...])
    piece = rows // wt
    for k in range(wt):
        at = pl.multiple_of(lax.bitwise_xor(meta[1], k) * piece, piece)
        pin_outs[k][...] = pin_s[pl.ds(at, piece), :].astype(BF)
    po_out[...] = dot(hidden, w_down[...]).astype(BF)
    keep.wait()


def put_blocks(n, me, scratch, even, odd):
    size = scratch.shape[0] // n
    if n > 8:
        even[...] = scratch[...].astype(BF)
        odd[...] = jnp.zeros(odd.shape, BF)
        return
    for k in range(n):
        at = pl.multiple_of(lax.bitwise_xor(me, k) * size, size)
        to = even if k % 2 == 0 else odd
        to[k // 2] = scratch[pl.ds(at, size), :].astype(BF)


def mlp_grad_kernel(n, meta, n2, gl, ul, hidden, cot, even, odd, scratch):
    width = gl.shape[1]
    scratch[:, :width] = dot_tn(n2[...], gl[...])
    scratch[:, width : 2 * width] = dot_tn(n2[...], ul[...])
    scratch[:, 2 * width :] = dot_tn(cot[...], hidden[...])
    put_blocks(n, meta[0], scratch, even, odd)


def query_grad_kernel(n, meta, normed, dq_t, att_low, branch, wq, gn_out, even, odd, scratch):
    width = normed.shape[1]
    dq = dq_t[...].T.astype(BF)
    scratch[:, :width] = dot_tn(normed[...], dq)
    scratch[:, width:] = dot_tn(att_low[...], branch[...])
    gn_out[...] = dot_nt(dq, wq[...])
    put_blocks(n, meta[0], scratch, even, odd)


def key_grad_kernel(n, count, meta, *refs):
    kv_parts = refs[:count]
    (normed, gnq, wk, wv, cos, sin, tok, gain, gm, gnorm_mlp) = refs[count : count + 10]
    gt_out, even, odd, scratch, norm_s = refs[count + 10 :]
    total = kv_parts[0][...].astype(F32)
    for part in kv_parts[1:]:
        total = total + part[...].astype(F32)
    dk, dv = [], []
    for g in range(KV_HEADS):
        k = total[:, g * PAIR : g * PAIR + HEAD]
        dk.append(k * cos[...] - swap_lanes(k) * sin[...])
        dv.append(total[:, g * PAIR + HEAD : (g + 1) * PAIR])
    dk = jnp.concatenate(dk, axis=1).astype(BF)
    dv = jnp.concatenate(dv, axis=1).astype(BF)
    both = jnp.concatenate([dk, dv], axis=1)
    gn = gnq[...] + dot_nt(dk, wk[...]) + dot_nt(dv, wv[...])
    x = tok[...].astype(F32)
    r = lax.rsqrt(jnp.mean(x * x, axis=-1, keepdims=True) + EPSILON)
    xn = x * r
    e = gn * gain[...].astype(F32)
    gt_out[...] = gm[...] + r * (e - xn * jnp.mean(e * xn, axis=-1, keepdims=True))
    scratch[...] = dot_tn(normed[...], both)
    width = normed.shape[1]
    norm_s[...] = jnp.zeros(norm_s.shape, F32)
    norm_s[0:1, :width] = jnp.sum(gn * xn, axis=0, keepdims=True)
    norm_s[1:2, :width] = gnorm_mlp[...]
    if n > 8:
        even[...] = scratch[...].astype(BF)
        odd[...] = norm_s[...].astype(BF)
        return
    size = scratch.shape[0] // n
    for k in range(n):
        who = lax.bitwise_xor(meta[0], k)
        to = even if k % 2 == 0 else odd
        to[k // 2, :size, :] = scratch[pl.ds(pl.multiple_of(who * size, size), size), :].astype(BF)
        cut = norm_s[:, pl.ds(pl.multiple_of(who * 128, 128), 128)]
        tail = jnp.concatenate([cut, jnp.zeros((8, scratch.shape[1] - 128), F32)], axis=1)
        to[k // 2, size:, :] = tail.astype(BF)


def join_kernel(n, splits, turned, norms, meta, *refs):
    evens = refs[: n // 2]
    odds = refs[n // 2]
    outs = refs[n // 2 + 1 :]
    scratch = outs[-2] if norms else outs[-1]
    size = scratch.shape[0] // n
    if norms:
        norm_s = outs[-1]
        norm_s[...] = jnp.zeros(norm_s.shape, F32)
    for k in range(n):
        who = lax.bitwise_xor(meta[0], k)
        block = evens[k // 2][...] if k % 2 == 0 else odds[k // 2]
        block = block.astype(F32)
        scratch[pl.ds(pl.multiple_of(who * size, size), size), :] = block[:size]
        if norms:
            norm_s[:, pl.ds(pl.multiple_of(who * 128, 128), 128)] = block[size:, :128]
    at = 0
    for i, width in enumerate(splits):
        part = scratch[:, at : at + width]
        outs[i][...] = part.T if i in turned else part
        at += width
    if norms:
        for i in range(2):
            outs[len(splits) + i][...] = norm_s[i : i + 1, : scratch.shape[0]]


def backward_kernel(n, wt, *refs):
    quarters = refs[:wt]
    (meta, order, mixed, cot, gain, w_out, att_t, lse, kv, q_ref, cos_t, sin_t) = refs[wt : wt + 12]
    gm_out, branch_out, gnorm_out, dq_out, even, odd, gn_s, do_s, dl_s, dkv, dq_s = refs[wt + 12 :]
    rows = mixed.shape[0]
    stretch = rows // 2
    wide = GROUP * stretch
    me = meta[0]
    c = order[0, 2 * me]
    g = pl.program_id(0)
    low_group, low_steps, unit_group, unit_steps = parts_of(n)

    @pl.when(g == 0)
    def _():
        piece = rows // wt
        for k in range(wt):
            at = pl.multiple_of(lax.bitwise_xor(meta[1], k) * piece, piece)
            gn_s[pl.ds(at, piece), :] = quarters[k][...].astype(F32)
        x = mixed[...]
        gn = gn_s[...]
        r = lax.rsqrt(jnp.mean(x * x, axis=-1, keepdims=True) + EPSILON)
        xn = x * r
        e = gn * gain[...].astype(F32)
        gm = cot[...].astype(F32) + r * (e - xn * jnp.mean(e * xn, axis=-1, keepdims=True))
        gm_out[...] = gm
        gnorm_out[...] = jnp.sum(gn * xn, axis=0, keepdims=True)
        branch = gm.astype(BF)
        branch_out[...] = branch
        ga = dot_nt(branch, w_out[...]).astype(BF).astype(F32)
        prod = ga.T * att_t[...]
        zero = jnp.zeros((rows, HEAD), F32)
        for h in range(Q_HEADS):
            gg, hh = h // GROUP, h % GROUP
            delta = jnp.sum(prod[h * HEAD : (h + 1) * HEAD, :], axis=0, keepdims=True)
            do = jnp.concatenate([zero, ga[:, h * HEAD : (h + 1) * HEAD]], axis=1).astype(BF)
            for sel in range(2):
                at = (sel * GROUP + hh) * stretch
                half = slice(sel * stretch, (sel + 1) * stretch)
                dl_s[2 * gg + sel, :, hh * stretch : (hh + 1) * stretch] = delta[:, half]
                do_s[gg, at : at + stretch, :] = do[half]

    dkv[n * stretch :, :] = jnp.zeros((n * stretch, PAIR), F32)
    dq_s[...] = jnp.zeros(dq_s.shape, F32)

    def low_step(i):
        size = low_group * stretch
        at = pl.multiple_of(i * size, size)
        keys = kv[pl.ds(at, size), :]
        q = q_ref[0, wide : 2 * wide, :]
        do = do_s[g, wide : 2 * wide, :]
        p = jnp.exp(dot_nt(keys, q) - lse[2 * g + 1])
        ds = (p * (dot_nt(keys, do) - dl_s[2 * g + 1])).astype(BF)
        dkv[pl.ds(at, size), :] = dot(ds, q) + dot(p.astype(BF), do)
        dq_s[1] += dot_tn(keys, ds)

    loop(low_steps, low_step)

    def unit_step(i):
        for j in range(unit_group):
            u = i * unit_group + j
            _, sel, st, diagonal = unit(u, c, n)
            at = pl.ds(pl.multiple_of(st * stretch, stretch), stretch)
            keys = kv[at, :]
            span = pl.ds(pl.multiple_of(sel * wide, wide), wide)
            q = q_ref[0, span, :]
            do = do_s[g, span, :]
            p = jnp.exp(dot_nt(keys, q) - lse[2 * g + sel])
            p = jnp.where(seen_mask(stretch, diagonal), p, 0.0)
            ds = (p * (dot_nt(keys, do) - dl_s[2 * g + sel])).astype(BF)
            dkv[at, :] += dot(ds, q) + dot(p.astype(BF), do)
            dq_s[sel] += dot_tn(keys, ds)

    loop(unit_steps, unit_step)
    for k in range(n):
        low = order[0, 2 * lax.bitwise_xor(me, k)]
        to = even if k % 2 == 0 else odd
        for half in range(2):
            st = low if half == 0 else 2 * n - 1 - low
            part = dkv[pl.ds(pl.multiple_of(st * stretch, stretch), stretch), :]
            to[k // 2, half * stretch : (half + 1) * stretch, :] = part.astype(BF)
    for sel in range(2):
        half = slice(sel * stretch, (sel + 1) * stretch)
        for hh in range(GROUP):
            x = dq_s[sel, :HEAD, hh * stretch : (hh + 1) * stretch] * HEAD**-0.5
            turned = jnp.concatenate([x[HEAD // 2 :], x[: HEAD // 2]], axis=0)
            dq_out[hh * HEAD : (hh + 1) * HEAD, half] = x * cos_t[:, half] - turned * sin_t[:, half]


def hop(x, axis, size, k):
    return lax.ppermute(x, axis, [(i, i ^ k) for i in range(size)])


def gather_blocks(x, axis, size):
    evens = [x] + [hop(x, axis, size, k) for k in range(2, size, 2)]
    odds = hop(jnp.stack(evens), axis, size, 1)
    return evens, odds


def scatter_terms(even, odd, axis, size):
    got = hop(odd, axis, size, 1).astype(F32)
    terms = []
    for i in range(size // 2):
        pair = even[i].astype(F32) + got[i]
        terms.append(pair if i == 0 else hop(pair.astype(BF), axis, size, 2 * i))
    return terms


def summed(terms):
    total = terms[0].astype(F32)
    for term in terms[1:]:
        total = total + term.astype(F32)
    return total


def reduce_blocks(even, odd, axis, size):
    if size > 8:
        return lax.psum((even, odd), axis)
    return gather_blocks(summed(scatter_terms(even, odd, axis, size)).astype(BF), axis, size)


def local(
    n,
    wt,
    tokens,
    w_query,
    w_key,
    w_value,
    w_out,
    norm_attn,
    norm_mlp,
    w_gate,
    w_up,
    w_down,
    stretch_order,
    cotangent,
):
    rows, width = tokens.shape
    stretch = rows // 2
    wide = GROUP * stretch
    kv_width = KV_HEADS * PAIR
    hidden_width = w_gate.shape[1]
    me = lax.axis_index("ctx")
    lane = lax.axis_index("wt")
    meta = jnp.stack([me, lane]).astype(jnp.int32)
    gain_attn = norm_attn.reshape(1, width)
    gain_mlp = norm_mlp.reshape(1, width)
    big = 30 if n <= 8 else 60

    pair = lax.dynamic_slice_in_dim(stretch_order[0], 2 * me, 2, 0)
    places = (pair[:, None] * stretch + jnp.arange(stretch, dtype=jnp.int32)[None, :]).reshape(rows)
    half = HEAD // 2
    rates = THETA ** (-jnp.arange(half, dtype=F32) / half)
    angle = places.astype(F32)[:, None] * rates[None, :]
    cosine, sine = jnp.cos(angle), jnp.sin(angle)
    cos = jnp.concatenate([cosine, cosine], axis=1)
    sin = jnp.concatenate([-sine, sine], axis=1)
    cos_t, sin_t = cos.T, sin.T

    normed, kv = call(
        key_kernel, (shape((rows, width), BF), shape((rows, kv_width), BF)), [VM] * 6, 16
    )(tokens, gain_attn, w_key, w_value, cos, sin)
    evens, odds = gather_blocks(kv, "ctx", n)
    q = call(query_kernel, shape((KV_HEADS, 2 * wide, PAIR), BF), [VM] * 4, 16)(
        normed, w_query, cos, sin
    )

    piece = rows // wt
    forward = call(
        functools.partial(forward_kernel, n, wt),
        (
            shape((n * rows, kv_width), BF),
            shape((width, rows), F32),
            shape((rows, width), BF),
            shape((2 * KV_HEADS, wide), F32),
            shape((rows, width), F32),
            shape((rows, width), BF),
            shape((rows, hidden_width), BF),
            shape((rows, hidden_width), BF),
            shape((rows, hidden_width), BF),
            shape((rows, width), BF),
        )
        + (shape((piece, width), BF),) * wt,
        [HB] * (n // 2) + [SM, SM, HB] + [VM] * 8,
        big,
        scratch=[
            pltpu.VMEM((n * rows, kv_width), BF),
            pltpu.VMEM((2 * KV_HEADS, 1, wide), F32),
            pltpu.VMEM((2 * KV_HEADS, 1, wide), F32),
            pltpu.VMEM((2 * KV_HEADS, PAIR, wide), F32),
            pltpu.VMEM((rows, width), F32),
            pltpu.SemaphoreType.DMA((2 * n,)),
            pltpu.SemaphoreType.DMA,
        ],
        out_specs=(HB,) + (VM,) * (9 + wt),
    )(*evens, meta, stretch_order, odds, q, tokens, cotangent, w_out, gain_mlp, w_gate, w_up, w_down)
    kv_all, att_t, att_low, lse, mixed, n2, hidden, gl, ul, part_out = forward[:10]
    part_in = forward[10:]

    terms = [part_in[0]] + [hop(part_in[k], "wt", wt, k) for k in range(1, wt)]
    quarter = summed(terms).astype(BF)
    quarters = [quarter] + [hop(quarter, "wt", wt, k) for k in range(1, wt)]

    mlp_total = lax.psum(part_out, "wt").astype(F32)
    output = (mixed + mlp_total).astype(BF)

    def block_shapes(columns, extra=0):
        if n > 8:
            return shape((width, columns), BF), shape((8, 128 * n), BF)
        size = width // n
        one = shape((n // 2, size + extra, columns), BF)
        return one, one

    def join(blocks, columns, splits, turned=(), norms=False):
        evens, odds = blocks
        if n > 8:
            cuts = [sum(splits[:i]) for i in range(len(splits) + 1)]
            parts = [evens[:, a:b].astype(F32) for a, b in zip(cuts, cuts[1:])]
            parts = [part.T if i in turned else part for i, part in enumerate(parts)]
            return parts + [odds[i : i + 1, :width].astype(F32) for i in range(2 * norms)]
        outs = tuple(
            shape((w, width) if i in turned else (width, w), F32) for i, w in enumerate(splits)
        )
        scratch = [pltpu.VMEM((width, columns), F32)]
        if norms:
            outs = outs + (shape((1, width), F32),) * 2
            scratch.append(pltpu.VMEM((8, 128 * n), F32))
        return call(
            functools.partial(join_kernel, n, splits, turned, norms),
            outs,
            [SM] + [VM] * (n // 2 + 1),
            24,
            scratch=scratch,
        )(meta, *evens, odds)

    mlp_columns = 3 * hidden_width
    even, odd = call(
        functools.partial(mlp_grad_kernel, n),
        block_shapes(mlp_columns),
        [SM] + [VM] * 5,
        24,
        scratch=[pltpu.VMEM((width, mlp_columns), F32)],
    )(meta, n2, gl, ul, hidden, cotangent)
    mlp_blocks = reduce_blocks(even, odd, "ctx", n)

    full = lambda *dims: pl.BlockSpec(dims, lambda g: (0,) * len(dims))
    gm, branch, gnorm_mlp, dq_t, even, odd = call(
        functools.partial(backward_kernel, n, wt),
        (
            shape((rows, width), F32),
            shape((rows, width), BF),
            shape((1, width), F32),
            shape((width, rows), F32),
            shape((n // 2, rows, kv_width), BF),
            shape((n // 2, rows, kv_width), BF),
        ),
        [VM] * wt
        + [SM, SM]
        + [VM] * 6
        + [
            pl.BlockSpec((n * rows, PAIR), lambda g: (0, g)),
            pl.BlockSpec((1, 2 * wide, PAIR), lambda g: (g, 0, 0)),
            VM,
            VM,
        ],
        big,
        scratch=[
            pltpu.VMEM((rows, width), F32),
            pltpu.VMEM((KV_HEADS, 2 * wide, PAIR), BF),
            pltpu.VMEM((2 * KV_HEADS, 1, wide), F32),
            pltpu.VMEM((n * rows, PAIR), F32),
            pltpu.VMEM((2, PAIR, wide), F32),
        ],
        out_specs=(
            full(rows, width),
            full(rows, width),
            full(1, width),
            pl.BlockSpec((GROUP * HEAD, rows), lambda g: (g, 0)),
            pl.BlockSpec((n // 2, rows, PAIR), lambda g: (0, 0, g)),
            pl.BlockSpec((n // 2, rows, PAIR), lambda g: (0, 0, g)),
        ),
        grid=(KV_HEADS,),
    )(
        *quarters,
        meta,
        stretch_order,
        mixed,
        cotangent,
        gain_mlp,
        w_out,
        att_t,
        lse.reshape(2 * KV_HEADS, 1, wide),
        kv_all,
        q,
        cos_t,
        sin_t,
    )
    kv_terms = scatter_terms(even, odd, "ctx", n)

    gn_query, even, odd = call(
        functools.partial(query_grad_kernel, n),
        (shape((rows, width), F32),) + block_shapes(2 * width),
        [SM] + [VM] * 5,
        24,
        scratch=[pltpu.VMEM((width, 2 * width), F32)],
    )(meta, normed, dq_t, att_low, branch, w_query)
    query_blocks = reduce_blocks(even, odd, "ctx", n)

    grad_tokens, even, odd = call(
        functools.partial(key_grad_kernel, n, len(kv_terms)),
        (shape((rows, width), F32),) + block_shapes(kv_width, 8),
        [SM] + [VM] * (len(kv_terms) + 10),
        24,
        scratch=[pltpu.VMEM((width, kv_width), F32), pltpu.VMEM((8, 128 * n), F32)],
    )(meta, *kv_terms, normed, gn_query, w_key, w_value, cos, sin, tokens, gain_attn, gm, gnorm_mlp)
    key_blocks = reduce_blocks(even, odd, "ctx", n)

    grad_gate, grad_up, grad_down = join(mlp_blocks, mlp_columns, (hidden_width,) * 3, (2,))
    grad_query, grad_out = join(query_blocks, 2 * width, (width, width))
    grad_key, grad_value, grad_norm_attn, grad_norm_mlp = join(
        key_blocks, kv_width, (kv_width // 2,) * 2, norms=True
    )
    return (
        output,
        grad_tokens,
        grad_query,
        grad_key,
        grad_value,
        grad_out,
        grad_norm_attn.reshape(width),
        grad_norm_mlp.reshape(width),
        grad_gate,
        grad_up,
        grad_down,
    )


def solution(mesh):
    return jax.shard_map(
        functools.partial(local, mesh.shape["ctx"], mesh.shape["wt"]),
        mesh=mesh,
        in_specs=(
            P("ctx", None),
            P(),
            P(),
            P(),
            P(),
            P(),
            P(),
            P(None, "wt"),
            P(None, "wt"),
            P("wt", None),
            P(),
            P("ctx", None),
        ),
        out_specs=(
            P("ctx", None),
            P("ctx", None),
            P(),
            P(),
            P(),
            P(),
            P(),
            P(),
            P(None, "wt"),
            P(None, "wt"),
            P("wt", None),
        ),
        check_vma=False,
    )
```

time: 442 us -> 182 us (0.41)
  waiting for transfers between devices: 193 us -> 41.5 us
  matrix products: 87.7 us -> 0 us
  local copies, waits for them, and re-layouts: 88 us -> 33.9 us
  starting transfers between devices: 0.34 us -> 39.9 us
  Pallas kernels: 0 us -> 39 us
  other arithmetic: 29.8 us -> 12 us
  blocking collectives: 14 us -> 0 us
  loops' own time: 13.1 us -> 0 us
    psum x2 -> x1, waiting for transfers between devices: 133 us -> 0.02 us  [local(): mlp_total = lax.psum(part_out, 'wt').astype(F32)]
    dot_general x77 -> x0, matrix products: 87.7 us -> none  [the longest x8 20.5 us: block_terms(): jnp.einsum('sgqd,sgkd->sgqk', out_groups, value_part, preferred_element_t...]
    ppermute x0 -> x38, waiting for transfers between devices: none -> 41.4 us  [hop(): return lax.ppermute(x, axis, [(i, i ^ k) for i in range(size)])]
    ppermute x0 -> x38, starting transfers between devices: none -> 39.9 us  [hop(): return lax.ppermute(x, axis, [(i, i ^ k) for i in range(size)])]
    pallas_call x0 -> x10, Pallas kernels: none -> 39 us  [the longest x1 13.2 us: local(): call(functools.partial(backward_kernel, n, wt), (shape((rows, width), F32...]
    reduce_scatter x1 -> x0, waiting for transfers between devices: 32.8 us -> none  [local(): lax.psum_scatter(terms.reshape(block_count * row_count, 2 * key_width), '...]
    all_gather x1 -> x0, waiting for transfers between devices: 26.5 us -> none  [local(): piece = lax.all_gather(keys_values, 'ctx', axis=0, tiled=True)]
    dynamic_slice x32 -> x0, local copies, waits for them, and re-layouts: 25.6 us -> none  [local(): lax.scan(block_step, initial, (blocks, jnp.arange(count, dtype=jnp.int32)))]
  transfers between devices with their start and end apart: 4 -> 39, of which waited for: 4 -> 18; matrix products, arithmetic and copies ran while one was open for 4% -> 12% of each run, Pallas kernels for 0% -> 12%
where the time goes in v1:
time: 182 us; the launch traced here: 181 us
  waiting for transfers between devices  41.5 us (23%)
  starting transfers between devices  39.9 us (22%)
  Pallas kernels  39 us (21%)
  local copies, waits for them, and re-layouts  33.9 us (19%)
  between operations  14.7 us (8%)
  other arithmetic  12 us (7%)
    ppermute x38, waiting for transfers between devices, hop(): return lax.ppermute(x, axis, [(i, i ^ k) for i in range(size)])  41.4 us
    ppermute x38, starting transfers between devices, hop(): return lax.ppermute(x, axis, [(i, i ^ k) for i in range(size)])  39.9 us
    unnamed x148, local copies, waits for them, and re-layouts  30.2 us
    pallas_call x1, Pallas kernels, local(): call(functools.partial(backward_kernel, n, wt), (shape((rows, width), F32...  13.2 us
    pallas_call x1, Pallas kernels, local(): call(functools.partial(forward_kernel, n, wt), (shape((n * rows, kv_width...  11.5 us
    pallas_call x3, Pallas kernels, join(): call(functools.partial(join_kernel, n, splits, turned, norms), outs, [SM]...  6.3 us
  transfers between devices with their start and end apart: 39, of which 18 were waited for; matrix products, arithmetic and copies ran while one was open for 12% of the time, Pallas kernels for 12%

profile of v1, /device:TPU:0, one launch (start us, length us, event | category | flops | bytes accessed | tf_op | source)
XLA Modules:
  0.0 181.0 jit_solution(382278210282516636)
XLA Ops:
  14.3 4.0 %collective-permute-start.2 = (bf16[256,384]{1,0:T(8,128)(2,1)S(1)}, bf16[256,384]{1,0:T(8,128)(2,1)S(1)}, u32[]{:S(2)}, u32[]{:S(2)}) collective-permute-start(bf16[256,384]{1,0:T(8,128)(2,1)S(1)} %get-tuple-element.50.refs_0_), channel_id=1, source_target_pairs={{0,24},{4,28},{8,16},{12,20},{16,8},{20,12},{24,0},{28,4},{1,25},{... | collective-permute-start | bytes 589832 | tf_op jit(solution)/shard_map/ppermute | solution.py:423
  18.9 5.1 %collective-permute-done.2.refs_3_ = bf16[256,384]{1,0:T(8,128)(2,1)S(1)} collective-permute-done((bf16[256,384]{1,0:T(8,128)(2,1)S(1)}, bf16[256,384]{1,0:T(8,128)(2,1)S(1)}, u32[]{:S(2)}, u32[]{:S(2)}) %collective-permute-start.2) | collective-permute-done | bytes 196640 | tf_op jit(solution)/shard_map/ppermute | solution.py:423
  24.0 3.3 %collective-permute-done.1.refs_2_ = bf16[256,384]{1,0:T(8,128)(2,1)S(1)} collective-permute-done((bf16[256,384]{1,0:T(8,128)(2,1)S(1)}, bf16[256,384]{1,0:T(8,128)(2,1)S(1)}, u32[]{:S(2)}, u32[]{:S(2)}) %collective-permute-start.1) | collective-permute-done | bytes 196640 | tf_op jit(solution)/shard_map/ppermute | solution.py:423
  35.8 11.5 %shard_map.205 = (bf16[2048,384]{1,0:T(8,128)(2,1)S(1)}, f32[576,256]{1,0:T(8,128)S(1)}, bf16[256,576]{1,0:T(8,128)(2,1)S(1)}, f32[6,384]{1,0:T(8,128)S(1)}, f32...) custom-call(bf16[256,384]{1,0:T(8,128)(2,1)S(1)} %copy-done.16, ...), custom_call_target="tpu_custom_call" | custom-call | bytes 4194304 | tf_op jit(solution)/shard_map/pallas_call | solution.py:501
  49.4 2.2 %shard_map.211 = (bf16[4,72,1152]{2,1,0:T(8,128)(2,1)S(1)}, bf16[4,72,1152]{2,1,0:T(8,128)(2,1)}) custom-call(s32[2]{0:T(128)S(1)} %pad_add_fusion.refs_4_.meta, bf16[256,576]{1,0:T(8,128)(2,1)S(1)} %get-tuple-element.80.n2, bf16[256,384]{1,0:T(8,128)(2,1)S(1)} %get-tuple-element.81.gl, bf16[256,384]{1,0:T(8,128)(2,1)S(1)} %get-tuple-element.82.ul, ...), custom_call_target="tpu_custom_call" | custom-call | bytes 4194304 | tf_op jit(solution)/shard_map/pallas_call | solution.py:569
  52.9 1.6 collective-permute-start.4
  54.5 2.6 %collective-permute-start.5 = (bf16[64,576]{1,0:T(8,128)(2,1)S(1)}, bf16[64,576]{1,0:T(8,128)(2,1)S(1)}, u32[]{:S(2)}, u32[]{:S(2)}) collective-permute-start(bf16[64,576]{1,0:T(8,128)(2,1)S(1)} %get-tuple-element.56), channel_id=1, source_target_pairs={{0,2},{1,3},{2,0},{3,1},{4,6},{5,7},{6,4},{7,5},{8,10},{9,11},{10,... | collective-permute-start | bytes 221192 | tf_op jit(solution)/shard_map/ppermute | solution.py:423
  57.4 6.6 %collective-permute-done.5 = bf16[64,576]{1,0:T(8,128)(2,1)S(1)} collective-permute-done((bf16[64,576]{1,0:T(8,128)(2,1)S(1)}, bf16[64,576]{1,0:T(8,128)(2,1)S(1)}, u32[]{:S(2)}, u32[]{:S(2)}) %collective-permute-start.5) | collective-permute-done | bytes 73760 | tf_op jit(solution)/shard_map/ppermute | solution.py:423
  64.0 2.5 %collective-permute-start.9 = (bf16[64,576]{1,0:T(8,128)(2,1)S(1)}, bf16[64,576]{1,0:T(8,128)(2,1)}, u32[]{:S(2)}, u32[]{:S(2)}) collective-permute-start(bf16[64,576]{1,0:T(8,128)(2,1)S(1)} %add_convert_fusion.1.refs_0_), channel_id=1, source_target_pairs={{0,3},{1,2},{2,1},{3,0},{4,7},{5,6},{6,5},{7,4},{8,11},{9,10},{10,... | collective-permute-start | bytes 221192 | tf_op jit(solution)/shard_map/ppermute | solution.py:423
  67.0 1.4 collective-permute-start.7
  68.5 1.6 copy.49.refs_14_
  71.5 2.0 %collective-permute-done.8.refs_2_ = bf16[64,576]{1,0:T(8,128)(2,1)} collective-permute-done((bf16[64,576]{1,0:T(8,128)(2,1)S(1)}, bf16[64,576]{1,0:T(8,128)(2,1)}, u32[]{:S(2)}, u32[]{:S(2)}) %collective-permute-start.8) | collective-permute-done | bytes 73760 | tf_op jit(solution)/shard_map/ppermute | solution.py:423
  80.7 13.2 %shard_map.206 = (f32[256,576]{1,0:T(8,128)S(1)}, bf16[256,576]{1,0:T(8,128)(2,1)S(1)}, f32[1,576]{1,0:T(1,128)S(1)}, f32[576,256]{1,0:T(8,128)S(1)}, bf16[4,256...) custom-call(bf16[64,576]{1,0:T(8,128)(2,1)S(1)} %add_convert_fusion.1.refs_0_, ...), custom_call_target="tpu_custom_call" | custom-call | bytes 4194304 | tf_op jit(solution)/shard_map/pallas_call | solution.py:579
  94.0 2.5 %shard_map.207 = (f32[256,576]{1,0:T(8,128)S(1)}, bf16[4,72,1152]{2,1,0:T(8,128)(2,1)S(1)}, bf16[4,72,1152]{2,1,0:T(8,128)(2,1)}) custom-call(s32[2]{0:T(128)S(1)} %copy-done.55, bf16[256,576]{1,0:T(8,128)(2,1)S(1)} %get-tuple-element.51.normed.refs_4_, f32[576,256]{1,0:T(8,128)S(1)} %get-tuple-element.63.dq_t, bf16[256,576]{1,0:T(8,128)(2,1)S(1)} %copy-done.48, ...), custom_call_target="tpu_custom_call" | custom-call | bytes 4194304 | tf_op jit(solution)/shard_map/pallas_call | solution.py:632
  99.3 1.6 collective-permute-start.31
  103.1 1.6 collective-permute-start.15
  107.9 3.0 %collective-permute-done.33 = bf16[72,1152]{1,0:T(8,128)(2,1)S(1)} collective-permute-done((bf16[72,1152]{1,0:T(8,128)(2,1)S(1)}, bf16[72,1152]{1,0:T(8,128)(2,1)S(1)}, u32[]{:S(2)}, u32[]{:S(2)}) %collective-permute-start.33) | collective-permute-done | bytes 165920 | tf_op jit(solution)/shard_map/ppermute | solution.py:423
  110.9 1.5 collective-permute-start.13
  112.9 1.6 collective-permute-start.36
  115.2 2.9 %collective-permute-done.17 = bf16[72,1152]{1,0:T(8,128)(2,1)S(1)} collective-permute-done((bf16[72,1152]{1,0:T(8,128)(2,1)S(1)}, bf16[72,1152]{1,0:T(8,128)(2,1)S(1)}, u32[]{:S(2)}, u32[]{:S(2)}) %collective-permute-start.17) | collective-permute-done | bytes 165920 | tf_op jit(solution)/shard_map/ppermute | solution.py:423
  118.9 8.7 %collective-permute-done.16 = bf16[72,1152]{1,0:T(8,128)(2,1)S(1)} collective-permute-done((bf16[72,1152]{1,0:T(8,128)(2,1)S(1)}, bf16[72,1152]{1,0:T(8,128)(2,1)S(1)}, u32[]{:S(2)}, u32[]{:S(2)}) %collective-permute-start.16) | collective-permute-done | bytes 165920 | tf_op jit(solution)/shard_map/ppermute | solution.py:423
  128.2 1.5 collective-permute-start.11
  130.7 3.3 %collective-permute-done.12.refs_2_ = bf16[256,384]{1,0:T(8,128)(2,1)S(1)} collective-permute-done((bf16[256,384]{1,0:T(8,128)(2,1)S(1)}, bf16[256,384]{1,0:T(8,128)(2,1)S(1)}, u32[]{:S(2)}, u32[]{:S(2)}) %collective-permute-start.12) | collective-permute-done | bytes 196640 | tf_op jit(solution)/shard_map/ppermute | solution.py:423
  134.0 1.5 collective-permute-start.20
  136.3 1.5 shard_map.208
  147.9 1.6 collective-permute-start.28
  151.5 2.1 %collective-permute-done.28.refs_3_ = bf16[80,384]{1,0:T(8,128)(2,1)S(1)} collective-permute-done((bf16[80,384]{1,0:T(8,128)(2,1)S(1)}, bf16[80,384]{1,0:T(8,128)(2,1)S(1)}, u32[]{:S(2)}, u32[]{:S(2)}) %collective-permute-start.28) | collective-permute-done | bytes 61472 | tf_op jit(solution)/shard_map/ppermute | solution.py:423
  155.7 1.8 %add_convert_fusion = bf16[256,576]{1,0:T(8,128)(2,1)} fusion(f32[256,576]{1,0:T(8,128)S(1)} %copy-done.6, bf16[256,576]{1,0:T(8,128)(2,1)} %all-reduce.2.cloned.1.call-done), kind=kLoop, calls=%fused_computation.3 | loop fusion | flops 442368 | bytes 1179648 | tf_op jit(solution)/shard_map/convert_element_type | solution.py:537
  157.5 1.8 %copy.55 = bf16[256,576]{0,1:T(8,128)(2,1)} copy(bf16[256,576]{1,0:T(8,128)(2,1)} %add_convert_fusion) | data formatting | bytes 589824
  159.4 2.1 %copy.56 = f32[256,576]{0,1:T(8,128)} copy(f32[256,576]{1,0:T(8,128)} %copy-done.38) | data formatting | bytes 1179648
  163.4 2.2 %shard_map.212 = (f32[576,384]{1,0:T(8,128)}, f32[576,384]{1,0:T(8,128)}, f32[384,576]{1,0:T(8,128)S(1)}) custom-call(s32[2]{0:T(128)S(1)} %copy-done.56, bf16[72,1152]{1,0:T(8,128)(2,1)S(1)} %fusion.11.refs_0_, bf16[72,1152]{1,0:T(8,128)(2,1)S(1)} %copy-done.35, bf16[72,1152]{1,0:T(8,128)(2,1)S(1)} %copy-done.31, bf16[72,1152]{1,0:T(8,128)(2,1)S(1)} %copy-done.29, ...), custom_call_target="tpu_custom_call" | custom-call | bytes 4194304 | tf_op jit(solution)/shard_map/pallas_call | solution.py:560
  171.4 2.8 %shard_map.209 = (f32[576,576]{1,0:T(8,128)}, f32[576,576]{1,0:T(8,128)}) custom-call(s32[2]{0:T(128)S(1)} %copy-done.56, bf16[72,1152]{1,0:T(8,128)(2,1)S(1)} %fusion.19.refs_0_, bf16[72,1152]{1,0:T(8,128)(2,1)S(1)} %collective-permute-done.18.refs_1_, bf16[72,1152]{1,0:T(8,128)(2,1)S(1)} %copy-done.37, bf16[72,1152]{1,0:T(8,128)(2,1)S(1)} %copy-done.33, ...), custom_call_target="tpu_custom_call" | custom-call | bytes 4194304 | tf_op jit(solution)/shard_map/pallas_call | solution.py:560
  (235 shorter events, 63.0 us)
Async XLA Ops:
  7.2 148.5 %all-reduce.2.cloned.1.call-start = ((), (), s32[]{:S(2)}) async-start(), calls=%async_computation | async-start | bytes 655360 | tf_op jit(solution)/shard_map/psum | solution.py:536
  14.3 9.7 %collective-permute-start.2 = (bf16[256,384]{1,0:T(8,128)(2,1)S(1)}, bf16[256,384]{1,0:T(8,128)(2,1)S(1)}, u32[]{:S(2)}, u32[]{:S(2)}) collective-permute-start(bf16[256,384]{1,0:T(8,128)(2,1)S(1)} %get-tuple-element.50.refs_0_), channel_id=1, source_target_pairs={{0,24},{4,28},{8,16},{12,20},{16,8},{20,12},{24,0},{28,4},{1,25},{... | collective-permute-start | bytes 589832 | tf_op jit(solution)/shard_map/ppermute | solution.py:423
  18.3 9.1 %collective-permute-start.1 = (bf16[256,384]{1,0:T(8,128)(2,1)S(1)}, bf16[256,384]{1,0:T(8,128)(2,1)S(1)}, u32[]{:S(2)}, u32[]{:S(2)}) collective-permute-start(bf16[256,384]{1,0:T(8,128)(2,1)S(1)} %get-tuple-element.50.refs_0_), channel_id=1, source_target_pairs={{0,16},{4,20},{8,24},{12,28},{16,0},{20,4},{24,8},{28,12},{1,17},{... | collective-permute-start | bytes 589832 | tf_op jit(solution)/shard_map/ppermute | solution.py:423
  18.8 8.9 %collective-permute-start = (bf16[256,384]{1,0:T(8,128)(2,1)S(1)}, bf16[256,384]{1,0:T(8,128)(2,1)S(1)}, u32[]{:S(2)}, u32[]{:S(2)}) collective-permute-start(bf16[256,384]{1,0:T(8,128)(2,1)S(1)} %get-tuple-element.50.refs_0_), channel_id=1, source_target_pairs={{0,8},{4,12},{8,0},{12,4},{16,24},{20,28},{24,16},{28,20},{1,9},{5... | collective-permute-start | bytes 589832 | tf_op jit(solution)/shard_map/ppermute | solution.py:423
  52.4 45.5 %collective-permute-start.30 = (bf16[4,72,1152]{2,1,0:T(8,128)(2,1)}, bf16[4,72,1152]{2,1,0:T(8,128)(2,1)}, u32[]{:S(2)}, u32[]{:S(2)}) collective-permute-start(bf16[4,72,1152]{2,1,0:T(8,128)(2,1)} %get-tuple-element.85), channel_id=1, source_target_pairs={{0,4},{4,0},{8,12},{12,8},{16,20},{20,16},{24,28},{28,24},{1,5},{5... | collective-permute-start | bytes 1990664 | tf_op jit(solution)/shard_map/ppermute | solution.py:423
  54.5 9.4 %collective-permute-start.5 = (bf16[64,576]{1,0:T(8,128)(2,1)S(1)}, bf16[64,576]{1,0:T(8,128)(2,1)S(1)}, u32[]{:S(2)}, u32[]{:S(2)}) collective-permute-start(bf16[64,576]{1,0:T(8,128)(2,1)S(1)} %get-tuple-element.56), channel_id=1, source_target_pairs={{0,2},{1,3},{2,0},{3,1},{4,6},{5,7},{6,4},{7,5},{8,10},{9,11},{10,... | collective-permute-start | bytes 221192 | tf_op jit(solution)/shard_map/ppermute | solution.py:423
  57.1 6.9 %collective-permute-start.6 = (bf16[64,576]{1,0:T(8,128)(2,1)S(1)}, bf16[64,576]{1,0:T(8,128)(2,1)S(1)}, u32[]{:S(2)}, u32[]{:S(2)}) collective-permute-start(bf16[64,576]{1,0:T(8,128)(2,1)S(1)} %get-tuple-element.57), channel_id=1, source_target_pairs={{0,3},{1,2},{2,1},{3,0},{4,7},{5,6},{6,5},{7,4},{8,11},{9,10},{10,... | collective-permute-start | bytes 221192 | tf_op jit(solution)/shard_map/ppermute | solution.py:423
  64.0 7.5 %collective-permute-start.9 = (bf16[64,576]{1,0:T(8,128)(2,1)S(1)}, bf16[64,576]{1,0:T(8,128)(2,1)}, u32[]{:S(2)}, u32[]{:S(2)}) collective-permute-start(bf16[64,576]{1,0:T(8,128)(2,1)S(1)} %add_convert_fusion.1.refs_0_), channel_id=1, source_target_pairs={{0,3},{1,2},{2,1},{3,0},{4,7},{5,6},{6,5},{7,4},{8,11},{9,10},{10,... | collective-permute-start | bytes 221192 | tf_op jit(solution)/shard_map/ppermute | solution.py:423
  66.5 6.9 %collective-permute-start.8 = (bf16[64,576]{1,0:T(8,128)(2,1)S(1)}, bf16[64,576]{1,0:T(8,128)(2,1)}, u32[]{:S(2)}, u32[]{:S(2)}) collective-permute-start(bf16[64,576]{1,0:T(8,128)(2,1)S(1)} %add_convert_fusion.1.refs_0_), channel_id=1, source_target_pairs={{0,2},{1,3},{2,0},{3,1},{4,6},{5,7},{6,4},{7,5},{8,10},{9,11},{10,... | collective-permute-start | bytes 221192 | tf_op jit(solution)/shard_map/ppermute | solution.py:423
  67.0 6.4 %collective-permute-start.7 = (bf16[64,576]{1,0:T(8,128)(2,1)S(1)}, bf16[64,576]{1,0:T(8,128)(2,1)}, u32[]{:S(2)}, u32[]{:S(2)}) collective-permute-start(bf16[64,576]{1,0:T(8,128)(2,1)S(1)} %add_convert_fusion.1.refs_0_), channel_id=1, source_target_pairs={{0,1},{1,0},{2,3},{3,2},{4,5},{5,4},{6,7},{7,6},{8,9},{9,8},{10,11... | collective-permute-start | bytes 221192 | tf_op jit(solution)/shard_map/ppermute | solution.py:423
  97.3 5.5 %collective-permute-start.14 = (bf16[4,72,1152]{2,1,0:T(8,128)(2,1)}, bf16[4,72,1152]{2,1,0:T(8,128)(2,1)S(1)}, u32[]{:S(2)}, u32[]{:S(2)}) collective-permute-start(bf16[4,72,1152]{2,1,0:T(8,128)(2,1)} %get-tuple-element.71), channel_id=1, source_target_pairs={{0,4},{4,0},{8,12},{12,8},{16,20},{20,16},{24,28},{28,24},{1,5},{5... | collective-permute-start | bytes 1990664 | tf_op jit(solution)/shard_map/ppermute | solution.py:423
  97.4 7.2 %collective-permute-start.10 = (bf16[4,256,384]{2,1,0:T(8,128)(2,1)}, bf16[4,256,384]{2,1,0:T(8,128)(2,1)S(1)}, u32[]{:S(2)}, u32[]{:S(2)}) collective-permute-start(bf16[4,256,384]{2,1,0:T(8,128)(2,1)} %copy-done.66), channel_id=1, source_target_pairs={{0,4},{4,0},{8,12},{12,8},{16,20},{20,16},{24,28},{28,24},{1,5},{5... | collective-permute-start | bytes 2359304 | tf_op jit(solution)/shard_map/ppermute | solution.py:423
  99.3 7.2 %collective-permute-start.31 = (bf16[72,1152]{1,0:T(8,128)(2,1)S(1)}, bf16[72,1152]{1,0:T(8,128)(2,1)S(1)}, u32[]{:S(2)}, u32[]{:S(2)}) collective-permute-start(bf16[72,1152]{1,0:T(8,128)(2,1)S(1)} %get-tuple-element.115), channel_id=1, source_target_pairs={{0,8},{4,12},{8,0},{12,4},{16,24},{20,28},{24,16},{28,20},{1,9},{5... | collective-permute-start | bytes 497672 | tf_op jit(solution)/shard_map/ppermute | solution.py:423
  100.8 10.1 %collective-permute-start.33 = (bf16[72,1152]{1,0:T(8,128)(2,1)S(1)}, bf16[72,1152]{1,0:T(8,128)(2,1)S(1)}, u32[]{:S(2)}, u32[]{:S(2)}) collective-permute-start(bf16[72,1152]{1,0:T(8,128)(2,1)S(1)} %get-tuple-element.116), channel_id=1, source_target_pairs={{0,24},{4,28},{8,16},{12,20},{16,8},{20,12},{24,0},{28,4},{1,25},{... | collective-permute-start | bytes 497672 | tf_op jit(solution)/shard_map/ppermute | solution.py:423
  102.2 10.6 %collective-permute-start.32 = (bf16[72,1152]{1,0:T(8,128)(2,1)S(1)}, bf16[72,1152]{1,0:T(8,128)(2,1)S(1)}, u32[]{:S(2)}, u32[]{:S(2)}) collective-permute-start(bf16[72,1152]{1,0:T(8,128)(2,1)S(1)} %get-tuple-element.117), channel_id=1, source_target_pairs={{0,16},{4,20},{8,24},{12,28},{16,0},{20,4},{24,8},{28,12},{1,17},{... | collective-permute-start | bytes 497672 | tf_op jit(solution)/shard_map/ppermute | solution.py:423
  103.1 11.4 %collective-permute-start.15 = (bf16[72,1152]{1,0:T(8,128)(2,1)S(1)}, bf16[72,1152]{1,0:T(8,128)(2,1)S(1)}, u32[]{:S(2)}, u32[]{:S(2)}) collective-permute-start(bf16[72,1152]{1,0:T(8,128)(2,1)S(1)} %get-tuple-element.118), channel_id=1, source_target_pairs={{0,8},{4,12},{8,0},{12,4},{16,24},{20,28},{24,16},{28,20},{1,9},{5... | collective-permute-start | bytes 497672 | tf_op jit(solution)/shard_map/ppermute | solution.py:423
  104.6 13.5 %collective-permute-start.17 = (bf16[72,1152]{1,0:T(8,128)(2,1)S(1)}, bf16[72,1152]{1,0:T(8,128)(2,1)S(1)}, u32[]{:S(2)}, u32[]{:S(2)}) collective-permute-start(bf16[72,1152]{1,0:T(8,128)(2,1)S(1)} %get-tuple-element.119), channel_id=1, source_target_pairs={{0,24},{4,28},{8,16},{12,20},{16,8},{20,12},{24,0},{28,4},{1,25},{... | collective-permute-start | bytes 497672 | tf_op jit(solution)/shard_map/ppermute | solution.py:423
  106.4 21.1 %collective-permute-start.16 = (bf16[72,1152]{1,0:T(8,128)(2,1)S(1)}, bf16[72,1152]{1,0:T(8,128)(2,1)S(1)}, u32[]{:S(2)}, u32[]{:S(2)}) collective-permute-start(bf16[72,1152]{1,0:T(8,128)(2,1)S(1)} %get-tuple-element.120), channel_id=1, source_target_pairs={{0,16},{4,20},{8,24},{12,28},{16,0},{20,4},{24,8},{28,12},{1,17},{... | collective-permute-start | bytes 497672 | tf_op jit(solution)/shard_map/ppermute | solution.py:423
  110.9 17.3 %collective-permute-start.13 = (bf16[256,384]{1,0:T(8,128)(2,1)S(1)}, bf16[256,384]{1,0:T(8,128)(2,1)S(1)}, u32[]{:S(2)}, u32[]{:S(2)}) collective-permute-start(bf16[256,384]{1,0:T(8,128)(2,1)S(1)} %get-tuple-element.111), channel_id=1, source_target_pairs={{0,24},{4,28},{8,16},{12,20},{16,8},{20,12},{24,0},{28,4},{1,25},{... | collective-permute-start | bytes 589832 | tf_op jit(solution)/shard_map/ppermute | solution.py:423
  112.9 25.0 %collective-permute-start.36 = (bf16[72,1152]{1,0:T(8,128)(2,1)S(1)}, bf16[72,1152]{1,0:T(8,128)(2,1)S(1)}, u32[]{:S(2)}, u32[]{:S(2)}) collective-permute-start(bf16[72,1152]{1,0:T(8,128)(2,1)S(1)} %fusion.11.refs_0_), channel_id=1, source_target_pairs={{0,24},{4,28},{8,16},{12,20},{16,8},{20,12},{24,0},{28,4},{1,25},{... | collective-permute-start | bytes 497672 | tf_op jit(solution)/shard_map/ppermute | solution.py:423
  114.5 24.7 %collective-permute-start.35 = (bf16[72,1152]{1,0:T(8,128)(2,1)S(1)}, bf16[72,1152]{1,0:T(8,128)(2,1)S(1)}, u32[]{:S(2)}, u32[]{:S(2)}) collective-permute-start(bf16[72,1152]{1,0:T(8,128)(2,1)S(1)} %fusion.11.refs_0_), channel_id=1, source_target_pairs={{0,16},{4,20},{8,24},{12,28},{16,0},{20,4},{24,8},{28,12},{1,17},{... | collective-permute-start | bytes 497672 | tf_op jit(solution)/shard_map/ppermute | solution.py:423
  118.1 21.1 %collective-permute-start.34 = (bf16[72,1152]{1,0:T(8,128)(2,1)S(1)}, bf16[72,1152]{1,0:T(8,128)(2,1)S(1)}, u32[]{:S(2)}, u32[]{:S(2)}) collective-permute-start(bf16[72,1152]{1,0:T(8,128)(2,1)S(1)} %fusion.11.refs_0_), channel_id=1, source_target_pairs={{0,8},{4,12},{8,0},{12,4},{16,24},{20,28},{24,16},{28,20},{1,9},{5... | collective-permute-start | bytes 497672 | tf_op jit(solution)/shard_map/ppermute | solution.py:423
  127.6 6.5 %collective-permute-start.12 = (bf16[256,384]{1,0:T(8,128)(2,1)S(1)}, bf16[256,384]{1,0:T(8,128)(2,1)S(1)}, u32[]{:S(2)}, u32[]{:S(2)}) collective-permute-start(bf16[256,384]{1,0:T(8,128)(2,1)S(1)} %get-tuple-element.112), channel_id=1, source_target_pairs={{0,16},{4,20},{8,24},{12,28},{16,0},{20,4},{24,8},{28,12},{1,17},{... | collective-permute-start | bytes 589832 | tf_op jit(solution)/shard_map/ppermute | solution.py:423
  128.2 7.4 %collective-permute-start.11 = (bf16[256,384]{1,0:T(8,128)(2,1)S(1)}, bf16[256,384]{1,0:T(8,128)(2,1)S(1)}, u32[]{:S(2)}, u32[]{:S(2)}) collective-permute-start(bf16[256,384]{1,0:T(8,128)(2,1)S(1)} %get-tuple-element.113), channel_id=1, source_target_pairs={{0,8},{4,12},{8,0},{12,4},{16,24},{20,28},{24,16},{28,20},{1,9},{5... | collective-permute-start | bytes 589832 | tf_op jit(solution)/shard_map/ppermute | solution.py:423
  134.0 7.7 %collective-permute-start.20 = (bf16[72,1152]{1,0:T(8,128)(2,1)S(1)}, bf16[72,1152]{1,0:T(8,128)(2,1)S(1)}, u32[]{:S(2)}, u32[]{:S(2)}) collective-permute-start(bf16[72,1152]{1,0:T(8,128)(2,1)S(1)} %fusion.19.refs_0_), channel_id=1, source_target_pairs={{0,24},{4,28},{8,16},{12,20},{16,8},{20,12},{24,0},{28,4},{1,25},{... | collective-permute-start | bytes 497672 | tf_op jit(solution)/shard_map/ppermute | solution.py:423
  135.6 7.8 %collective-permute-start.19 = (bf16[72,1152]{1,0:T(8,128)(2,1)S(1)}, bf16[72,1152]{1,0:T(8,128)(2,1)S(1)}, u32[]{:S(2)}, u32[]{:S(2)}) collective-permute-start(bf16[72,1152]{1,0:T(8,128)(2,1)S(1)} %fusion.19.refs_0_), channel_id=1, source_target_pairs={{0,16},{4,20},{8,24},{12,28},{16,0},{20,4},{24,8},{28,12},{1,17},{... | collective-permute-start | bytes 497672 | tf_op jit(solution)/shard_map/ppermute | solution.py:423
  137.9 6.5 %collective-permute-start.18 = (bf16[72,1152]{1,0:T(8,128)(2,1)S(1)}, bf16[72,1152]{1,0:T(8,128)(2,1)S(1)}, u32[]{:S(2)}, u32[]{:S(2)}) collective-permute-start(bf16[72,1152]{1,0:T(8,128)(2,1)S(1)} %fusion.19.refs_0_), channel_id=1, source_target_pairs={{0,8},{4,12},{8,0},{12,4},{16,24},{20,28},{24,16},{28,20},{1,9},{5... | collective-permute-start | bytes 497672 | tf_op jit(solution)/shard_map/ppermute | solution.py:423
  140.2 21.3 %collective-permute-start.37 = (bf16[4,72,1152]{2,1,0:T(8,128)(2,1)}, bf16[4,72,1152]{2,1,0:T(8,128)(2,1)S(1)}, u32[]{:S(2)}, u32[]{:S(2)}) collective-permute-start(bf16[4,72,1152]{2,1,0:T(8,128)(2,1)} %pad_maximum_fusion.2), channel_id=1, source_target_pairs={{0,4},{4,0},{8,12},{12,8},{16,20},{20,16},{24,28},{28,24},{1,5},{5... | collective-permute-start | bytes 1990664 | tf_op jit(solution)/shard_map/ppermute | solution.py:423
  140.8 5.2 %collective-permute-start.23 = (bf16[80,384]{1,0:T(8,128)(2,1)S(1)}, bf16[80,384]{1,0:T(8,128)(2,1)S(1)}, u32[]{:S(2)}, u32[]{:S(2)}) collective-permute-start(bf16[80,384]{1,0:T(8,128)(2,1)S(1)} %get-tuple-element.121), channel_id=1, source_target_pairs={{0,8},{4,12},{8,0},{12,4},{16,24},{20,28},{24,16},{28,20},{1,9},{5... | collective-permute-start | bytes 184328 | tf_op jit(solution)/shard_map/ppermute | solution.py:423
  146.0 25.4 %collective-permute-start.21 = (bf16[4,72,1152]{2,1,0:T(8,128)(2,1)}, bf16[4,72,1152]{2,1,0:T(8,128)(2,1)S(1)}, u32[]{:S(2)}, u32[]{:S(2)}) collective-permute-start(bf16[4,72,1152]{2,1,0:T(8,128)(2,1)} %pad_maximum_fusion.1), channel_id=1, source_target_pairs={{0,4},{4,0},{8,12},{12,8},{16,20},{20,16},{24,28},{28,24},{1,5},{5... | collective-permute-start | bytes 1990664 | tf_op jit(solution)/shard_map/ppermute | solution.py:423
  147.9 5.7 %collective-permute-start.28 = (bf16[80,384]{1,0:T(8,128)(2,1)S(1)}, bf16[80,384]{1,0:T(8,128)(2,1)S(1)}, u32[]{:S(2)}, u32[]{:S(2)}) collective-permute-start(bf16[80,384]{1,0:T(8,128)(2,1)S(1)} %fusion.36.refs_0_), channel_id=1, source_target_pairs={{0,24},{4,28},{8,16},{12,20},{16,8},{20,12},{24,0},{28,4},{1,25},{... | collective-permute-start | bytes 184328 | tf_op jit(solution)/shard_map/ppermute | solution.py:423
  155.6 11.3 %collective-permute-start.29 = (bf16[4,80,384]{2,1,0:T(8,128)(2,1)}, bf16[4,80,384]{2,1,0:T(8,128)(2,1)}, u32[]{:S(2)}, u32[]{:S(2)}) collective-permute-start(bf16[4,80,384]{2,1,0:T(8,128)(2,1)} %pad_maximum_fusion.3), channel_id=1, source_target_pairs={{0,4},{4,0},{8,12},{12,8},{16,20},{20,16},{24,28},{28,24},{1,5},{5... | collective-permute-start | bytes 737288 | tf_op jit(solution)/shard_map/ppermute | solution.py:423
  (76 other events, 511.5 us)
Sparse Core Ops, SparseCore 0:
  97.5 34.7 all-reduce.1

commit v2 on v1

v2 whole, which is shorter than its diff:
```python
import functools

import jax
import jax.numpy as jnp
import numpy as np
from jax import lax
from jax.experimental import pallas as pl
from jax.experimental.pallas import tpu as pltpu
from jax.sharding import PartitionSpec as P

Q_HEADS = 9
KV_HEADS = 3
GROUP = 3
HEAD = 64
HALF = 32
PAIR = 2 * HEAD
EPSILON = 1e-05
THETA = 100000.0
NEGATIVE = -1e30
BF = jnp.bfloat16
F32 = jnp.float32
MIB = 1 << 20


def dot(left, right):
    return jnp.dot(left, right, preferred_element_type=F32)


def dot_nt(left, right):
    return lax.dot_general(left, right, (((1,), (1,)), ((), ())), preferred_element_type=F32)


def dot_tn(left, right):
    return lax.dot_general(left, right, (((0,), (0,)), ((), ())), preferred_element_type=F32)


def shape(dims, dtype):
    return jax.ShapeDtypeStruct(dims, dtype)


SPEC = {
    "v": pl.BlockSpec(memory_space=pltpu.VMEM),
    "s": pl.BlockSpec(memory_space=pltpu.SMEM),
    "h": pl.BlockSpec(memory_space=pltpu.HBM),
    "c": pl.BlockSpec(memory_space=pltpu.HBM),
}


class Fetched:
    def __init__(self, copy, ref):
        self.copy, self.ref, self.waited = copy, ref, False

    def get(self):
        if not self.waited:
            self.copy.wait()
            self.waited = True
        return self.ref


class Stored:
    def __init__(self, copy, ref):
        self.copy, self.ref, self.sent = copy, ref, False

    def send(self):
        self.copy.start()
        self.sent = True


def call(body, ins, in_kinds, outs, out_kinds, scratch=(), vmem=60, flops=0):
    real = [(a, kind) for a, kind in zip(ins, in_kinds) if kind != "m"]
    staged = [a for a, kind in real if kind == "c"]
    staged_out = [o for o, kind in zip(outs, out_kinds) if kind == "c"]
    count = len(staged) + len(staged_out)
    buffers = [pltpu.VMEM(a.shape, a.dtype) for a in staged + staged_out]
    if count:
        buffers.append(pltpu.SemaphoreType.DMA((count,)))

    def kernel(*refs):
        in_refs = iter(refs[: len(real)])
        out_refs = refs[len(real) : len(real) + len(outs)]
        own = refs[len(real) + len(outs) : len(refs) - len(buffers)]
        extra = refs[len(refs) - len(buffers) :]
        at = 0
        given, results = [], []
        for kind in in_kinds:
            ref = (lax.axis_index("ctx"), lax.axis_index("wt")) if kind == "m" else next(in_refs)
            if kind == "c":
                copy = pltpu.make_async_copy(ref, extra[at], extra[-1].at[at])
                copy.start()
                ref = Fetched(copy, extra[at])
                at += 1
            given.append(ref)
        for ref, kind in zip(out_refs, out_kinds):
            if kind == "c":
                ref = Stored(pltpu.make_async_copy(extra[at], ref, extra[-1].at[at]), extra[at])
                at += 1
            results.append(ref)
        body(given, results, own)
        for item in given:
            if isinstance(item, Fetched):
                item.get()
        for item in results:
            if isinstance(item, Stored):
                if not item.sent:
                    item.send()
                item.copy.wait()

    return pl.pallas_call(
        kernel,
        out_shape=tuple(outs),
        in_specs=[SPEC[k] for _, k in real],
        out_specs=tuple(SPEC[k] for k in out_kinds),
        scratch_shapes=list(scratch) + buffers,
        compiler_params=pltpu.CompilerParams(vmem_limit_bytes=vmem * MIB),
        cost_estimate=pl.CostEstimate(flops=flops, bytes_accessed=4 * MIB, transcendentals=0),
    )(*[a for a, _ in real])


def angle_tables(n, stretch):
    rates = THETA ** (-np.arange(HALF, dtype=np.float64) / HALF)
    places = np.arange(2 * n * stretch, dtype=np.float64).reshape(2 * n, 1, stretch)
    angle = places * rates[None, :, None]
    turned = np.concatenate([np.cos(angle), np.sin(angle)], axis=1).astype(np.float32)
    sign = np.concatenate([np.ones(HALF), -np.ones(HALF)])
    lanes = np.concatenate([rates, rates])
    start = np.arange(2 * n)[:, None] * stretch * lanes[None, :]
    offset = np.arange(stretch)[:, None] * lanes[None, :]

    def widen(table, fill):
        return np.concatenate([table, np.full(table.shape, fill)], axis=1).astype(np.float32)

    first = np.stack([widen(np.cos(start), 1.0), widen(np.sin(start) * sign, 0.0)], axis=1)
    inner = np.stack([widen(np.cos(offset), 1.0), widen(np.sin(offset) * sign, 0.0)])
    return turned, first, inner


def row_of(ref):
    return ref[...].astype(F32).reshape(1, ref.shape[0])


def norm_scale(x, axis):
    return lax.rsqrt(jnp.mean(x * x, axis=axis, keepdims=True) + EPSILON)


def key_body(ins, outs, scratch):
    meta, order, gain, tok, wk, wv, turned = ins
    normed_out, kv_out, angle_out, normed_q = outs
    (normed_s,) = scratch
    me = meta[0]
    low, high = order[0, 2 * me], order[0, 2 * me + 1]
    x = tok[...].astype(F32)
    gain = jnp.broadcast_to(row_of(gain), (8, x.shape[0])).T[:, 0:1]
    normed = (x * norm_scale(x, 0) * gain).astype(BF)
    normed_out[...] = normed
    normed_s[...] = normed.astype(F32)
    normed_q[...] = normed_s[span(meta[1], normed_q.shape[0]), :].astype(BF)
    turned = turned.get()
    angle = jnp.concatenate([turned[low], turned[high]], axis=1)
    angle_out[...] = angle
    cos, sin = angle[:HALF], angle[HALF:]
    k = dot(wk.get()[...], normed)
    v = dot(wv.get()[...], normed)
    parts = []
    for g in range(KV_HEADS):
        a, b = k[g * HEAD : g * HEAD + HALF], k[g * HEAD + HALF : (g + 1) * HEAD]
        parts += [a * cos - b * sin, b * cos + a * sin, v[g * HEAD : (g + 1) * HEAD]]
    kv_out[...] = jnp.concatenate(parts, axis=0).T.astype(BF)


def query_body(ins, outs, scratch):
    normed, wq, angle = ins
    q_out = outs[0].ref
    rows = normed.shape[1]
    stretch = rows // 2
    q = dot(normed[...].astype(F32).T.astype(BF), wq.get()[...])
    table = angle[...].T
    cos = jnp.concatenate([table[:, :HALF]] * 2, axis=1)
    sin = jnp.concatenate([-table[:, HALF:], table[:, HALF:]], axis=1)
    zero = jnp.zeros((rows, HEAD), F32)
    for h in range(Q_HEADS):
        qh = q[:, h * HEAD : (h + 1) * HEAD]
        swapped = jnp.concatenate([qh[:, HALF:], qh[:, :HALF]], axis=1)
        qr = (qh * cos + swapped * sin) * HEAD**-0.5
        wide = jnp.concatenate([qr, zero], axis=1).astype(BF)
        g, hh = h // GROUP, h % GROUP
        for sel in range(2):
            at = (sel * GROUP + hh) * stretch
            q_out[g, at : at + stretch, :] = wide[sel * stretch : (sel + 1) * stretch]


def parts_of(n):
    low_group = min(n, 8)
    unit_group = max(d for d in range(1, 14) if (n + 1) % d == 0)
    return low_group, n // low_group, unit_group, (n + 1) // unit_group


def loop(count, body):
    if count == 1:
        body(0)
    else:
        lax.fori_loop(0, count, lambda i, c: (body(i), c)[1], 0)


def unit(u, c, n):
    is_low = u <= c
    sel = jnp.where(is_low, 0, 1)
    stretch_id = jnp.where(is_low, u, n - 1 + u - c)
    diagonal = jnp.logical_or(u == c, u == n)
    return is_low, sel, stretch_id, diagonal


def seen_mask(stretch, diagonal):
    keys = lax.broadcasted_iota(jnp.int32, (stretch, GROUP * stretch), 0)
    cols = lax.broadcasted_iota(jnp.int32, (stretch, GROUP * stretch), 1)
    queries = lax.bitwise_and(cols, stretch - 1)
    return jnp.logical_or(keys <= queries, jnp.logical_not(diagonal))


def span(index, size):
    return pl.ds(pl.multiple_of(index * size, size), size)


def forward_body(n, wt, ins, outs, scratch):
    evens = ins[: n // 2]
    odds, meta, order, q_in, tok, w_out, gain, w_gate, w_up, cot, w_down = ins[n // 2 :]
    kv_all, att_t_out, lse_out, mixed_out, even, odd = outs[:6]
    pin_outs, out_parts = outs[6 : 6 + wt], outs[6 + wt :]
    kvn, m_s, l_s, o_s, part, grads, sems = scratch
    rows = tok.ref.shape[1]
    stretch = rows // 2
    wide = GROUP * stretch
    me = meta[0]
    copies = []
    for k in range(n):
        low = order[0, 2 * lax.bitwise_xor(me, k)]
        src = evens[k // 2] if k % 2 == 0 else odds.at[k // 2]
        for half in range(2):
            to = low if half == 0 else 2 * n - 1 - low
            copies.append(
                pltpu.make_async_copy(
                    src.at[half * stretch : (half + 1) * stretch],
                    kvn.at[span(to, stretch)],
                    sems.at[2 * k + half],
                )
            )
    for copy in copies:
        copy.start()
    for copy in copies:
        copy.wait()
    keep = pltpu.make_async_copy(kvn, kv_all, sems.at[2 * n])
    keep.start()
    c = order[0, 2 * me]
    low_group, low_steps, unit_group, unit_steps = parts_of(n)
    q_ref = q_in.get()
    att_t = att_t_out.ref

    def one_head(g):
        lanes = span(g, PAIR)
        for sel in range(2):
            m_s[2 * g + sel] = jnp.full((1, wide), NEGATIVE, F32)
            l_s[2 * g + sel] = jnp.zeros((1, wide), F32)
            o_s[2 * g + sel] = jnp.zeros((PAIR, wide), F32)

        def low_step(i):
            keys = kvn[span(i, low_group * stretch), lanes]
            s = dot_nt(keys, q_ref[g, wide : 2 * wide, :])
            at = 2 * g + 1
            top = jnp.maximum(m_s[at], jnp.max(s, axis=0, keepdims=True))
            fade = jnp.exp(m_s[at] - top)
            p = jnp.exp(s - top)
            l_s[at] = l_s[at] * fade + jnp.sum(p, axis=0, keepdims=True)
            o_s[at] = o_s[at] * fade + dot_tn(keys, p.astype(BF))
            m_s[at] = top

        loop(low_steps, low_step)

        def unit_step(i):
            scores = []
            tops = [m_s[2 * g], m_s[2 * g + 1]]
            for j in range(unit_group):
                u = i * unit_group + j
                is_low, sel, st, diagonal = unit(u, c, n)
                keys = kvn[span(st, stretch), lanes]
                s = dot_nt(keys, q_ref[g, span(sel, wide), :])
                s = jnp.where(seen_mask(stretch, diagonal), s, NEGATIVE)
                peak = jnp.max(s, axis=0, keepdims=True)
                tops[0] = jnp.where(is_low, jnp.maximum(tops[0], peak), tops[0])
                tops[1] = jnp.where(is_low, tops[1], jnp.maximum(tops[1], peak))
                scores.append((s, keys, is_low, sel))
            sums = []
            for sel in range(2):
                at = 2 * g + sel
                fade = jnp.exp(m_s[at] - tops[sel])
                sums.append(l_s[at] * fade)
                o_s[at] = o_s[at] * fade
                m_s[at] = tops[sel]
            for s, keys, is_low, sel in scores:
                p = jnp.exp(s - jnp.where(is_low, tops[0], tops[1]))
                part = jnp.sum(p, axis=0, keepdims=True)
                sums[0] = sums[0] + jnp.where(is_low, part, 0.0)
                sums[1] = sums[1] + jnp.where(is_low, 0.0, part)
                o_s[2 * g + sel] += dot_tn(keys, p.astype(BF))
            for sel in range(2):
                l_s[2 * g + sel] = sums[sel]

        loop(unit_steps, unit_step)
        for sel in range(2):
            at = 2 * g + sel
            total = l_s[at]
            lse_out.ref[at] = m_s[at] + jnp.log(total)
            result = o_s[at][HEAD:, :] / total
            for hh in range(GROUP):
                att_t[span(g * GROUP + hh, HEAD), sel * stretch : (sel + 1) * stretch] = result[
                    :, hh * stretch : (hh + 1) * stretch
                ]

    loop(KV_HEADS, one_head)
    lse_out.send()
    att_t_out.send()
    att_low = att_t[...].T.astype(BF)
    mixed = tok.get()[...].astype(F32).T + dot(att_low, w_out.get()[...])
    mixed_out.ref[...] = mixed
    mixed_out.send()
    n2 = (mixed * norm_scale(mixed, -1) * row_of(gain)).astype(BF)
    gate = dot(n2, w_gate.get()[...])
    up = dot(n2, w_up.get()[...])
    sig = 1.0 / (1.0 + jnp.exp(-gate))
    silu = gate * sig
    hidden = (silu * up).astype(BF)
    grad_hidden = dot_tn(cot.get()[...], w_down.get()[...])
    gl = (grad_hidden * up * (sig * (1.0 + gate * (1.0 - sig)))).astype(BF)
    ul = (grad_hidden * silu).astype(BF)
    piece = rows // wt
    part[...] = dot_nt(gl, w_gate.get()[...]) + dot_nt(ul, w_up.get()[...])
    for k in range(wt):
        pin_outs[k][...] = part[span(lax.bitwise_xor(meta[1], k), piece), :].astype(BF)
    part[...] = dot_nt(hidden, w_down.get()[...])
    for k in range(wt):
        out_parts[k][...] = part[span(lax.bitwise_xor(meta[1], k), piece), :].astype(BF)
    width = gl.shape[1]
    grads[:, :width] = dot_tn(n2, gl)
    grads[:, width : 2 * width] = dot_tn(n2, ul)
    grads[:, 2 * width :] = dot(cot.get()[...], hidden)
    if n > 8:
        even[...] = grads[...].astype(BF)
        odd[...] = jnp.zeros(odd.shape, BF)
    else:
        size = grads.shape[0] // n
        for k in range(n):
            to = even if k % 2 == 0 else odd
            to[k // 2] = grads[span(lax.bitwise_xor(me, k), size), :].astype(BF)
    keep.wait()


def backward_body(n, wt, ins, outs, scratch):
    quarters = ins[:wt]
    (meta, order, gain, mixed, cot, w_out, att_t, lse, kv, q_in, angle) = ins[wt : wt + 11]
    (first, inner, normed, wq, wk, wv, strip_odds) = ins[wt + 11 : wt + 18]
    strips = ins[wt + 18 :]
    gm_out, dq_out, even, odd = outs[:4]
    gn_s, do_s, dl_s, dkv, dq_s, dq_t, grads, norm_s, all_s, w_s, sems = scratch
    rows = mixed.ref.shape[0]
    width = mixed.ref.shape[1]
    stretch = rows // 2
    wide = GROUP * stretch
    me = meta[0]
    c = order[0, 2 * me]
    low_group, low_steps, unit_group, unit_steps = parts_of(n)
    copies = []
    for k in range(n):
        low = order[0, 2 * lax.bitwise_xor(me, k)]
        src = strips[k // 2] if k % 2 == 0 else strip_odds.at[k // 2]
        for half in range(2):
            to = low if half == 0 else 2 * n - 1 - low
            copies.append(
                pltpu.make_async_copy(
                    src.at[:, half * stretch : (half + 1) * stretch],
                    all_s.at[:, span(to, stretch)],
                    sems.at[2 * k + half],
                )
            )
    for copy in copies:
        copy.start()

    piece = rows // wt
    for k in range(wt):
        gn_s[span(lax.bitwise_xor(meta[1], k), piece), :] = quarters[k][...].astype(F32)
    x = mixed.get()[...]
    gn = gn_s[...]
    r = norm_scale(x, -1)
    xn = x * r
    e = gn * row_of(gain)
    gm = cot.get()[...].astype(F32).T + r * (e - xn * jnp.mean(e * xn, axis=-1, keepdims=True))
    gm_out.ref[...] = gm
    gm_out.send()
    norm_s[...] = jnp.zeros(norm_s.shape, F32)
    norm_s[1:2, :width] = jnp.sum(gn * xn, axis=0, keepdims=True)
    branch = gm.astype(BF)
    ga = dot_nt(branch, w_out.get()[...]).astype(BF).astype(F32)
    prod = ga.T * att_t.get()[...]
    zero = jnp.zeros((rows, HEAD), F32)
    for h in range(Q_HEADS):
        g, hh = h // GROUP, h % GROUP
        delta = jnp.sum(prod[h * HEAD : (h + 1) * HEAD, :], axis=0, keepdims=True)
        do = jnp.concatenate([zero, ga[:, h * HEAD : (h + 1) * HEAD]], axis=1).astype(BF)
        for sel in range(2):
            at = (sel * GROUP + hh) * stretch
            half = slice(sel * stretch, (sel + 1) * stretch)
            dl_s[2 * g + sel, :, hh * stretch : (hh + 1) * stretch] = delta[:, half]
            do_s[g, at : at + stretch, :] = do[half]
    strip = grads.shape[0]
    mine = span(meta[1], strip)
    grads[:, width : 2 * width] = dot(att_t.get()[mine, :].astype(BF), branch)
    lse, kv, q_ref, angle = lse.get(), kv.get(), q_in.get(), angle.get()
    first, inner = first.get(), inner.get()
    pre = kv
    lane_ids = lax.broadcasted_iota(jnp.int32, (stretch, PAIR), 1)

    def one_head(g):
        lanes = span(g, PAIR)
        dkv[n * stretch :, :] = jnp.zeros((n * stretch, PAIR), F32)
        dq_s[...] = jnp.zeros(dq_s.shape, F32)

        def low_step(i):
            at = span(i, low_group * stretch)
            keys = kv[at, lanes]
            q = q_ref[g, wide : 2 * wide, :]
            do = do_s[g, wide : 2 * wide, :]
            p = jnp.exp(dot_nt(keys, q) - lse[2 * g + 1])
            ds = (p * (dot_nt(keys, do) - dl_s[2 * g + 1])).astype(BF)
            dkv[at, :] = dot(ds, q) + dot(p.astype(BF), do)
            dq_s[1] += dot_tn(keys, ds)

        loop(low_steps, low_step)

        def unit_step(i):
            for j in range(unit_group):
                _, sel, st, diagonal = unit(i * unit_group + j, c, n)
                at = span(st, stretch)
                keys = kv[at, lanes]
                q = q_ref[g, span(sel, wide), :]
                do = do_s[g, span(sel, wide), :]
                p = jnp.exp(dot_nt(keys, q) - lse[2 * g + sel])
                p = jnp.where(seen_mask(stretch, diagonal), p, 0.0)
                ds = (p * (dot_nt(keys, do) - dl_s[2 * g + sel])).astype(BF)
                dkv[at, :] += dot(ds, q) + dot(p.astype(BF), do)
                dq_s[sel] += dot_tn(keys, ds)

        loop(unit_steps, unit_step)

        def turn(i):
            ct, st = inner[0], inner[1]
            cs, ss = first[i, 0:1, :], first[i, 1:2, :]
            part = dkv[span(i, stretch), :]
            back = pltpu.roll(part, PAIR - HALF, 1)
            ahead = pltpu.roll(part, HALF, 1)
            swapped = jnp.where(lane_ids < HALF, back, ahead)
            result = part * (ct * cs - st * ss) + swapped * (st * cs + ct * ss)
            pre[span(i, stretch), lanes] = result.astype(BF)

        if n <= 8:
            for i in range(2 * n):
                turn(i)
        else:
            loop(2 * n, turn)
        for sel in range(2):
            half = slice(sel * stretch, (sel + 1) * stretch)
            cos, sin = angle[:HALF, half], angle[HALF:, half]
            for hh in range(GROUP):
                dq = dq_s[sel, :HEAD, hh * stretch : (hh + 1) * stretch] * HEAD**-0.5
                a, b = dq[:HALF], dq[HALF:]
                turned = jnp.concatenate([a * cos + b * sin, b * cos - a * sin], axis=0)
                dq_t[span(g * GROUP + hh, HEAD), half] = turned

    loop(KV_HEADS, one_head)
    dq = dq_t[...].T.astype(BF)
    dq_out.ref[...] = dq
    dq_out.send()
    grads[:, :width] = dot(normed.get()[...], dq)
    for copy in copies:
        copy.wait()
    grads[:, 2 * width :] = dot(all_s[...], pre[...])
    wk, wv = wk.get()[...].astype(F32), wv.get()[...].astype(F32)
    chunks = []
    for g in range(KV_HEADS):
        chunks += [wk[g * HEAD : (g + 1) * HEAD], wv[g * HEAD : (g + 1) * HEAD]]
    w_s[...] = jnp.concatenate(chunks, axis=0).T
    sums = jnp.sum(grads[:, :width] * wq.get()[mine, :].astype(F32), axis=1, keepdims=True)
    sums = sums + jnp.sum(grads[:, 2 * width :] * w_s[mine, :], axis=1, keepdims=True)
    norm_s[0:1, :strip] = jnp.broadcast_to(sums, (strip, 128)).T[0:1, :]
    quarter = meta[1] * piece
    upper = quarter >= stretch
    inside = jnp.where(upper, quarter - stretch, quarter)

    def rows_for(who):
        low = order[0, 2 * who]
        st = jnp.where(upper, 2 * n - 1 - low, low)
        return pre[pl.ds(pl.multiple_of(st * stretch + inside, piece), piece), :]

    if n > 8:
        even[...] = grads[...].astype(BF)
        odd[...] = norm_s[...].astype(BF)
        for k in range(n):
            outs[4][k] = rows_for(k)
        return
    for k in range(n):
        who = lax.bitwise_xor(me, k)
        to = even if k % 2 == 0 else odd
        to[k // 2, :piece, :] = rows_for(who)
        block = grads[block_rows(strip, who), block_lanes(who)]
        cut = norm_s[:, span(who, 128)]
        tail = jnp.concatenate([cut, jnp.zeros((8, block.shape[1] - 128), F32)], axis=1)
        to[k // 2, piece:, :] = jnp.concatenate([block, tail], axis=0).astype(BF)


def block_rows(strip, who):
    size = strip // 2
    return pl.ds(pl.multiple_of(lax.shift_right_logical(who, 2) * size, size), size)


def block_lanes(who):
    return span(lax.bitwise_and(who, 3), KV_HEADS * PAIR)


def finish_body(wt, count, ins, outs, scratch):
    terms = ins[:count]
    out_terms = ins[count : count + wt]
    meta, gain, tok, mixed, gm, dq, wq, wk, wv = ins[count + wt :]
    (both_out,) = outs
    (x_s,) = scratch
    piece = both_out.shape[0]
    width = gain.shape[0]
    total = terms[0][:piece, :].astype(F32)
    for term in terms[1:]:
        total = total + term[:piece, :].astype(F32)
    mine = span(meta[1], piece)
    out = out_terms[0][...].astype(F32)
    for term in out_terms[1:]:
        out = out + term[...].astype(F32)
    both_out[:, 640:] = (mixed.get()[mine, :] + out).astype(BF)
    x_s[...] = tok.get()[...].astype(F32).T
    x = x_s[mine, :]
    dk, dv = [], []
    for g in range(KV_HEADS):
        dk.append(total[:, g * PAIR : g * PAIR + HEAD])
        dv.append(total[:, g * PAIR + HEAD : (g + 1) * PAIR])
    dk = jnp.concatenate(dk, axis=1).astype(BF)
    dv = jnp.concatenate(dv, axis=1).astype(BF)
    gn = dot_nt(dq.get()[mine, :], wq.get()[...])
    gn = gn + dot(dk, wk.get()[...]) + dot(dv, wv.get()[...])
    r = norm_scale(x, -1)
    xn = x * r
    e = gn * row_of(gain)
    result = gm.get()[mine, :] + r * (e - xn * jnp.mean(e * xn, axis=-1, keepdims=True))
    both_out[:, :width] = result.astype(BF)
    both_out[:, width:640] = jnp.zeros((piece, 640 - width), BF)


def mlp_join_body(n, wt, ins, outs, scratch):
    meta = ins[0]
    quarters = ins[1 : 1 + wt]
    blocks = ins[1 + wt :]
    grads, rows_s, out_s = scratch
    piece, width = quarters[0].shape[0], rows_s.shape[1]
    for k in range(wt):
        at = span(lax.bitwise_xor(meta[1], k), piece)
        rows_s[at, :] = quarters[k][:, :width].astype(F32)
        out_s[at, :] = quarters[k][:, 640:].astype(F32)
    outs[0][...] = rows_s[...].T
    outs[1][...] = out_s[...].T.astype(BF)
    if n > 8:
        grads[...] = blocks[0][...].astype(F32)
    else:
        size = grads.shape[0] // n
        for k in range(n):
            block = blocks[k // 2][...] if k % 2 == 0 else blocks[-1][k // 2]
            grads[span(lax.bitwise_xor(meta[0], k), size), :] = block.astype(F32)
    width = outs[2].shape[1]
    for i in range(3):
        outs[2 + i][...] = grads[:, i * width : (i + 1) * width]


def join_body(n, wt, ins, outs, scratch):
    meta, gain = ins[:2]
    blocks = ins[2:]
    gq, go, gk, gv, norm_attn, norm_mlp = outs
    grads, norm_s = scratch
    width = gq.shape[0]
    strip = width // wt
    norm_s[...] = jnp.zeros(norm_s.shape, F32)
    if n > 8:
        grads[...] = blocks[0][...].astype(F32)
        norm_s[...] = blocks[1][...].astype(F32)
    else:
        size = strip // 2
        for k in range(n):
            who = lax.bitwise_xor(meta[0], k)
            for kz in range(wt):
                lane = lax.bitwise_xor(meta[1], kz)
                block = blocks[k // 2][kz] if k % 2 == 0 else blocks[-1][k // 2, kz]
                block = block.astype(F32)
                at = lane * strip + lax.shift_right_logical(who, 2) * size
                grads[pl.ds(pl.multiple_of(at, size), size), block_lanes(who)] = block[:size]
                norm_s[lane, :, span(who, 128)] = block[size:, :128]
    gq[...] = grads[:, :width]
    go[...] = grads[:, width : 2 * width]
    both = grads[:, 2 * width :].T
    for g in range(KV_HEADS):
        gk[g * HEAD : (g + 1) * HEAD, :] = both[g * PAIR : g * PAIR + HEAD]
        gv[g * HEAD : (g + 1) * HEAD, :] = both[g * PAIR + HEAD : (g + 1) * PAIR]
    attn = jnp.concatenate([norm_s[lane, 0:1, :strip] for lane in range(wt)], axis=1)
    norm_attn[...] = (attn / row_of(gain)).reshape(width)
    norm_mlp[...] = norm_s[0, 1:2, :width].reshape(width)


def hop(x, axis, size, k):
    return lax.ppermute(x, axis, [(i, i ^ k) for i in range(size)])


def gather_blocks(x, axis, size):
    evens = [x] + [hop(x, axis, size, k) for k in range(2, size, 2)]
    odds = hop(jnp.stack(evens), axis, size, 1)
    return evens, odds


def pair_terms(even, odd, axis, size):
    got = hop(odd, axis, size, 1).astype(F32)
    pairs = [even[i].astype(F32) + got[i] for i in range(size // 2)]
    return pairs[:1] + [pair.astype(BF) for pair in pairs[1:]]


def scatter_terms(pairs, axis, size):
    return pairs[:1] + [hop(pairs[i], axis, size, 2 * i) for i in range(1, size // 2)]


def summed(terms):
    total = terms[0].astype(F32)
    for term in terms[1:]:
        total = total + term.astype(F32)
    return total


def after(dep, *arrays):
    held = lax.optimization_barrier((dep,) + arrays)
    return held[1:] if len(arrays) > 1 else held[1]


def local(
    n,
    wt,
    tokens,
    w_query,
    w_key,
    w_value,
    w_out,
    norm_attn,
    norm_mlp,
    w_gate,
    w_up,
    w_down,
    stretch_order,
    cotangent,
):
    rows, width = tokens.shape
    stretch = rows // 2
    wide = GROUP * stretch
    kv_width = KV_HEADS * PAIR
    hidden_width = w_gate.shape[1]
    piece = rows // wt
    size = width // n
    strip = width // wt
    small = n <= 8
    turned, first, inner = (jnp.asarray(t) for t in angle_tables(n, stretch))
    tok, cot, wk, wv, w_down = tokens.T, cotangent.T, w_key.T, w_value.T, w_down.T

    normed, kv, angle, normed_q = call(
        key_body,
        [None, stretch_order, norm_attn, tok, wk, wv, turned],
        "msvvccc",
        [shape((width, rows), BF), shape((rows, kv_width), BF), shape((HEAD, rows), F32)]
        + [shape((strip, rows), BF)],
        "vvvv",
        scratch=[pltpu.VMEM((width, rows), F32)],
    )
    (q,) = call(
        query_body,
        [normed, w_query, angle],
        "vcv",
        [shape((KV_HEADS, 2 * wide, PAIR), BF)],
        "c",
    )
    evens = [kv] + [hop(kv, "ctx", n, k) for k in range(2, n, 2)]
    odds = hop(jnp.stack(after(q, *evens)), "ctx", n, 1)

    mlp_columns = 3 * hidden_width
    if small:
        block_shapes = [shape((n // 2, size, mlp_columns), BF)] * 2
    else:
        block_shapes = [shape((width, mlp_columns), BF), shape((8, 128), BF)]
    kv_all, att_t, lse, mixed, even, odd, *pieces = call(
        functools.partial(forward_body, n, wt),
        [*evens, odds, None, stretch_order, q, tok, w_out, norm_mlp, w_gate, w_up, cot, w_down],
        "h" * (n // 2 + 1) + "msccc" + "v" + "cccc",
        [
            shape((n * rows, kv_width), BF),
            shape((width, rows), F32),
            shape((2 * KV_HEADS, 1, wide), F32),
            shape((rows, width), F32),
        ]
        + block_shapes
        + [shape((piece, width), BF)] * (2 * wt),
        "hccc" + "vv" + "v" * (2 * wt),
        scratch=[
            pltpu.VMEM((n * rows, kv_width), BF),
            pltpu.VMEM((2 * KV_HEADS, 1, wide), F32),
            pltpu.VMEM((2 * KV_HEADS, 1, wide), F32),
            pltpu.VMEM((2 * KV_HEADS, PAIR, wide), F32),
            pltpu.VMEM((rows, width), F32),
            pltpu.VMEM((width, mlp_columns), F32),
            pltpu.SemaphoreType.DMA((2 * n + 1,)),
        ],
    )
    part_in, out_parts = pieces[:wt], pieces[wt:]

    terms = [part_in[0]] + [hop(part_in[k], "wt", wt, k) for k in range(1, wt)]
    quarter = summed(terms).astype(BF)
    quarters = [quarter] + [hop(quarter, "wt", wt, k) for k in range(1, wt)]

    strips, strip_odds = gather_blocks(after(part_in[0], normed_q), "ctx", n)
    if small:
        mlp_own = summed(scatter_terms(pair_terms(even, odd, "ctx", n), "ctx", n)).astype(BF)
        quarters = after(mlp_own, *quarters)
        mlp_evens, mlp_odds = gather_blocks(mlp_own, "ctx", n)
        mlp_blocks = [*mlp_evens, mlp_odds]
    else:
        mlp_blocks = [lax.psum(even, "ctx")]

    columns = 2 * width + kv_width
    if small:
        out_blocks = [shape((n // 2, piece + strip // 2 + 8, kv_width), BF)] * 2
    else:
        out_blocks = [
            shape((strip, columns), BF),
            shape((8, 128 * n), BF),
            shape((n, piece, kv_width), BF),
        ]
    gm, dq, *message = call(
        functools.partial(backward_body, n, wt),
        [*quarters, None, stretch_order, norm_mlp, mixed, cot, w_out, att_t, lse, kv_all, q, angle]
        + [first, inner, normed_q, w_query, wk, wv, strip_odds, *strips],
        "v" * wt + "msv" + "c" * 8 + "c" * 6 + "h" * (1 + n // 2),
        [shape((rows, width), F32), shape((rows, width), BF)] + out_blocks,
        "cc" + "v" * len(out_blocks),
        scratch=[
            pltpu.VMEM((rows, width), F32),
            pltpu.VMEM((KV_HEADS, 2 * wide, PAIR), BF),
            pltpu.VMEM((2 * KV_HEADS, 1, wide), F32),
            pltpu.VMEM((n * rows, PAIR), F32),
            pltpu.VMEM((2, PAIR, wide), F32),
            pltpu.VMEM((width, rows), F32),
            pltpu.VMEM((strip, columns), F32),
            pltpu.VMEM((8, max(128 * n, 640)), F32),
            pltpu.VMEM((strip, n * rows), BF),
            pltpu.VMEM((width, kv_width), F32),
            pltpu.SemaphoreType.DMA((2 * n,)),
        ],
    )
    if small:
        message[1] = after(mlp_evens[-1], message[1])
        parts = scatter_terms(pair_terms(message[0], message[1], "ctx", n), "ctx", n)
        own = summed([part[piece:] for part in parts]).astype(BF)
        owns = [own] + [hop(own, "wt", wt, k) for k in range(1, wt)]
    else:
        parts = [lax.psum_scatter(message[2].astype(F32), "ctx", scatter_dimension=0)]
        last_blocks = list(lax.psum((message[0], message[1]), "ctx"))
        last_blocks = [lax.all_gather(b, "wt", axis=0, tiled=i == 0) for i, b in enumerate(last_blocks)]
    held = after(dq, *out_parts)
    out_parts = [held[0]] + [hop(held[k], "wt", wt, k) for k in range(1, wt)]
    (both,) = call(
        functools.partial(finish_body, wt, len(parts)),
        [*parts, *out_parts, None, norm_attn, tok, mixed, gm, dq, w_query, wk, wv],
        "v" * (len(parts) + wt) + "mv" + "c" * 7,
        [shape((piece, 640 + width), BF)],
        "v",
        scratch=[pltpu.VMEM((rows, width), F32)],
        vmem=16,
    )
    if small:
        own = jnp.stack(after(both, *owns))
        last_evens = [own] + [hop(own, "ctx", n, k) for k in range(2, n, 2)]
    boths = [both] + [hop(both, "wt", wt, k) for k in range(1, wt)]

    grad_tokens, output, grad_gate, grad_up, grad_down = call(
        functools.partial(mlp_join_body, n, wt),
        [None, *boths, *mlp_blocks],
        "m" + "v" * (wt + len(mlp_blocks)),
        [shape((width, rows), F32), shape((width, rows), BF)]
        + [shape((width, hidden_width), F32)] * 3,
        "vvvvv",
        scratch=[
            pltpu.VMEM((width, mlp_columns), F32),
            pltpu.VMEM((rows, width), F32),
            pltpu.VMEM((rows, width), F32),
        ],
        vmem=24,
    )
    if small:
        last_blocks = [*last_evens, hop(after(grad_gate, jnp.stack(last_evens)), "ctx", n, 1)]
    grad_query, grad_out, grad_key, grad_value, grad_norm_attn, grad_norm_mlp = call(
        functools.partial(join_body, n, wt),
        [None, norm_attn, *last_blocks],
        "mv" + "v" * len(last_blocks),
        [shape((width, width), F32)] * 2
        + [shape((kv_width // 2, width), F32)] * 2
        + [shape((width,), F32)] * 2,
        "vvvvvv",
        scratch=[
            pltpu.VMEM((width, columns), F32),
            pltpu.VMEM((wt, 8, max(128 * n, 640)), F32),
        ],
        vmem=24,
    )
    return (
        output.T,
        grad_tokens.T,
        grad_query,
        grad_key.T,
        grad_value.T,
        grad_out,
        grad_norm_attn,
        grad_norm_mlp,
        grad_gate,
        grad_up,
        grad_down.T,
    )


def solution(mesh):
    return jax.shard_map(
        functools.partial(local, mesh.shape["ctx"], mesh.shape["wt"]),
        mesh=mesh,
        in_specs=(
            P("ctx", None),
            P(),
            P(),
            P(),
            P(),
            P(),
            P(),
            P(None, "wt"),
            P(None, "wt"),
            P("wt", None),
            P(),
            P("ctx", None),
        ),
        out_specs=(
            P("ctx", None),
            P("ctx", None),
            P(),
            P(),
            P(),
            P(),
            P(),
            P(),
            P(None, "wt"),
            P(None, "wt"),
            P("wt", None),
        ),
        check_vma=False,
    )
```

time: 182 us -> 137 us (0.75)
  local copies, waits for them, and re-layouts: 33.9 us -> 1.7 us
  between operations: 14.7 us -> 1.11 us
  starting transfers between devices: 39.9 us -> 52.4 us
  other arithmetic: 12 us -> 0.98 us
  Pallas kernels: 39 us -> 48.7 us
  waiting for transfers between devices: 41.5 us -> 32.3 us
    unnamed x148 -> x64, local copies, waits for them, and re-layouts: 30.2 us -> 1.7 us
    ppermute x38 -> x39, starting transfers between devices: 39.9 us -> 52.4 us  [hop(): return lax.ppermute(x, axis, [(i, i ^ k) for i in range(size)])]
    pallas_call x10 -> x7, Pallas kernels: 39 us -> 48.7 us  [call(): pl.pallas_call(kernel, out_shape=tuple(outs), in_specs=[SPEC[k] for _, k...]
    ppermute x38 -> x39, waiting for transfers between devices: 41.4 us -> 32.3 us  [hop(): return lax.ppermute(x, axis, [(i, i ^ k) for i in range(size)])]
    convert_element_type x13 -> x6, other arithmetic: 4.99 us -> 0.46 us  [the longest x2 0.17 us: pair_terms(): return pairs[:1] + [pair.astype(BF) for pair in pairs[1:]]]
    another operation x4 -> x2, other arithmetic: 3.62 us -> 0.14 us  [gather_blocks(): odds = hop(jnp.stack(evens), axis, size, 1)]
    transpose x2 -> x0, local copies, waits for them, and re-layouts: 2.33 us -> none  [local(): cos_t, sin_t = (cos.T, sin.T)]
  transfers between devices with their start and end apart: 39 -> 39, of which waited for: 18 -> 17; matrix products, arithmetic and copies ran while one was open for 12% -> 1% of each run, Pallas kernels for 12% -> 20%
where the time goes in v2:
time: 137 us
  starting transfers between devices  52.4 us (38%)
  Pallas kernels  48.7 us (36%)
  waiting for transfers between devices  32.3 us (24%)
  local copies, waits for them, and re-layouts  1.7 us (1%)
    ppermute x39, starting transfers between devices, hop(): return lax.ppermute(x, axis, [(i, i ^ k) for i in range(size)])  52.4 us
    pallas_call x7, Pallas kernels, call(): pl.pallas_call(kernel, out_shape=tuple(outs), in_specs=[SPEC[k] for _, k...  48.7 us
    ppermute x39, waiting for transfers between devices, hop(): return lax.ppermute(x, axis, [(i, i ^ k) for i in range(size)])  32.3 us
  transfers between devices with their start and end apart: 39, of which 17 were waited for; matrix products, arithmetic and copies ran while one was open for 1% of the time, Pallas kernels for 20%

profile of v2, /device:TPU:0, one launch (start us, length us, event | category | flops | bytes accessed | tf_op | source)
XLA Modules:
  0.0 137.1 jit_solution(9572863267989745876)
XLA Ops:
  0.6 3.7 %shard_map.230 = (bf16[576,256]{1,0:T(8,128)(2,1)}, bf16[256,384]{1,0:T(8,128)(2,1)}, f32[64,256]{1,0:T(8,128)}, bf16[144,256]{1,0:T(8,128)(2,1)}) custom-call(s32[1,16]{1,0:T(1,128)} %refs_4_.1, bf16[576]{0:T(1024)(128)(2,1)} %refs_0_.3, bf16[576,256]{1,0:T(8,128)(2,1)} %bitcast.64, bf16[192,576]{1,0:T(8,128)(2,1)} %bitcast.67, bf16[192,576]{1,0:T(8,128)(2,1)} %bitcast.70, ...), custom_call_target="tpu_custom_call" | custom-call | bytes 4194304 | tf_op jit(solution)/shard_map/pallas_call | solution.py:108
  4.3 4.0 %collective-permute-start.2 = (bf16[256,384]{1,0:T(8,128)(2,1)}, bf16[256,384]{1,0:T(8,128)(2,1)S(1)}, u32[]{:S(2)}, u32[]{:S(2)}) collective-permute-start(bf16[256,384]{1,0:T(8,128)(2,1)} %get-tuple-element.66.refs_0_), channel_id=1, source_target_pairs={{0,24},{4,28},{8,16},{12,20},{16,8},{20,12},{24,0},{28,4},{1,25},{... | collective-permute-start | bytes 589832 | tf_op jit(solution)/shard_map/ppermute | solution.py:617
  8.9 4.0 %shard_map.231.refs_6_.refs_12_ = bf16[3,768,128]{2,1,0:T(8,128)(2,1)} custom-call(bf16[576,256]{1,0:T(8,128)(2,1)} %get-tuple-element.64.refs_0_, bf16[576,576]{1,0:T(8,128)(2,1)} %refs_13_.1, f32[64,256]{1,0:T(8,128)} %get-tuple-element.65.refs_2_.refs_13_), custom_call_target="tpu_custom_call" | custom-call | bytes 4194304 | tf_op jit(solution)/shard_map/pallas_call | solution.py:108
  14.3 3.3 %collective-permute-done.1.refs_2_ = bf16[256,384]{1,0:T(8,128)(2,1)S(1)} collective-permute-done((bf16[256,384]{1,0:T(8,128)(2,1)}, bf16[256,384]{1,0:T(8,128)(2,1)S(1)}, u32[]{:S(2)}, u32[]{:S(2)}) %collective-permute-start.1) | collective-permute-done | bytes 196640 | tf_op jit(solution)/shard_map/ppermute | solution.py:617
  18.1 2.3 %collective-permute-done.3.refs_4_ = bf16[4,256,384]{2,1,0:T(8,128)(2,1)S(1)} collective-permute-done((bf16[4,256,384]{2,1,0:T(8,128)(2,1)S(1)}, bf16[4,256,384]{2,1,0:T(8,128)(2,1)S(1)}, u32[]{:S(2)}, u32[]{:S(2)}) %collective-permute-start.3) | collective-permute-done | bytes 786464 | tf_op jit(solution)/shard_map/ppermute | solution.py:617
  21.3 14.2 %shard_map.232 = (bf16[2048,384]{1,0:T(8,128)(2,1)}, f32[576,256]{1,0:T(8,128)}, f32[6,1,384]{2,1,0:T(1,128)}, f32[256,576]{1,0:T(8,128)}, bf16[4,72,1152]{2,1,0...) custom-call(bf16[256,384]{1,0:T(8,128)(2,1)} %get-tuple-element.66.r, ...), custom_call_target="tpu_custom_call" | custom-call | bytes 4194304 | tf_op jit(solution)/shard_map/pallas_call | solution.py:108
  35.7 1.6 %collective-permute-start.16 = (bf16[144,256]{1,0:T(8,128)(2,1)S(1)}, bf16[144,256]{1,0:T(8,128)(2,1)S(1)}, u32[]{:S(2)}, u32[]{:S(2)}) collective-permute-start(bf16[144,256]{1,0:T(8,128)(2,1)S(1)} %copy-done.15), channel_id=1, source_target_pairs={{0,24},{4,28},{8,16},{12,20},{16,8},{20,12},{24,0},{28,4},{1,25},{... | collective-permute-start | bytes 221192 | tf_op jit(solution)/shard_map/ppermute | solution.py:617
  37.3 1.4 %collective-permute-start.15 = (bf16[144,256]{1,0:T(8,128)(2,1)S(1)}, bf16[144,256]{1,0:T(8,128)(2,1)S(1)}, u32[]{:S(2)}, u32[]{:S(2)}) collective-permute-start(bf16[144,256]{1,0:T(8,128)(2,1)S(1)} %copy-done.15), channel_id=1, source_target_pairs={{0,16},{4,20},{8,24},{12,28},{16,0},{20,4},{24,8},{28,12},{1,17},{... | collective-permute-start | bytes 221192 | tf_op jit(solution)/shard_map/ppermute | solution.py:617
  39.5 1.6 %collective-permute-start.5 = (bf16[72,1152]{1,0:T(8,128)(2,1)S(1)}, bf16[72,1152]{1,0:T(8,128)(2,1)S(1)}, u32[]{:S(2)}, u32[]{:S(2)}) collective-permute-start(bf16[72,1152]{1,0:T(8,128)(2,1)S(1)} %get-tuple-element.115), channel_id=1, source_target_pairs={{0,8},{4,12},{8,0},{12,4},{16,24},{20,28},{24,16},{28,20},{1,9},{5... | collective-permute-start | bytes 497672 | tf_op jit(solution)/shard_map/ppermute | solution.py:617
  43.0 1.6 %collective-permute-start.8 = (bf16[64,576]{1,0:T(8,128)(2,1)S(1)}, bf16[64,576]{1,0:T(8,128)(2,1)S(1)}, u32[]{:S(2)}, u32[]{:S(2)}) collective-permute-start(bf16[64,576]{1,0:T(8,128)(2,1)S(1)} %copy-done.31), channel_id=1, source_target_pairs={{0,1},{1,0},{2,3},{3,2},{4,5},{5,4},{6,7},{7,6},{8,9},{9,8},{10,11... | collective-permute-start | bytes 221192 | tf_op jit(solution)/shard_map/ppermute | solution.py:617
  44.7 2.7 %collective-permute-start.9 = (bf16[64,576]{1,0:T(8,128)(2,1)S(1)}, bf16[64,576]{1,0:T(8,128)(2,1)S(1)}, u32[]{:S(2)}, u32[]{:S(2)}) collective-permute-start(bf16[64,576]{1,0:T(8,128)(2,1)S(1)} %copy-done.30), channel_id=1, source_target_pairs={{0,2},{1,3},{2,0},{3,1},{4,6},{5,7},{6,4},{7,5},{8,10},{9,11},{10,... | collective-permute-start | bytes 221192 | tf_op jit(solution)/shard_map/ppermute | solution.py:617
  47.4 3.6 %collective-permute-start.10 = (bf16[64,576]{1,0:T(8,128)(2,1)S(1)}, bf16[64,576]{1,0:T(8,128)(2,1)S(1)}, u32[]{:S(2)}, u32[]{:S(2)}) collective-permute-start(bf16[64,576]{1,0:T(8,128)(2,1)S(1)} %copy-done.29), channel_id=1, source_target_pairs={{0,3},{1,2},{2,1},{3,0},{4,7},{5,6},{6,5},{7,4},{8,11},{9,10},{10,... | collective-permute-start | bytes 221192 | tf_op jit(solution)/shard_map/ppermute | solution.py:617
  51.3 1.5 %collective-permute-start.18 = (bf16[72,1152]{1,0:T(8,128)(2,1)S(1)}, bf16[72,1152]{1,0:T(8,128)(2,1)S(1)}, u32[]{:S(2)}, u32[]{:S(2)}) collective-permute-start(bf16[72,1152]{1,0:T(8,128)(2,1)S(1)} %fusion.7.refs_4_), channel_id=1, source_target_pairs={{0,24},{4,28},{8,16},{12,20},{16,8},{20,12},{24,0},{28,4},{1,25},{... | collective-permute-start | bytes 497672 | tf_op jit(solution)/shard_map/ppermute | solution.py:617
  53.9 3.5 %collective-permute-start.13 = (bf16[64,576]{1,0:T(8,128)(2,1)S(1)}, bf16[64,576]{1,0:T(8,128)(2,1)S(1)}, u32[]{:S(2)}, u32[]{:S(2)}) collective-permute-start(bf16[64,576]{1,0:T(8,128)(2,1)S(1)} %add_convert_fusion.refs_0_), channel_id=1, source_target_pairs={{0,3},{1,2},{2,1},{3,0},{4,7},{5,6},{6,5},{7,4},{8,11},{9,10},{10,... | collective-permute-start | bytes 221192 | tf_op jit(solution)/shard_map/ppermute | solution.py:617
  58.3 1.9 %collective-permute-done.13.refs_3_ = bf16[64,576]{1,0:T(8,128)(2,1)S(1)} collective-permute-done((bf16[64,576]{1,0:T(8,128)(2,1)S(1)}, bf16[64,576]{1,0:T(8,128)(2,1)S(1)}, u32[]{:S(2)}, u32[]{:S(2)}) %collective-permute-start.13) | collective-permute-done | bytes 73760 | tf_op jit(solution)/shard_map/ppermute | solution.py:617
  60.2 3.3 %collective-permute-done.12.refs_2_ = bf16[64,576]{1,0:T(8,128)(2,1)S(1)} collective-permute-done((bf16[64,576]{1,0:T(8,128)(2,1)S(1)}, bf16[64,576]{1,0:T(8,128)(2,1)S(1)}, u32[]{:S(2)}, u32[]{:S(2)}) %collective-permute-start.12) | collective-permute-done | bytes 73760 | tf_op jit(solution)/shard_map/ppermute | solution.py:617
  64.3 19.2 %shard_map.233 = (f32[256,576]{1,0:T(8,128)}, bf16[256,576]{1,0:T(8,128)(2,1)}, bf16[4,144,384]{2,1,0:T(8,128)(2,1)}, bf16[4,144,384]{2,1,0:T(8,128)(2,1)}) custom-call(bf16[64,576]{1,0:T(8,128)(2,1)} %copy-done.17, bf16[64,576]{1,0:T(8,128)(2,1)} %copy-done.25, bf16[64,576]{1,0:T(8,128)(2,1)} %copy-done.24, bf16[64,576]{1,0:T(8,128)(2,1)} %copy-done.23, ...), custom_call_target="tpu_custom_call" | custom-call | bytes 4194304 | tf_op jit(solution)/shard_map/pallas_call | solution.py:108
  85.8 4.5 %collective-permute-done.30.refs_6_ = bf16[72,1152]{1,0:T(8,128)(2,1)S(1)} collective-permute-done((bf16[72,1152]{1,0:T(8,128)(2,1)S(1)}, bf16[72,1152]{1,0:T(8,128)(2,1)S(1)}, u32[]{:S(2)}, u32[]{:S(2)}) %collective-permute-start.30) | collective-permute-done | bytes 165920 | tf_op jit(solution)/shard_map/ppermute | solution.py:617
  91.5 1.5 %collective-permute-start.22 = (bf16[144,384]{1,0:T(8,128)(2,1)S(1)}, bf16[144,384]{1,0:T(8,128)(2,1)S(1)}, u32[]{:S(2)}, u32[]{:S(2)}) collective-permute-start(bf16[144,384]{1,0:T(8,128)(2,1)S(1)} %get-tuple-element.118), channel_id=1, source_target_pairs={{0,24},{4,28},{8,16},{12,20},{16,8},{20,12},{24,0},{28,4},{1,25},{... | collective-permute-start | bytes 331784 | tf_op jit(solution)/shard_map/ppermute | solution.py:617
  95.5 2.9 %collective-permute-done.22.refs_3_ = bf16[144,384]{1,0:T(8,128)(2,1)S(1)} collective-permute-done((bf16[144,384]{1,0:T(8,128)(2,1)S(1)}, bf16[144,384]{1,0:T(8,128)(2,1)S(1)}, u32[]{:S(2)}, u32[]{:S(2)}) %collective-permute-start.22) | collective-permute-done | bytes 110624 | tf_op jit(solution)/shard_map/ppermute | solution.py:617
  100.3 2.5 %collective-permute-start.25 = (bf16[64,576]{1,0:T(8,128)(2,1)S(1)}, bf16[64,576]{1,0:T(8,128)(2,1)S(1)}, u32[]{:S(2)}, u32[]{:S(2)}) collective-permute-start(bf16[64,576]{1,0:T(8,128)(2,1)S(1)} %copy-done.26), channel_id=1, source_target_pairs={{0,3},{1,2},{2,1},{3,0},{4,7},{5,6},{6,5},{7,4},{8,11},{9,10},{10,... | collective-permute-start | bytes 221192 | tf_op jit(solution)/shard_map/ppermute | solution.py:617
  104.2 2.9 %collective-permute-done.24.refs_6_ = bf16[64,576]{1,0:T(8,128)(2,1)S(1)} collective-permute-done((bf16[64,576]{1,0:T(8,128)(2,1)S(1)}, bf16[64,576]{1,0:T(8,128)(2,1)S(1)}, u32[]{:S(2)}, u32[]{:S(2)}) %collective-permute-start.24) | collective-permute-done | bytes 73760 | tf_op jit(solution)/shard_map/ppermute | solution.py:617
  107.3 2.6 %shard_map.234.refs_0_ = bf16[64,1216]{1,0:T(8,128)(2,1)S(1)} custom-call(f32[144,384]{1,0:T(8,128)S(1)} %bitcast.74, bf16[144,384]{1,0:T(8,128)(2,1)S(1)} %collective-permute-done.20.refs_1_, bf16[144,384]{1,0:T(8,128)(2,1)S(1)} %collective-permute-done.21.refs_2_, bf16[144,384]{1,0:T(8,128)(2,1)S(1)} %collective-permute-done.22.refs_3_, ...), custom_call_target="tpu_custom_call" | custom-call | bytes 4194304 | tf_op jit(solution)/shard_map/pallas_call | solution.py:108
  110.0 4.2 %collective-permute-start.28 = (bf16[64,1216]{1,0:T(8,128)(2,1)S(1)}, bf16[64,1216]{1,0:T(8,128)(2,1)S(1)}, u32[]{:S(2)}, u32[]{:S(2)}) collective-permute-start(bf16[64,1216]{1,0:T(8,128)(2,1)S(1)} %shard_map.234.refs_0_), channel_id=1, source_target_pairs={{0,3},{1,2},{2,1},{3,0},{4,7},{5,6},{6,5},{7,4},{8,11},{9,10},{10,... | collective-permute-start | bytes 466952 | tf_op jit(solution)/shard_map/ppermute | solution.py:617
  114.3 1.8 %collective-permute-start.37 = (bf16[4,80,384]{2,1,0:T(8,128)(2,1)S(1)}, bf16[4,80,384]{2,1,0:T(8,128)(2,1)S(1)}, u32[]{:S(2)}, u32[]{:S(2)}) collective-permute-start(bf16[4,80,384]{2,1,0:T(8,128)(2,1)S(1)} %get-tuple-element.123.refs_1_), channel_id=1, source_target_pairs={{0,24},{4,28},{8,16},{12,20},{16,8},{20,12},{24,0},{28,4},{1,25},{... | collective-permute-start | bytes 737288 | tf_op jit(solution)/shard_map/ppermute | solution.py:617
  117.8 2.1 %collective-permute-start.27 = (bf16[64,1216]{1,0:T(8,128)(2,1)S(1)}, bf16[64,1216]{1,0:T(8,128)(2,1)S(1)}, u32[]{:S(2)}, u32[]{:S(2)}) collective-permute-start(bf16[64,1216]{1,0:T(8,128)(2,1)S(1)} %shard_map.234.refs_0_), channel_id=1, source_target_pairs={{0,2},{1,3},{2,0},{3,1},{4,6},{5,7},{6,4},{7,5},{8,10},{9,11},{10,... | collective-permute-start | bytes 466952 | tf_op jit(solution)/shard_map/ppermute | solution.py:617
  120.0 5.4 %collective-permute-start.26 = (bf16[64,1216]{1,0:T(8,128)(2,1)S(1)}, bf16[64,1216]{1,0:T(8,128)(2,1)S(1)}, u32[]{:S(2)}, u32[]{:S(2)}) collective-permute-start(bf16[64,1216]{1,0:T(8,128)(2,1)S(1)} %shard_map.234.refs_0_), channel_id=1, source_target_pairs={{0,1},{1,0},{2,3},{3,2},{4,5},{5,4},{6,7},{7,6},{8,9},{9,8},{10,11... | collective-permute-start | bytes 466952 | tf_op jit(solution)/shard_map/ppermute | solution.py:617
  125.3 2.4 %collective-permute-done.27.refs_2_ = bf16[64,1216]{1,0:T(8,128)(2,1)S(1)} collective-permute-done((bf16[64,1216]{1,0:T(8,128)(2,1)S(1)}, bf16[64,1216]{1,0:T(8,128)(2,1)S(1)}, u32[]{:S(2)}, u32[]{:S(2)}) %collective-permute-start.27) | collective-permute-done | bytes 155680 | tf_op jit(solution)/shard_map/ppermute | solution.py:617
  127.7 1.7 %collective-permute-done.26.refs_1_ = bf16[64,1216]{1,0:T(8,128)(2,1)S(1)} collective-permute-done((bf16[64,1216]{1,0:T(8,128)(2,1)S(1)}, bf16[64,1216]{1,0:T(8,128)(2,1)S(1)}, u32[]{:S(2)}, u32[]{:S(2)}) %collective-permute-start.26) | collective-permute-done | bytes 155680 | tf_op jit(solution)/shard_map/ppermute | solution.py:617
  129.4 2.1 %shard_map.235 = (f32[576,256]{1,0:T(8,128)}, bf16[576,256]{1,0:T(8,128)(2,1)}, f32[576,384]{1,0:T(8,128)}, f32[576,384]{1,0:T(8,128)}, f32[576,384]{1,0:T(8,128)}) custom-call(bf16[64,1216]{1,0:T(8,128)(2,1)S(1)} %shard_map.234.refs_0_, bf16[64,1216]{1,0:T(8,128)(2,1)S(1)} %collective-permute-done.26.refs_1_, ...), custom_call_target="tpu_custom_call" | custom-call | bytes 4194304 | tf_op jit(solution)/shard_map/pallas_call | solution.py:108
  131.7 2.6 %collective-permute-done.38.refs_5_ = bf16[4,4,80,384]{3,2,1,0:T(8,128)(2,1)S(1)} collective-permute-done((bf16[4,4,80,384]{3,2,1,0:T(8,128)(2,1)S(1)}, bf16[4,4,80,384]{3,2,1,0:T(8,128)(2,1)S(1)}, u32[]{:S(2)}, u32[]{:S(2)}) %collective-permute-start.38) | collective-permute-done | bytes 983072 | tf_op jit(solution)/shard_map/ppermute | solution.py:617
  134.3 2.9 %shard_map.236 = (f32[576,576]{1,0:T(8,128)}, f32[576,576]{1,0:T(8,128)}, f32[192,576]{1,0:T(8,128)}, f32[192,576]{1,0:T(8,128)}, f32[576]{0:T(1024)}, /*index=5*/f32[576]{0:T(1024)}) custom-call(bf16[576]{0:T(1024)(128)(2,1)S(1)} %copy-done.8, bf16[4,80,384]{2,1,0:T(8,128)(2,1)S(1)} %get-tuple-element.123.refs_1_, ...), custom_call_target="tpu_custom_call" | custom-call | bytes 4194304 | tf_op jit(solution)/shard_map/pallas_call | solution.py:108
  (129 shorter events, 20.8 us)
Async XLA Ops:
  4.3 9.9 %collective-permute-start.2 = (bf16[256,384]{1,0:T(8,128)(2,1)}, bf16[256,384]{1,0:T(8,128)(2,1)S(1)}, u32[]{:S(2)}, u32[]{:S(2)}) collective-permute-start(bf16[256,384]{1,0:T(8,128)(2,1)} %get-tuple-element.66.refs_0_), channel_id=1, source_target_pairs={{0,24},{4,28},{8,16},{12,20},{16,8},{20,12},{24,0},{28,4},{1,25},{... | collective-permute-start | bytes 589832 | tf_op jit(solution)/shard_map/ppermute | solution.py:617
  8.3 9.3 %collective-permute-start.1 = (bf16[256,384]{1,0:T(8,128)(2,1)}, bf16[256,384]{1,0:T(8,128)(2,1)S(1)}, u32[]{:S(2)}, u32[]{:S(2)}) collective-permute-start(bf16[256,384]{1,0:T(8,128)(2,1)} %get-tuple-element.66.refs_0_), channel_id=1, source_target_pairs={{0,16},{4,20},{8,24},{12,28},{16,0},{20,4},{24,8},{28,12},{1,17},{... | collective-permute-start | bytes 589832 | tf_op jit(solution)/shard_map/ppermute | solution.py:617
  8.8 9.1 %collective-permute-start = (bf16[256,384]{1,0:T(8,128)(2,1)}, bf16[256,384]{1,0:T(8,128)(2,1)S(1)}, u32[]{:S(2)}, u32[]{:S(2)}) collective-permute-start(bf16[256,384]{1,0:T(8,128)(2,1)} %get-tuple-element.66.refs_0_), channel_id=1, source_target_pairs={{0,8},{4,12},{8,0},{12,4},{16,24},{20,28},{24,16},{28,20},{1,9},{5... | collective-permute-start | bytes 589832 | tf_op jit(solution)/shard_map/ppermute | solution.py:617
  35.7 6.7 %collective-permute-start.16 = (bf16[144,256]{1,0:T(8,128)(2,1)S(1)}, bf16[144,256]{1,0:T(8,128)(2,1)S(1)}, u32[]{:S(2)}, u32[]{:S(2)}) collective-permute-start(bf16[144,256]{1,0:T(8,128)(2,1)S(1)} %copy-done.15), channel_id=1, source_target_pairs={{0,24},{4,28},{8,16},{12,20},{16,8},{20,12},{24,0},{28,4},{1,25},{... | collective-permute-start | bytes 221192 | tf_op jit(solution)/shard_map/ppermute | solution.py:617
  39.5 8.0 %collective-permute-start.5 = (bf16[72,1152]{1,0:T(8,128)(2,1)S(1)}, bf16[72,1152]{1,0:T(8,128)(2,1)S(1)}, u32[]{:S(2)}, u32[]{:S(2)}) collective-permute-start(bf16[72,1152]{1,0:T(8,128)(2,1)S(1)} %get-tuple-element.115), channel_id=1, source_target_pairs={{0,8},{4,12},{8,0},{12,4},{16,24},{20,28},{24,16},{28,20},{1,9},{5... | collective-permute-start | bytes 497672 | tf_op jit(solution)/shard_map/ppermute | solution.py:617
  41.0 10.0 %collective-permute-start.7 = (bf16[72,1152]{1,0:T(8,128)(2,1)S(1)}, bf16[72,1152]{1,0:T(8,128)(2,1)S(1)}, u32[]{:S(2)}, u32[]{:S(2)}) collective-permute-start(bf16[72,1152]{1,0:T(8,128)(2,1)S(1)} %get-tuple-element.116), channel_id=1, source_target_pairs={{0,24},{4,28},{8,16},{12,20},{16,8},{20,12},{24,0},{28,4},{1,25},{... | collective-permute-start | bytes 497672 | tf_op jit(solution)/shard_map/ppermute | solution.py:617
  42.4 8.8 %collective-permute-start.6 = (bf16[72,1152]{1,0:T(8,128)(2,1)S(1)}, bf16[72,1152]{1,0:T(8,128)(2,1)S(1)}, u32[]{:S(2)}, u32[]{:S(2)}) collective-permute-start(bf16[72,1152]{1,0:T(8,128)(2,1)S(1)} %get-tuple-element.117), channel_id=1, source_target_pairs={{0,16},{4,20},{8,24},{12,28},{16,0},{20,4},{24,8},{28,12},{1,17},{... | collective-permute-start | bytes 497672 | tf_op jit(solution)/shard_map/ppermute | solution.py:617
  43.0 9.8 %collective-permute-start.8 = (bf16[64,576]{1,0:T(8,128)(2,1)S(1)}, bf16[64,576]{1,0:T(8,128)(2,1)S(1)}, u32[]{:S(2)}, u32[]{:S(2)}) collective-permute-start(bf16[64,576]{1,0:T(8,128)(2,1)S(1)} %copy-done.31), channel_id=1, source_target_pairs={{0,1},{1,0},{2,3},{3,2},{4,5},{5,4},{6,7},{7,6},{8,9},{9,8},{10,11... | collective-permute-start | bytes 221192 | tf_op jit(solution)/shard_map/ppermute | solution.py:617
  44.7 8.2 %collective-permute-start.9 = (bf16[64,576]{1,0:T(8,128)(2,1)S(1)}, bf16[64,576]{1,0:T(8,128)(2,1)S(1)}, u32[]{:S(2)}, u32[]{:S(2)}) collective-permute-start(bf16[64,576]{1,0:T(8,128)(2,1)S(1)} %copy-done.30), channel_id=1, source_target_pairs={{0,2},{1,3},{2,0},{3,1},{4,6},{5,7},{6,4},{7,5},{8,10},{9,11},{10,... | collective-permute-start | bytes 221192 | tf_op jit(solution)/shard_map/ppermute | solution.py:617
  47.4 6.4 %collective-permute-start.10 = (bf16[64,576]{1,0:T(8,128)(2,1)S(1)}, bf16[64,576]{1,0:T(8,128)(2,1)S(1)}, u32[]{:S(2)}, u32[]{:S(2)}) collective-permute-start(bf16[64,576]{1,0:T(8,128)(2,1)S(1)} %copy-done.29), channel_id=1, source_target_pairs={{0,3},{1,2},{2,1},{3,0},{4,7},{5,6},{6,5},{7,4},{8,11},{9,10},{10,... | collective-permute-start | bytes 221192 | tf_op jit(solution)/shard_map/ppermute | solution.py:617
  51.0 12.5 %collective-permute-start.17 = (bf16[4,144,256]{2,1,0:T(8,128)(2,1)S(1)}, bf16[4,144,256]{2,1,0:T(8,128)(2,1)S(1)}, u32[]{:S(2)}, u32[]{:S(2)}) collective-permute-start(bf16[4,144,256]{2,1,0:T(8,128)(2,1)S(1)} %pad_maximum_fusion.3), channel_id=1, source_target_pairs={{0,4},{4,0},{8,12},{12,8},{16,20},{20,16},{24,28},{28,24},{1,5},{5... | collective-permute-start | bytes 884744 | tf_op jit(solution)/shard_map/ppermute | solution.py:617
  51.3 32.2 %collective-permute-start.18 = (bf16[72,1152]{1,0:T(8,128)(2,1)S(1)}, bf16[72,1152]{1,0:T(8,128)(2,1)S(1)}, u32[]{:S(2)}, u32[]{:S(2)}) collective-permute-start(bf16[72,1152]{1,0:T(8,128)(2,1)S(1)} %fusion.7.refs_4_), channel_id=1, source_target_pairs={{0,24},{4,28},{8,16},{12,20},{16,8},{20,12},{24,0},{28,4},{1,25},{... | collective-permute-start | bytes 497672 | tf_op jit(solution)/shard_map/ppermute | solution.py:617
  53.9 6.3 %collective-permute-start.13 = (bf16[64,576]{1,0:T(8,128)(2,1)S(1)}, bf16[64,576]{1,0:T(8,128)(2,1)S(1)}, u32[]{:S(2)}, u32[]{:S(2)}) collective-permute-start(bf16[64,576]{1,0:T(8,128)(2,1)S(1)} %add_convert_fusion.refs_0_), channel_id=1, source_target_pairs={{0,3},{1,2},{2,1},{3,0},{4,7},{5,6},{6,5},{7,4},{8,11},{9,10},{10,... | collective-permute-start | bytes 221192 | tf_op jit(solution)/shard_map/ppermute | solution.py:617
  83.5 7.8 %collective-permute-start.19 = (bf16[4,144,384]{2,1,0:T(8,128)(2,1)}, bf16[4,144,384]{2,1,0:T(8,128)(2,1)S(1)}, u32[]{:S(2)}, u32[]{:S(2)}) collective-permute-start(bf16[4,144,384]{2,1,0:T(8,128)(2,1)} %get-tuple-element.88), channel_id=1, source_target_pairs={{0,4},{4,0},{8,12},{12,8},{16,20},{20,16},{24,28},{28,24},{1,5},{5... | collective-permute-start | bytes 1327112 | tf_op jit(solution)/shard_map/ppermute | solution.py:617
  83.6 6.7 %collective-permute-start.30 = (bf16[72,1152]{1,0:T(8,128)(2,1)S(1)}, bf16[72,1152]{1,0:T(8,128)(2,1)S(1)}, u32[]{:S(2)}, u32[]{:S(2)}) collective-permute-start(bf16[72,1152]{1,0:T(8,128)(2,1)S(1)} %fusion.7.refs_4_), channel_id=1, source_target_pairs={{0,16},{4,20},{8,24},{12,28},{16,0},{20,4},{24,8},{28,12},{1,17},{... | collective-permute-start | bytes 497672 | tf_op jit(solution)/shard_map/ppermute | solution.py:617
  84.7 6.3 %collective-permute-start.29 = (bf16[72,1152]{1,0:T(8,128)(2,1)S(1)}, bf16[72,1152]{1,0:T(8,128)(2,1)S(1)}, u32[]{:S(2)}, u32[]{:S(2)}) collective-permute-start(bf16[72,1152]{1,0:T(8,128)(2,1)S(1)} %fusion.7.refs_4_), channel_id=1, source_target_pairs={{0,8},{4,12},{8,0},{12,4},{16,24},{20,28},{24,16},{28,20},{1,9},{5... | collective-permute-start | bytes 497672 | tf_op jit(solution)/shard_map/ppermute | solution.py:617
  91.2 26.6 %collective-permute-start.31 = (bf16[4,72,1152]{2,1,0:T(8,128)(2,1)S(1)}, bf16[4,72,1152]{2,1,0:T(8,128)(2,1)S(1)}, u32[]{:S(2)}, u32[]{:S(2)}) collective-permute-start(bf16[4,72,1152]{2,1,0:T(8,128)(2,1)S(1)} %pad_maximum_fusion.2), channel_id=1, source_target_pairs={{0,4},{4,0},{8,12},{12,8},{16,20},{20,16},{24,28},{28,24},{1,5},{5... | collective-permute-start | bytes 1990664 | tf_op jit(solution)/shard_map/ppermute | solution.py:617
  91.5 6.8 %collective-permute-start.22 = (bf16[144,384]{1,0:T(8,128)(2,1)S(1)}, bf16[144,384]{1,0:T(8,128)(2,1)S(1)}, u32[]{:S(2)}, u32[]{:S(2)}) collective-permute-start(bf16[144,384]{1,0:T(8,128)(2,1)S(1)} %get-tuple-element.118), channel_id=1, source_target_pairs={{0,24},{4,28},{8,16},{12,20},{16,8},{20,12},{24,0},{28,4},{1,25},{... | collective-permute-start | bytes 331784 | tf_op jit(solution)/shard_map/ppermute | solution.py:617
  93.0 7.3 %collective-permute-start.21 = (bf16[144,384]{1,0:T(8,128)(2,1)S(1)}, bf16[144,384]{1,0:T(8,128)(2,1)S(1)}, u32[]{:S(2)}, u32[]{:S(2)}) collective-permute-start(bf16[144,384]{1,0:T(8,128)(2,1)S(1)} %get-tuple-element.119), channel_id=1, source_target_pairs={{0,16},{4,20},{8,24},{12,28},{16,0},{20,4},{24,8},{28,12},{1,17},{... | collective-permute-start | bytes 331784 | tf_op jit(solution)/shard_map/ppermute | solution.py:617
  94.1 8.7 %collective-permute-start.20 = (bf16[144,384]{1,0:T(8,128)(2,1)S(1)}, bf16[144,384]{1,0:T(8,128)(2,1)S(1)}, u32[]{:S(2)}, u32[]{:S(2)}) collective-permute-start(bf16[144,384]{1,0:T(8,128)(2,1)S(1)} %get-tuple-element.120), channel_id=1, source_target_pairs={{0,8},{4,12},{8,0},{12,4},{16,24},{20,28},{24,16},{28,20},{1,9},{5... | collective-permute-start | bytes 331784 | tf_op jit(solution)/shard_map/ppermute | solution.py:617
  95.1 9.2 %collective-permute-start.23 = (bf16[64,576]{1,0:T(8,128)(2,1)S(1)}, bf16[64,576]{1,0:T(8,128)(2,1)S(1)}, u32[]{:S(2)}, u32[]{:S(2)}) collective-permute-start(bf16[64,576]{1,0:T(8,128)(2,1)S(1)} %copy-done.28), channel_id=1, source_target_pairs={{0,1},{1,0},{2,3},{3,2},{4,5},{5,4},{6,7},{7,6},{8,9},{9,8},{10,11... | collective-permute-start | bytes 221192 | tf_op jit(solution)/shard_map/ppermute | solution.py:617
  98.3 8.8 %collective-permute-start.24 = (bf16[64,576]{1,0:T(8,128)(2,1)S(1)}, bf16[64,576]{1,0:T(8,128)(2,1)S(1)}, u32[]{:S(2)}, u32[]{:S(2)}) collective-permute-start(bf16[64,576]{1,0:T(8,128)(2,1)S(1)} %copy-done.27), channel_id=1, source_target_pairs={{0,2},{1,3},{2,0},{3,1},{4,6},{5,7},{6,4},{7,5},{8,10},{9,11},{10,... | collective-permute-start | bytes 221192 | tf_op jit(solution)/shard_map/ppermute | solution.py:617
  100.3 7.0 %collective-permute-start.25 = (bf16[64,576]{1,0:T(8,128)(2,1)S(1)}, bf16[64,576]{1,0:T(8,128)(2,1)S(1)}, u32[]{:S(2)}, u32[]{:S(2)}) collective-permute-start(bf16[64,576]{1,0:T(8,128)(2,1)S(1)} %copy-done.26), channel_id=1, source_target_pairs={{0,3},{1,2},{2,1},{3,0},{4,7},{5,6},{6,5},{7,4},{8,11},{9,10},{10,... | collective-permute-start | bytes 221192 | tf_op jit(solution)/shard_map/ppermute | solution.py:617
  102.8 11.4 %collective-permute-start.34 = (bf16[80,384]{1,0:T(8,128)(2,1)S(1)}, bf16[80,384]{1,0:T(8,128)(2,1)S(1)}, u32[]{:S(2)}, u32[]{:S(2)}) collective-permute-start(bf16[80,384]{1,0:T(8,128)(2,1)S(1)} %fusion.17), channel_id=1, source_target_pairs={{0,3},{1,2},{2,1},{3,0},{4,7},{5,6},{6,5},{7,4},{8,11},{9,10},{10,... | collective-permute-start | bytes 184328 | tf_op jit(solution)/shard_map/ppermute | solution.py:617
  104.2 10.0 %collective-permute-start.33 = (bf16[80,384]{1,0:T(8,128)(2,1)S(1)}, bf16[80,384]{1,0:T(8,128)(2,1)S(1)}, u32[]{:S(2)}, u32[]{:S(2)}) collective-permute-start(bf16[80,384]{1,0:T(8,128)(2,1)S(1)} %fusion.17), channel_id=1, source_target_pairs={{0,2},{1,3},{2,0},{3,1},{4,6},{5,7},{6,4},{7,5},{8,10},{9,11},{10,... | collective-permute-start | bytes 184328 | tf_op jit(solution)/shard_map/ppermute | solution.py:617
  107.1 7.1 %collective-permute-start.32 = (bf16[80,384]{1,0:T(8,128)(2,1)S(1)}, bf16[80,384]{1,0:T(8,128)(2,1)S(1)}, u32[]{:S(2)}, u32[]{:S(2)}) collective-permute-start(bf16[80,384]{1,0:T(8,128)(2,1)S(1)} %fusion.17), channel_id=1, source_target_pairs={{0,1},{1,0},{2,3},{3,2},{4,5},{5,4},{6,7},{7,6},{8,9},{9,8},{10,11... | collective-permute-start | bytes 184328 | tf_op jit(solution)/shard_map/ppermute | solution.py:617
  110.0 10.0 %collective-permute-start.28 = (bf16[64,1216]{1,0:T(8,128)(2,1)S(1)}, bf16[64,1216]{1,0:T(8,128)(2,1)S(1)}, u32[]{:S(2)}, u32[]{:S(2)}) collective-permute-start(bf16[64,1216]{1,0:T(8,128)(2,1)S(1)} %shard_map.234.refs_0_), channel_id=1, source_target_pairs={{0,3},{1,2},{2,1},{3,0},{4,7},{5,6},{6,5},{7,4},{8,11},{9,10},{10,... | collective-permute-start | bytes 466952 | tf_op jit(solution)/shard_map/ppermute | solution.py:617
  114.3 17.2 %collective-permute-start.37 = (bf16[4,80,384]{2,1,0:T(8,128)(2,1)S(1)}, bf16[4,80,384]{2,1,0:T(8,128)(2,1)S(1)}, u32[]{:S(2)}, u32[]{:S(2)}) collective-permute-start(bf16[4,80,384]{2,1,0:T(8,128)(2,1)S(1)} %get-tuple-element.123.refs_1_), channel_id=1, source_target_pairs={{0,24},{4,28},{8,16},{12,20},{16,8},{20,12},{24,0},{28,4},{1,25},{... | collective-permute-start | bytes 737288 | tf_op jit(solution)/shard_map/ppermute | solution.py:617
  116.0 15.4 %collective-permute-start.36 = (bf16[4,80,384]{2,1,0:T(8,128)(2,1)S(1)}, bf16[4,80,384]{2,1,0:T(8,128)(2,1)S(1)}, u32[]{:S(2)}, u32[]{:S(2)}) collective-permute-start(bf16[4,80,384]{2,1,0:T(8,128)(2,1)S(1)} %get-tuple-element.123.refs_1_), channel_id=1, source_target_pairs={{0,16},{4,20},{8,24},{12,28},{16,0},{20,4},{24,8},{28,12},{1,17},{... | collective-permute-start | bytes 737288 | tf_op jit(solution)/shard_map/ppermute | solution.py:617
  117.0 14.5 %collective-permute-start.35 = (bf16[4,80,384]{2,1,0:T(8,128)(2,1)S(1)}, bf16[4,80,384]{2,1,0:T(8,128)(2,1)S(1)}, u32[]{:S(2)}, u32[]{:S(2)}) collective-permute-start(bf16[4,80,384]{2,1,0:T(8,128)(2,1)S(1)} %get-tuple-element.123.refs_1_), channel_id=1, source_target_pairs={{0,8},{4,12},{8,0},{12,4},{16,24},{20,28},{24,16},{28,20},{1,9},{5... | collective-permute-start | bytes 737288 | tf_op jit(solution)/shard_map/ppermute | solution.py:617
  117.8 9.9 %collective-permute-start.27 = (bf16[64,1216]{1,0:T(8,128)(2,1)S(1)}, bf16[64,1216]{1,0:T(8,128)(2,1)S(1)}, u32[]{:S(2)}, u32[]{:S(2)}) collective-permute-start(bf16[64,1216]{1,0:T(8,128)(2,1)S(1)} %shard_map.234.refs_0_), channel_id=1, source_target_pairs={{0,2},{1,3},{2,0},{3,1},{4,6},{5,7},{6,4},{7,5},{8,10},{9,11},{10,... | collective-permute-start | bytes 466952 | tf_op jit(solution)/shard_map/ppermute | solution.py:617
  120.0 9.4 %collective-permute-start.26 = (bf16[64,1216]{1,0:T(8,128)(2,1)S(1)}, bf16[64,1216]{1,0:T(8,128)(2,1)S(1)}, u32[]{:S(2)}, u32[]{:S(2)}) collective-permute-start(bf16[64,1216]{1,0:T(8,128)(2,1)S(1)} %shard_map.234.refs_0_), channel_id=1, source_target_pairs={{0,1},{1,0},{2,3},{3,2},{4,5},{5,4},{6,7},{7,6},{8,9},{9,8},{10,11... | collective-permute-start | bytes 466952 | tf_op jit(solution)/shard_map/ppermute | solution.py:617
  (39 other events, 357.7 us)

commit v3 on v2

--- a/solution.py
+++ b/solution.py
@@ -66,7 +66,7 @@
         self.sent = True
 
 
-def call(body, ins, in_kinds, outs, out_kinds, scratch=(), vmem=60, flops=0):
+def call(body, ins, in_kinds, outs, out_kinds, scratch=(), vmem=60, early=None, early_at=0, micros=3):
     real = [(a, kind) for a, kind in zip(ins, in_kinds) if kind != "m"]
     staged = [a for a, kind in real if kind == "c"]
     staged_out = [o for o, kind in zip(outs, out_kinds) if kind == "c"]
@@ -83,19 +83,24 @@
         at = 0
         given, results = [], []
         for kind in in_kinds:
-            ref = (lax.axis_index("ctx"), lax.axis_index("wt")) if kind == "m" else next(in_refs)
+            place = (lax.axis_index("ctx"), lax.axis_index("wt")) if kind == "m" else next(in_refs)
+            given.append(place)
+        state = ()
+        for i, kind in enumerate(in_kinds):
+            if early is not None and i == early_at:
+                state = (early(given, own),)
             if kind == "c":
+                ref = given[i]
                 copy = pltpu.make_async_copy(ref, extra[at], extra[-1].at[at])
                 copy.start()
-                ref = Fetched(copy, extra[at])
+                given[i] = Fetched(copy, extra[at])
                 at += 1
-            given.append(ref)
         for ref, kind in zip(out_refs, out_kinds):
             if kind == "c":
                 ref = Stored(pltpu.make_async_copy(extra[at], ref, extra[-1].at[at]), extra[at])
                 at += 1
             results.append(ref)
-        body(given, results, own)
+        body(given, results, own, *state)
         for item in given:
             if isinstance(item, Fetched):
                 item.get()
@@ -112,7 +117,7 @@
         out_specs=tuple(SPEC[k] for k in out_kinds),
         scratch_shapes=list(scratch) + buffers,
         compiler_params=pltpu.CompilerParams(vmem_limit_bytes=vmem * MIB),
-        cost_estimate=pl.CostEstimate(flops=flops, bytes_accessed=4 * MIB, transcendentals=0),
+        cost_estimate=pl.CostEstimate(flops=micros * 1_150_000_000, bytes_accessed=MIB, transcendentals=0),
     )(*[a for a, _ in real])
 
 
@@ -142,20 +147,29 @@
     return lax.rsqrt(jnp.mean(x * x, axis=axis, keepdims=True) + EPSILON)
 
 
-def key_body(ins, outs, scratch):
+def key_early(ins, scratch):
+    meta, order, turned = ins[0], ins[1], ins[-1]
+    copies = []
+    for half in range(2):
+        src = turned.at[order[0, 2 * meta[0] + half]]
+        copies.append(pltpu.make_async_copy(src, scratch[1].at[half], scratch[2].at[half]))
+        copies[-1].start()
+    return copies
+
+
+def key_body(ins, outs, scratch, copies):
     meta, order, gain, tok, wk, wv, turned = ins
     normed_out, kv_out, angle_out, normed_q = outs
-    (normed_s,) = scratch
-    me = meta[0]
-    low, high = order[0, 2 * me], order[0, 2 * me + 1]
-    x = tok[...].astype(F32)
-    gain = jnp.broadcast_to(row_of(gain), (8, x.shape[0])).T[:, 0:1]
+    normed_s, angle_s, sems = scratch
+    x = tok.get()[...].astype(F32)
+    gain = jnp.broadcast_to(row_of(gain.get()), (8, x.shape[0])).T[:, 0:1]
     normed = (x * norm_scale(x, 0) * gain).astype(BF)
     normed_out[...] = normed
     normed_s[...] = normed.astype(F32)
     normed_q[...] = normed_s[span(meta[1], normed_q.shape[0]), :].astype(BF)
-    turned = turned.get()
-    angle = jnp.concatenate([turned[low], turned[high]], axis=1)
+    for copy in copies:
+        copy.wait()
+    angle = jnp.concatenate([angle_s[0], angle_s[1]], axis=1)
     angle_out[...] = angle
     cos, sin = angle[:HALF], angle[HALF:]
     k = dot(wk.get()[...], normed)
@@ -220,35 +234,37 @@
     return pl.ds(pl.multiple_of(index * size, size), size)
 
 
-def forward_body(n, wt, ins, outs, scratch):
-    evens = ins[: n // 2]
+def natural_copies(n, me, order, evens, odds, to, sems, stretch, lanes=False):
+    copies = []
+    for k in range(n):
+        low = order[0, 2 * lax.bitwise_xor(me, k)]
+        src = evens[k // 2] if k % 2 == 0 else odds.at[k // 2]
+        for half in range(2):
+            at = span(low if half == 0 else 2 * n - 1 - low, stretch)
+            cut = slice(half * stretch, (half + 1) * stretch)
+            src_cut, to_cut = (src.at[:, cut], to.at[:, at]) if lanes else (src.at[cut], to.at[at])
+            copies.append(pltpu.make_async_copy(src_cut, to_cut, sems.at[2 * k + half]))
+    for copy in copies:
+        copy.start()
+    return copies
+
+
+def forward_early(n, ins, scratch):
+    evens, (odds, meta, order) = ins[: n // 2], ins[n // 2 : n // 2 + 3]
+    return natural_copies(n, meta[0], order, evens, odds, scratch[0], scratch[-1], evens[0].shape[0] // 2)
+
+
+def forward_body(n, wt, ins, outs, scratch, copies):
     odds, meta, order, q_in, tok, w_out, gain, w_gate, w_up, cot, w_down = ins[n // 2 :]
-    kv_all, att_t_out, lse_out, mixed_out, even, odd = outs[:6]
+    att_t_out, lse_out, mixed_out, even, odd, mixed_q = outs[:6]
     pin_outs, out_parts = outs[6 : 6 + wt], outs[6 + wt :]
     kvn, m_s, l_s, o_s, part, grads, sems = scratch
     rows = tok.ref.shape[1]
     stretch = rows // 2
     wide = GROUP * stretch
     me = meta[0]
-    copies = []
-    for k in range(n):
-        low = order[0, 2 * lax.bitwise_xor(me, k)]
-        src = evens[k // 2] if k % 2 == 0 else odds.at[k // 2]
-        for half in range(2):
-            to = low if half == 0 else 2 * n - 1 - low
-            copies.append(
-                pltpu.make_async_copy(
-                    src.at[half * stretch : (half + 1) * stretch],
-                    kvn.at[span(to, stretch)],
-                    sems.at[2 * k + half],
-                )
-            )
-    for copy in copies:
-        copy.start()
     for copy in copies:
         copy.wait()
-    keep = pltpu.make_async_copy(kvn, kv_all, sems.at[2 * n])
-    keep.start()
     c = order[0, 2 * me]
     low_group, low_steps, unit_group, unit_steps = parts_of(n)
     q_ref = q_in.get()
@@ -319,9 +335,12 @@
     att_t_out.send()
     att_low = att_t[...].T.astype(BF)
     mixed = tok.get()[...].astype(F32).T + dot(att_low, w_out.get()[...])
-    mixed_out.ref[...] = mixed
+    width = mixed.shape[1]
+    part[...] = jnp.zeros(part.shape, F32)
+    part[:, :width] = mixed
+    mixed_out.ref[...] = part[...]
     mixed_out.send()
-    n2 = (mixed * norm_scale(mixed, -1) * row_of(gain)).astype(BF)
+    n2 = (mixed * norm_scale(mixed, -1) * row_of(gain.get())).astype(BF)
     gate = dot(n2, w_gate.get()[...])
     up = dot(n2, w_up.get()[...])
     sig = 1.0 / (1.0 + jnp.exp(-gate))
@@ -331,67 +350,69 @@
     gl = (grad_hidden * up * (sig * (1.0 + gate * (1.0 - sig)))).astype(BF)
     ul = (grad_hidden * silu).astype(BF)
     piece = rows // wt
-    part[...] = dot_nt(gl, w_gate.get()[...]) + dot_nt(ul, w_up.get()[...])
+    mixed_q.ref[...] = part[span(meta[1], piece), :]
+    mixed_q.send()
+    part[:, :width] = dot_nt(gl, w_gate.get()[...]) + dot_nt(ul, w_up.get()[...])
     for k in range(wt):
-        pin_outs[k][...] = part[span(lax.bitwise_xor(meta[1], k), piece), :].astype(BF)
-    part[...] = dot_nt(hidden, w_down.get()[...])
+        pin_outs[k].ref[...] = part[span(lax.bitwise_xor(meta[1], k), piece), :].astype(BF)
+        pin_outs[k].send()
+    part[:, :width] = dot_nt(hidden, w_down.get()[...])
     for k in range(wt):
-        out_parts[k][...] = part[span(lax.bitwise_xor(meta[1], k), piece), :].astype(BF)
-    width = gl.shape[1]
-    grads[:, :width] = dot_tn(n2, gl)
-    grads[:, width : 2 * width] = dot_tn(n2, ul)
-    grads[:, 2 * width :] = dot(cot.get()[...], hidden)
+        out_parts[k].ref[...] = part[span(lax.bitwise_xor(meta[1], k), piece), :].astype(BF)
+        out_parts[k].send()
+    units = gl.shape[1]
+    grads[:, :units] = dot_tn(n2, gl)
+    grads[:, units : 2 * units] = dot_tn(n2, ul)
+    grads[:, 2 * units :] = dot(cot.get()[...], hidden)
     if n > 8:
-        even[...] = grads[...].astype(BF)
-        odd[...] = jnp.zeros(odd.shape, BF)
+        even.ref[...] = grads[...].astype(BF)
+        odd.ref[...] = jnp.zeros(odd.ref.shape, BF)
     else:
         size = grads.shape[0] // n
         for k in range(n):
-            to = even if k % 2 == 0 else odd
+            to = even.ref if k % 2 == 0 else odd.ref
             to[k // 2] = grads[span(lax.bitwise_xor(me, k), size), :].astype(BF)
-    keep.wait()
-
-
-def backward_body(n, wt, ins, outs, scratch):
+
+
+def backward_early(n, wt, ins, scratch):
+    meta, order = ins[wt], ins[wt + 1]
+    blocks = ins[wt + 16 :]
+    count = n // 2 + 1
+    evens, odds = blocks[: count - 1], blocks[count - 1]
+    strips, strip_odds = blocks[count : 2 * count - 1], blocks[2 * count - 1]
+    stretch = evens[0].shape[0] // 2
+    all_s, kv, sems, strip_sems = scratch[8], scratch[10], scratch[11], scratch[12]
+    kv_copies = natural_copies(n, meta[0], order, evens, odds, kv, sems, stretch)
+    return kv_copies, natural_copies(
+        n, meta[0], order, strips, strip_odds, all_s, strip_sems, stretch, True
+    )
+
+
+def backward_body(n, wt, ins, outs, scratch, copies):
+    kv_copies, strip_copies = copies
     quarters = ins[:wt]
-    (meta, order, gain, mixed, cot, w_out, att_t, lse, kv, q_in, angle) = ins[wt : wt + 11]
-    (first, inner, normed, wq, wk, wv, strip_odds) = ins[wt + 11 : wt + 18]
-    strips = ins[wt + 18 :]
+    (meta, order, gain, mixed, cot, w_out, att_t, lse, q_in, angle) = ins[wt : wt + 10]
+    (first, inner, normed, wq, wk, wv) = ins[wt + 10 : wt + 16]
     gm_out, dq_out, even, odd = outs[:4]
-    gn_s, do_s, dl_s, dkv, dq_s, dq_t, grads, norm_s, all_s, w_s, sems = scratch
+    gn_s, do_s, dl_s, dkv, dq_s, dq_t, grads, norm_s, all_s, w_s, kv = scratch[:11]
     rows = mixed.ref.shape[0]
-    width = mixed.ref.shape[1]
+    width = gain.ref.shape[0]
     stretch = rows // 2
     wide = GROUP * stretch
     me = meta[0]
     c = order[0, 2 * me]
     low_group, low_steps, unit_group, unit_steps = parts_of(n)
-    copies = []
-    for k in range(n):
-        low = order[0, 2 * lax.bitwise_xor(me, k)]
-        src = strips[k // 2] if k % 2 == 0 else strip_odds.at[k // 2]
-        for half in range(2):
-            to = low if half == 0 else 2 * n - 1 - low
-            copies.append(
-                pltpu.make_async_copy(
-                    src.at[:, half * stretch : (half + 1) * stretch],
-                    all_s.at[:, span(to, stretch)],
-                    sems.at[2 * k + half],
-                )
-            )
-    for copy in copies:
-        copy.start()
-
     piece = rows // wt
     for k in range(wt):
-        gn_s[span(lax.bitwise_xor(meta[1], k), piece), :] = quarters[k][...].astype(F32)
-    x = mixed.get()[...]
-    gn = gn_s[...]
+        gn_s[span(lax.bitwise_xor(meta[1], k), piece), :] = quarters[k].get()[...].astype(F32)
+    x = mixed.get()[:, :width]
+    gn = gn_s[:, :width]
     r = norm_scale(x, -1)
     xn = x * r
-    e = gn * row_of(gain)
+    e = gn * row_of(gain.get())
     gm = cot.get()[...].astype(F32).T + r * (e - xn * jnp.mean(e * xn, axis=-1, keepdims=True))
-    gm_out.ref[...] = gm
+    gn_s[:, :width] = gm
+    gm_out.ref[...] = gn_s[span(meta[1], piece), :]
     gm_out.send()
     norm_s[...] = jnp.zeros(norm_s.shape, F32)
     norm_s[1:2, :width] = jnp.sum(gn * xn, axis=0, keepdims=True)
@@ -411,8 +432,15 @@
     strip = grads.shape[0]
     mine = span(meta[1], strip)
     grads[:, width : 2 * width] = dot(att_t.get()[mine, :].astype(BF), branch)
-    lse, kv, q_ref, angle = lse.get(), kv.get(), q_in.get(), angle.get()
+    lse, q_ref, angle = lse.get(), q_in.get(), angle.get()
+    for copy in kv_copies:
+        copy.wait()
     first, inner = first.get(), inner.get()
+    chunk = 4
+    low_chunks = lax.shift_right_logical(c, 2)
+    key_ids = lax.broadcasted_iota(jnp.int32, (chunk * stretch, wide), 0)
+    query_ids = lax.broadcasted_iota(jnp.int32, (chunk * stretch, wide), 1)
+    query_ids = lax.bitwise_and(query_ids, stretch - 1)
     pre = kv
     lane_ids = lax.broadcasted_iota(jnp.int32, (stretch, PAIR), 1)
 
@@ -433,20 +461,26 @@
 
         loop(low_steps, low_step)
 
-        def unit_step(i):
-            for j in range(unit_group):
-                _, sel, st, diagonal = unit(i * unit_group + j, c, n)
-                at = span(st, stretch)
-                keys = kv[at, lanes]
-                q = q_ref[g, span(sel, wide), :]
-                do = do_s[g, span(sel, wide), :]
-                p = jnp.exp(dot_nt(keys, q) - lse[2 * g + sel])
-                p = jnp.where(seen_mask(stretch, diagonal), p, 0.0)
-                ds = (p * (dot_nt(keys, do) - dl_s[2 * g + sel])).astype(BF)
-                dkv[at, :] += dot(ds, q) + dot(p.astype(BF), do)
-                dq_s[sel] += dot_tn(keys, ds)
-
-        loop(unit_steps, unit_step)
+        def unit_step(u):
+            is_low = u <= low_chunks
+            sel = jnp.where(is_low, 0, 1)
+            low_key = jnp.where(is_low, u, u - low_chunks - 1 + n // chunk) * (chunk * stretch)
+            at = pl.ds(pl.multiple_of(low_key, chunk * stretch), chunk * stretch)
+            keys = kv[at, lanes]
+            q = q_ref[g, span(sel, wide), :]
+            do = do_s[g, span(sel, wide), :]
+            p = jnp.exp(dot_nt(keys, q) - lse[2 * g + sel])
+            ahead = low_key - jnp.where(is_low, c, 2 * n - 1 - c) * stretch
+            p = jnp.where(key_ids + ahead <= query_ids, p, 0.0)
+            ds = (p * (dot_nt(keys, do) - dl_s[2 * g + sel])).astype(BF)
+            dkv[at, :] += dot(ds, q) + dot(p.astype(BF), do)
+            dq_s[sel] += dot_tn(keys, ds)
+
+        if n <= 8:
+            for u in range(n // chunk + 1):
+                unit_step(u)
+        else:
+            loop(n // chunk + 1, unit_step)
 
         def turn(i):
             ct, st = inner[0], inner[1]
@@ -474,10 +508,11 @@
 
     loop(KV_HEADS, one_head)
     dq = dq_t[...].T.astype(BF)
-    dq_out.ref[...] = dq
+    gn_s[:, :width] = dq.astype(F32)
+    dq_out.ref[...] = gn_s[span(meta[1], piece), :].astype(BF)
     dq_out.send()
     grads[:, :width] = dot(normed.get()[...], dq)
-    for copy in copies:
+    for copy in strip_copies:
         copy.wait()
     grads[:, 2 * width :] = dot(all_s[...], pre[...])
     wk, wv = wk.get()[...].astype(F32), wv.get()[...].astype(F32)
@@ -522,22 +557,16 @@
     return span(lax.bitwise_and(who, 3), KV_HEADS * PAIR)
 
 
-def finish_body(wt, count, ins, outs, scratch):
+def finish_body(count, ins, outs, scratch):
     terms = ins[:count]
-    out_terms = ins[count : count + wt]
-    meta, gain, tok, mixed, gm, dq, wq, wk, wv = ins[count + wt :]
-    (both_out,) = outs
+    meta, gain, tok, gm, dq, wq, wk, wv = ins[count:]
+    (gt_out,) = outs
     (x_s,) = scratch
-    piece = both_out.shape[0]
-    width = gain.shape[0]
+    piece = gt_out.shape[0]
     total = terms[0][:piece, :].astype(F32)
     for term in terms[1:]:
         total = total + term[:piece, :].astype(F32)
     mine = span(meta[1], piece)
-    out = out_terms[0][...].astype(F32)
-    for term in out_terms[1:]:
-        out = out + term[...].astype(F32)
-    both_out[:, 640:] = (mixed.get()[mine, :] + out).astype(BF)
     x_s[...] = tok.get()[...].astype(F32).T
     x = x_s[mine, :]
     dk, dv = [], []
@@ -546,28 +575,31 @@
         dv.append(total[:, g * PAIR + HEAD : (g + 1) * PAIR])
     dk = jnp.concatenate(dk, axis=1).astype(BF)
     dv = jnp.concatenate(dv, axis=1).astype(BF)
-    gn = dot_nt(dq.get()[mine, :], wq.get()[...])
+    width = gain.shape[0]
+    gn = dot_nt(dq[:, :width], wq.get()[...])
     gn = gn + dot(dk, wk.get()[...]) + dot(dv, wv.get()[...])
     r = norm_scale(x, -1)
     xn = x * r
     e = gn * row_of(gain)
-    result = gm.get()[mine, :] + r * (e - xn * jnp.mean(e * xn, axis=-1, keepdims=True))
-    both_out[:, :width] = result.astype(BF)
-    both_out[:, width:640] = jnp.zeros((piece, 640 - width), BF)
-
-
-def mlp_join_body(n, wt, ins, outs, scratch):
+    result = gm[:, :width] + r * (e - xn * jnp.mean(e * xn, axis=-1, keepdims=True))
+    gt_out[:, :width] = result.astype(BF)
+    gt_out[:, width:] = jnp.zeros((piece, gt_out.shape[1] - width), BF)
+
+
+def token_join_body(wt, ins, outs, scratch):
     meta = ins[0]
-    quarters = ins[1 : 1 + wt]
-    blocks = ins[1 + wt :]
-    grads, rows_s, out_s = scratch
-    piece, width = quarters[0].shape[0], rows_s.shape[1]
-    for k in range(wt):
-        at = span(lax.bitwise_xor(meta[1], k), piece)
-        rows_s[at, :] = quarters[k][:, :width].astype(F32)
-        out_s[at, :] = quarters[k][:, 640:].astype(F32)
-    outs[0][...] = rows_s[...].T
-    outs[1][...] = out_s[...].T.astype(BF)
+    (rows_s,) = scratch
+    for i in range(2):
+        quarters = ins[1 + i * wt : 1 + (i + 1) * wt]
+        for k in range(wt):
+            at = span(lax.bitwise_xor(meta[1], k), quarters[0].shape[0])
+            rows_s[at, :] = quarters[k][:, : rows_s.shape[1]].astype(F32)
+        outs[i][...] = rows_s[...].T.astype(outs[i].dtype)
+
+
+def mlp_join_body(n, ins, outs, scratch):
+    meta, blocks = ins[0], ins[1:]
+    (grads,) = scratch
     if n > 8:
         grads[...] = blocks[0][...].astype(F32)
     else:
@@ -575,9 +607,9 @@
         for k in range(n):
             block = blocks[k // 2][...] if k % 2 == 0 else blocks[-1][k // 2]
             grads[span(lax.bitwise_xor(meta[0], k), size), :] = block.astype(F32)
-    width = outs[2].shape[1]
+    width = outs[0].shape[1]
     for i in range(3):
-        outs[2 + i][...] = grads[:, i * width : (i + 1) * width]
+        outs[i][...] = grads[:, i * width : (i + 1) * width]
 
 
 def join_body(n, wt, ins, outs, scratch):
@@ -642,7 +674,7 @@
 
 def after(dep, *arrays):
     held = lax.optimization_barrier((dep,) + arrays)
-    return held[1:] if len(arrays) > 1 else held[1]
+    return list(held[1:]) if len(arrays) > 1 else held[1]
 
 
 def local(
@@ -670,17 +702,23 @@
     size = width // n
     strip = width // wt
     small = n <= 8
+    padded = -(-width // 128) * 128
     turned, first, inner = (jnp.asarray(t) for t in angle_tables(n, stretch))
     tok, cot, wk, wv, w_down = tokens.T, cotangent.T, w_key.T, w_value.T, w_down.T
 
     normed, kv, angle, normed_q = call(
         key_body,
         [None, stretch_order, norm_attn, tok, wk, wv, turned],
-        "msvvccc",
+        "mscccch",
         [shape((width, rows), BF), shape((rows, kv_width), BF), shape((HEAD, rows), F32)]
         + [shape((strip, rows), BF)],
         "vvvv",
-        scratch=[pltpu.VMEM((width, rows), F32)],
+        scratch=[
+            pltpu.VMEM((width, rows), F32),
+            pltpu.VMEM((2, HEAD, stretch), F32),
+            pltpu.SemaphoreType.DMA((2,)),
+        ],
+        early=key_early,
     )
     (q,) = call(
         query_body,
@@ -690,35 +728,39 @@
         "c",
     )
     evens = [kv] + [hop(kv, "ctx", n, k) for k in range(2, n, 2)]
-    odds = hop(jnp.stack(after(q, *evens)), "ctx", n, 1)
+    strips = [normed_q] + [hop(normed_q, "ctx", n, k) for k in range(2, n, 2)]
+    odds = hop(jnp.stack(after((q, strips), *evens)), "ctx", n, 1)
+    strip_odds = hop(jnp.stack(strips), "ctx", n, 1)
 
     mlp_columns = 3 * hidden_width
     if small:
         block_shapes = [shape((n // 2, size, mlp_columns), BF)] * 2
     else:
         block_shapes = [shape((width, mlp_columns), BF), shape((8, 128), BF)]
-    kv_all, att_t, lse, mixed, even, odd, *pieces = call(
+    att_t, lse, mixed, even, odd, mixed_q, *pieces = call(
         functools.partial(forward_body, n, wt),
         [*evens, odds, None, stretch_order, q, tok, w_out, norm_mlp, w_gate, w_up, cot, w_down],
-        "h" * (n // 2 + 1) + "msccc" + "v" + "cccc",
+        "h" * (n // 2 + 1) + "msccc" + "c" + "cccc",
         [
-            shape((n * rows, kv_width), BF),
             shape((width, rows), F32),
             shape((2 * KV_HEADS, 1, wide), F32),
-            shape((rows, width), F32),
+            shape((rows, padded), F32),
         ]
         + block_shapes
-        + [shape((piece, width), BF)] * (2 * wt),
-        "hccc" + "vv" + "v" * (2 * wt),
+        + [shape((piece, padded), F32)]
+        + [shape((piece, padded), BF)] * (2 * wt),
+        "ccc" + "ccc" + "c" * (2 * wt),
         scratch=[
             pltpu.VMEM((n * rows, kv_width), BF),
             pltpu.VMEM((2 * KV_HEADS, 1, wide), F32),
             pltpu.VMEM((2 * KV_HEADS, 1, wide), F32),
             pltpu.VMEM((2 * KV_HEADS, PAIR, wide), F32),
-            pltpu.VMEM((rows, width), F32),
+            pltpu.VMEM((rows, padded), F32),
             pltpu.VMEM((width, mlp_columns), F32),
-            pltpu.SemaphoreType.DMA((2 * n + 1,)),
+            pltpu.SemaphoreType.DMA((2 * n,)),
         ],
+        early=functools.partial(forward_early, n),
+        micros=14,
     )
     part_in, out_parts = pieces[:wt], pieces[wt:]
 
@@ -726,12 +768,10 @@
     quarter = summed(terms).astype(BF)
     quarters = [quarter] + [hop(quarter, "wt", wt, k) for k in range(1, wt)]
 
-    strips, strip_odds = gather_blocks(after(part_in[0], normed_q), "ctx", n)
     if small:
-        mlp_own = summed(scatter_terms(pair_terms(even, odd, "ctx", n), "ctx", n)).astype(BF)
-        quarters = after(mlp_own, *quarters)
-        mlp_evens, mlp_odds = gather_blocks(mlp_own, "ctx", n)
-        mlp_blocks = [*mlp_evens, mlp_odds]
+        pairs = pair_terms(even, odd, "ctx", n)
+        quarters = after(pairs[0], *quarters)
+        mlp_own = summed(scatter_terms(pairs, "ctx", n)).astype(BF)
     else:
         mlp_blocks = [lax.psum(even, "ctx")]
 
@@ -744,15 +784,15 @@
             shape((8, 128 * n), BF),
             shape((n, piece, kv_width), BF),
         ]
-    gm, dq, *message = call(
+    gm_q, dq_q, *message = call(
         functools.partial(backward_body, n, wt),
-        [*quarters, None, stretch_order, norm_mlp, mixed, cot, w_out, att_t, lse, kv_all, q, angle]
-        + [first, inner, normed_q, w_query, wk, wv, strip_odds, *strips],
-        "v" * wt + "msv" + "c" * 8 + "c" * 6 + "h" * (1 + n // 2),
-        [shape((rows, width), F32), shape((rows, width), BF)] + out_blocks,
+        [*quarters, None, stretch_order, norm_mlp, mixed, cot, w_out, att_t, lse, q, angle]
+        + [first, inner, normed_q, w_query, wk, wv, *evens, odds, *strips, strip_odds],
+        "c" * wt + "msc" + "c" * 7 + "c" * 6 + "h" * (n + 2),
+        [shape((piece, padded), F32), shape((piece, padded), BF)] + out_blocks,
         "cc" + "v" * len(out_blocks),
         scratch=[
-            pltpu.VMEM((rows, width), F32),
+            pltpu.VMEM((rows, padded), F32),
             pltpu.VMEM((KV_HEADS, 2 * wide, PAIR), BF),
             pltpu.VMEM((2 * KV_HEADS, 1, wide), F32),
             pltpu.VMEM((n * rows, PAIR), F32),
@@ -762,50 +802,65 @@
             pltpu.VMEM((8, max(128 * n, 640)), F32),
             pltpu.VMEM((strip, n * rows), BF),
             pltpu.VMEM((width, kv_width), F32),
+            pltpu.VMEM((n * rows, kv_width), BF),
+            pltpu.SemaphoreType.DMA((2 * n,)),
             pltpu.SemaphoreType.DMA((2 * n,)),
         ],
-    )
+        early=functools.partial(backward_early, n, wt),
+        early_at=wt + 10,
+        micros=17,
+    )
+    out_terms = [out_parts[0]] + [hop(out_parts[k], "wt", wt, k) for k in range(1, wt)]
+    out_q = (mixed_q + summed(out_terms)).astype(BF)
+    out_qs = [out_q] + [hop(out_q, "wt", wt, k) for k in range(1, wt)]
     if small:
-        message[1] = after(mlp_evens[-1], message[1])
+        mlp_evens, mlp_odds = gather_blocks(mlp_own, "ctx", n)
+        mlp_blocks = [*mlp_evens, mlp_odds]
+        message[1] = after((mlp_evens, out_terms), message[1])
         parts = scatter_terms(pair_terms(message[0], message[1], "ctx", n), "ctx", n)
+        parts = after(out_qs, *parts)
         own = summed([part[piece:] for part in parts]).astype(BF)
         owns = [own] + [hop(own, "wt", wt, k) for k in range(1, wt)]
     else:
         parts = [lax.psum_scatter(message[2].astype(F32), "ctx", scatter_dimension=0)]
         last_blocks = list(lax.psum((message[0], message[1]), "ctx"))
         last_blocks = [lax.all_gather(b, "wt", axis=0, tiled=i == 0) for i, b in enumerate(last_blocks)]
-    held = after(dq, *out_parts)
-    out_parts = [held[0]] + [hop(held[k], "wt", wt, k) for k in range(1, wt)]
-    (both,) = call(
-        functools.partial(finish_body, wt, len(parts)),
-        [*parts, *out_parts, None, norm_attn, tok, mixed, gm, dq, w_query, wk, wv],
-        "v" * (len(parts) + wt) + "mv" + "c" * 7,
-        [shape((piece, 640 + width), BF)],
+    (gt,) = call(
+        functools.partial(finish_body, len(parts)),
+        [*parts, None, norm_attn, tok, gm_q, dq_q, w_query, wk, wv],
+        "v" * len(parts) + "mvcvvccc",
+        [shape((piece, padded), BF)],
         "v",
         scratch=[pltpu.VMEM((rows, width), F32)],
         vmem=16,
+        micros=2,
+    )
+    gts = [gt] + [hop(gt, "wt", wt, k) for k in range(1, wt)]
+    grad_gate, grad_up, grad_down = call(
+        functools.partial(mlp_join_body, n),
+        [None, *mlp_blocks],
+        "m" + "v" * len(mlp_blocks),
+        [shape((width, hidden_width), F32)] * 3,
+        "vvv",
+        scratch=[pltpu.VMEM((width, mlp_columns), F32)],
+        vmem=24,
+        micros=2,
+    )
+    grad_tokens, output = call(
+        functools.partial(token_join_body, wt),
+        [None, *gts, *out_qs],
+        "m" + "v" * (2 * wt),
+        [shape((width, rows), F32), shape((width, rows), BF)],
+        "vv",
+        scratch=[pltpu.VMEM((rows, width), F32)],
+        vmem=24,
+        micros=2,
     )
     if small:
-        own = jnp.stack(after(both, *owns))
-        last_evens = [own] + [hop(own, "ctx", n, k) for k in range(2, n, 2)]
-    boths = [both] + [hop(both, "wt", wt, k) for k in range(1, wt)]
-
-    grad_tokens, output, grad_gate, grad_up, grad_down = call(
-        functools.partial(mlp_join_body, n, wt),
-        [None, *boths, *mlp_blocks],
-        "m" + "v" * (wt + len(mlp_blocks)),
-        [shape((width, rows), F32), shape((width, rows), BF)]
-        + [shape((width, hidden_width), F32)] * 3,
-        "vvvvv",
-        scratch=[
-            pltpu.VMEM((width, mlp_columns), F32),
-            pltpu.VMEM((rows, width), F32),
-            pltpu.VMEM((rows, width), F32),
-        ],
-        vmem=24,
-    )
-    if small:
-        last_blocks = [*last_evens, hop(after(grad_gate, jnp.stack(last_evens)), "ctx", n, 1)]
+        last = jnp.stack(after(gt, *owns))
+        last_evens = [last] + [hop(last, "ctx", n, k) for k in range(2, n, 2)]
+        last = hop(after((grad_gate, gts), jnp.stack(last_evens)), "ctx", n, 1)
+        last_blocks = [*last_evens, after(grad_tokens, last)]
     grad_query, grad_out, grad_key, grad_value, grad_norm_attn, grad_norm_mlp = call(
         functools.partial(join_body, n, wt),
         [None, norm_attn, *last_blocks],

time: 137 us -> 129 us (0.942)
  waiting for transfers between devices: 32.3 us -> 25.4 us
    ppermute x39 -> x42, waiting for transfers between devices: 32.3 us -> 25.4 us  [hop(): return lax.ppermute(x, axis, [(i, i ^ k) for i in range(size)])]
    pallas_call x7 -> x8, Pallas kernels: 48.7 us -> 47.4 us  [call(): pl.pallas_call(kernel, out_shape=tuple(outs), in_specs=[SPEC[k] for _, k...]
    ppermute x39 -> x42, starting transfers between devices: 52.4 us -> 52.5 us  [hop(): return lax.ppermute(x, axis, [(i, i ^ k) for i in range(size)])]
  transfers between devices with their start and end apart: 39 -> 42, of which waited for: 17 -> 17; matrix products, arithmetic and copies ran while one was open for 1% -> 1% of each run, Pallas kernels for 20% -> 21%
where the time goes in v3:
time: 129 us
  starting transfers between devices  52.5 us (41%)
  Pallas kernels  47.4 us (37%)
  waiting for transfers between devices  25.4 us (20%)
    ppermute x42, starting transfers between devices, hop(): return lax.ppermute(x, axis, [(i, i ^ k) for i in range(size)])  52.5 us
    pallas_call x8, Pallas kernels, call(): pl.pallas_call(kernel, out_shape=tuple(outs), in_specs=[SPEC[k] for _, k...  47.4 us
    ppermute x42, waiting for transfers between devices, hop(): return lax.ppermute(x, axis, [(i, i ^ k) for i in range(size)])  25.4 us
  transfers between devices with their start and end apart: 42, of which 17 were waited for; matrix products, arithmetic and copies ran while one was open for 1% of the time, Pallas kernels for 21%

profile of v3, /device:TPU:0, one launch (start us, length us, event | category | flops | bytes accessed | tf_op | source)
XLA Modules:
  0.0 128.5 jit_solution(14236258781483686188)
XLA Ops:
  0.6 3.4 %shard_map.230 = (bf16[576,256]{1,0:T(8,128)(2,1)}, bf16[256,384]{1,0:T(8,128)(2,1)}, f32[64,256]{1,0:T(8,128)}, bf16[144,256]{1,0:T(8,128)(2,1)}) custom-call(s32[1,16]{1,0:T(1,128)} %refs_4_.2, bf16[576]{0:T(1024)(128)(2,1)} %refs_0_.3, bf16[576,256]{1,0:T(8,128)(2,1)} %bitcast.55, bf16[192,576]{1,0:T(8,128)(2,1)} %bitcast.58, bf16[192,576]{1,0:T(8,128)(2,1)} %bitcast.61, ...), custom_call_target="tpu_custom_call" | custom-call | flops 3449999872 | bytes 1048576 | tf_op jit(solution)/shard_map/pallas_call | solution.py:113
  4.0 4.0 %collective-permute-start.5 = (bf16[144,256]{1,0:T(8,128)(2,1)}, bf16[144,256]{1,0:T(8,128)(2,1)S(1)}, u32[]{:S(2)}, u32[]{:S(2)}) collective-permute-start(bf16[144,256]{1,0:T(8,128)(2,1)} %get-tuple-element.66.refs_15_.refs_24_), channel_id=1, source_target_pairs={{0,24},{4,28},{8,16},{12,20},{16,8},{20,12},{24,0},{28,4},{1,25},{... | collective-permute-start | bytes 221192 | tf_op jit(solution)/shard_map/ppermute | solution.py:649
  8.7 2.8 %collective-permute-start.2 = (bf16[256,384]{1,0:T(8,128)(2,1)}, bf16[256,384]{1,0:T(8,128)(2,1)S(1)}, u32[]{:S(2)}, u32[]{:S(2)}) collective-permute-start(bf16[256,384]{1,0:T(8,128)(2,1)} %get-tuple-element.67.refs_0_.refs_19_), channel_id=1, source_target_pairs={{0,24},{4,28},{8,16},{12,20},{16,8},{20,12},{24,0},{28,4},{1,25},{... | collective-permute-start | bytes 589832 | tf_op jit(solution)/shard_map/ppermute | solution.py:649
  13.0 4.0 %shard_map.231.refs_6_.refs_11_ = bf16[3,768,128]{2,1,0:T(8,128)(2,1)} custom-call(bf16[576,256]{1,0:T(8,128)(2,1)} %get-tuple-element.64.refs_0_, bf16[576,576]{1,0:T(8,128)(2,1)} %refs_8_.5, f32[64,256]{1,0:T(8,128)} %get-tuple-element.65.refs_2_.refs_12_), custom_call_target="tpu_custom_call" | custom-call | flops 3449999872 | bytes 1048576 | tf_op jit(solution)/shard_map/pallas_call | solution.py:113
  17.1 2.0 %collective-permute-done.2.refs_3_.refs_22_ = bf16[256,384]{1,0:T(8,128)(2,1)S(1)} collective-permute-done((bf16[256,384]{1,0:T(8,128)(2,1)}, bf16[256,384]{1,0:T(8,128)(2,1)S(1)}, u32[]{:S(2)}, u32[]{:S(2)}) %collective-permute-start.2) | collective-permute-done | bytes 196640 | tf_op jit(solution)/shard_map/ppermute | solution.py:649
  19.2 1.8 %collective-permute-done.1.refs_2_.refs_21_ = bf16[256,384]{1,0:T(8,128)(2,1)S(1)} collective-permute-done((bf16[256,384]{1,0:T(8,128)(2,1)}, bf16[256,384]{1,0:T(8,128)(2,1)S(1)}, u32[]{:S(2)}, u32[]{:S(2)}) %collective-permute-start.1) | collective-permute-done | bytes 196640 | tf_op jit(solution)/shard_map/ppermute | solution.py:649
  21.3 2.3 %collective-permute-done.6.refs_4_.refs_23_ = bf16[4,256,384]{2,1,0:T(8,128)(2,1)S(1)} collective-permute-done((bf16[4,256,384]{2,1,0:T(8,128)(2,1)S(1)}, bf16[4,256,384]{2,1,0:T(8,128)(2,1)S(1)}, u32[]{:S(2)}, u32[]{:S(2)}) %collective-permute-start.6) | collective-permute-done | bytes 786464 | tf_op jit(solution)/shard_map/ppermute | solution.py:649
  24.5 14.8 %shard_map.232 = (f32[576,256]{1,0:T(8,128)}, f32[6,1,384]{2,1,0:T(1,128)}, f32[256,640]{1,0:T(8,128)}, bf16[4,72,1152]{2,1,0:T(8,128)(2,1)}, bf16[4,72,1152]{2,...) custom-call(bf16[256,384]{1,0:T(8,128)(2,1)} %get-tuple-element.67.r, ...), custom_call_target="tpu_custom_call" | custom-call | flops 16099999744 | bytes 1048576 | tf_op jit(solution)/shard_map/pallas_call | solution.py:113
  39.9 1.6 %collective-permute-start.7 = (bf16[64,640]{1,0:T(8,128)(2,1)}, bf16[64,640]{1,0:T(8,128)(2,1)S(1)}, u32[]{:S(2)}, u32[]{:S(2)}) collective-permute-start(bf16[64,640]{1,0:T(8,128)(2,1)} %get-tuple-element.73), channel_id=1, source_target_pairs={{0,1},{1,0},{2,3},{3,2},{4,5},{5,4},{6,7},{7,6},{8,9},{9,8},{10,11... | collective-permute-start | bytes 245768 | tf_op jit(solution)/shard_map/ppermute | solution.py:649
  42.0 2.6 %collective-permute-start.15 = (bf16[64,640]{1,0:T(8,128)(2,1)}, bf16[64,640]{1,0:T(8,128)(2,1)S(1)}, u32[]{:S(2)}, u32[]{:S(2)}) collective-permute-start(bf16[64,640]{1,0:T(8,128)(2,1)} %get-tuple-element.80), channel_id=1, source_target_pairs={{0,2},{1,3},{2,0},{3,1},{4,6},{5,7},{6,4},{7,5},{8,10},{9,11},{10,... | collective-permute-start | bytes 245768 | tf_op jit(solution)/shard_map/ppermute | solution.py:649
  46.1 2.0 %collective-permute-done.14 = bf16[64,640]{1,0:T(8,128)(2,1)S(1)} collective-permute-done((bf16[64,640]{1,0:T(8,128)(2,1)}, bf16[64,640]{1,0:T(8,128)(2,1)S(1)}, u32[]{:S(2)}, u32[]{:S(2)}) %collective-permute-start.14) | collective-permute-done | bytes 81952 | tf_op jit(solution)/shard_map/ppermute | solution.py:649
  49.3 1.4 %collective-permute-start.23 = (bf16[72,1152]{1,0:T(8,128)(2,1)S(1)}, bf16[72,1152]{1,0:T(8,128)(2,1)S(1)}, u32[]{:S(2)}, u32[]{:S(2)}) collective-permute-start(bf16[72,1152]{1,0:T(8,128)(2,1)S(1)} %get-tuple-element.118), channel_id=1, source_target_pairs={{0,24},{4,28},{8,16},{12,20},{16,8},{20,12},{24,0},{28,4},{1,25},{... | collective-permute-start | bytes 497672 | tf_op jit(solution)/shard_map/ppermute | solution.py:649
  54.6 3.0 %collective-permute-start.19 = (bf16[64,640]{1,0:T(8,128)(2,1)S(1)}, bf16[64,640]{1,0:T(8,128)(2,1)S(1)}, u32[]{:S(2)}, u32[]{:S(2)}) collective-permute-start(bf16[64,640]{1,0:T(8,128)(2,1)S(1)} %add_convert_fusion.1.refs_0_), channel_id=1, source_target_pairs={{0,3},{1,2},{2,1},{3,0},{4,7},{5,6},{6,5},{7,4},{8,11},{9,10},{10,... | collective-permute-start | bytes 245768 | tf_op jit(solution)/shard_map/ppermute | solution.py:649
  59.6 2.2 %collective-permute-start.17 = (bf16[64,640]{1,0:T(8,128)(2,1)S(1)}, bf16[64,640]{1,0:T(8,128)(2,1)S(1)}, u32[]{:S(2)}, u32[]{:S(2)}) collective-permute-start(bf16[64,640]{1,0:T(8,128)(2,1)S(1)} %add_convert_fusion.1.refs_0_), channel_id=1, source_target_pairs={{0,1},{1,0},{2,3},{3,2},{4,5},{5,4},{6,7},{7,6},{8,9},{9,8},{10,11... | collective-permute-start | bytes 245768 | tf_op jit(solution)/shard_map/ppermute | solution.py:649
  62.0 2.4 %collective-permute-start.8 = (bf16[64,640]{1,0:T(8,128)(2,1)S(1)}, bf16[64,640]{1,0:T(8,128)(2,1)S(1)}, u32[]{:S(2)}, u32[]{:S(2)}) collective-permute-start(bf16[64,640]{1,0:T(8,128)(2,1)S(1)} %copy-done.24), channel_id=1, source_target_pairs={{0,2},{1,3},{2,0},{3,1},{4,6},{5,7},{6,4},{7,5},{8,10},{9,11},{10,... | collective-permute-start | bytes 245768 | tf_op jit(solution)/shard_map/ppermute | solution.py:649
  64.4 2.2 %collective-permute-start.9 = (bf16[64,640]{1,0:T(8,128)(2,1)S(1)}, bf16[64,640]{1,0:T(8,128)(2,1)S(1)}, u32[]{:S(2)}, u32[]{:S(2)}) collective-permute-start(bf16[64,640]{1,0:T(8,128)(2,1)S(1)} %copy-done.23), channel_id=1, source_target_pairs={{0,3},{1,2},{2,1},{3,0},{4,7},{5,6},{6,5},{7,4},{8,11},{9,10},{10,... | collective-permute-start | bytes 245768 | tf_op jit(solution)/shard_map/ppermute | solution.py:649
  66.6 1.4 %collective-permute-start.26 = (bf16[72,1152]{1,0:T(8,128)(2,1)S(1)}, bf16[72,1152]{1,0:T(8,128)(2,1)S(1)}, u32[]{:S(2)}, u32[]{:S(2)}) collective-permute-start(bf16[72,1152]{1,0:T(8,128)(2,1)S(1)} %add_convert_fusion), channel_id=1, source_target_pairs={{0,24},{4,28},{8,16},{12,20},{16,8},{20,12},{24,0},{28,4},{1,25},{... | collective-permute-start | bytes 497672 | tf_op jit(solution)/shard_map/ppermute | solution.py:649
  70.2 17.4 %shard_map.233 = (f32[64,640]{1,0:T(8,128)}, bf16[64,640]{1,0:T(8,128)(2,1)}, bf16[4,144,384]{2,1,0:T(8,128)(2,1)}, bf16[4,144,384]{2,1,0:T(8,128)(2,1)}) custom-call(bf16[64,640]{1,0:T(8,128)(2,1)} %copy-done.15, bf16[64,640]{1,0:T(8,128)(2,1)} %copy-done.27, bf16[64,640]{1,0:T(8,128)(2,1)} %copy-done.26, bf16[64,640]{1,0:T(8,128)(2,1)} %copy-done.25, ...), custom_call_target="tpu_custom_call" | custom-call | flops 19549999104 | bytes 1048576 | tf_op jit(solution)/shard_map/pallas_call | solution.py:113
  87.8 1.7 %collective-permute-start.12 = (bf16[64,640]{1,0:T(8,128)(2,1)S(1)}, bf16[64,640]{1,0:T(8,128)(2,1)S(1)}, u32[]{:S(2)}, u32[]{:S(2)}) collective-permute-start(bf16[64,640]{1,0:T(8,128)(2,1)S(1)} %add_convert_fusion.2.refs_4_), channel_id=1, source_target_pairs={{0,3},{1,2},{2,1},{3,0},{4,7},{5,6},{6,5},{7,4},{8,11},{9,10},{10,... | collective-permute-start | bytes 245768 | tf_op jit(solution)/shard_map/ppermute | solution.py:649
  89.5 2.7 %collective-permute-start.10 = (bf16[64,640]{1,0:T(8,128)(2,1)S(1)}, bf16[64,640]{1,0:T(8,128)(2,1)S(1)}, u32[]{:S(2)}, u32[]{:S(2)}) collective-permute-start(bf16[64,640]{1,0:T(8,128)(2,1)S(1)} %add_convert_fusion.2.refs_4_), channel_id=1, source_target_pairs={{0,1},{1,0},{2,3},{3,2},{4,5},{5,4},{6,7},{7,6},{8,9},{9,8},{10,11... | collective-permute-start | bytes 245768 | tf_op jit(solution)/shard_map/ppermute | solution.py:649
  92.5 1.5 %collective-permute-start.30 = (bf16[144,384]{1,0:T(8,128)(2,1)S(1)}, bf16[144,384]{1,0:T(8,128)(2,1)S(1)}, u32[]{:S(2)}, u32[]{:S(2)}) collective-permute-start(bf16[144,384]{1,0:T(8,128)(2,1)S(1)} %get-tuple-element.120), channel_id=1, source_target_pairs={{0,24},{4,28},{8,16},{12,20},{16,8},{20,12},{24,0},{28,4},{1,25},{... | collective-permute-start | bytes 331784 | tf_op jit(solution)/shard_map/ppermute | solution.py:649
  96.3 1.7 %collective-permute-done.11.refs_6_ = bf16[64,640]{1,0:T(8,128)(2,1)S(1)} collective-permute-done((bf16[64,640]{1,0:T(8,128)(2,1)S(1)}, bf16[64,640]{1,0:T(8,128)(2,1)S(1)}, u32[]{:S(2)}, u32[]{:S(2)}) %collective-permute-start.11) | collective-permute-done | bytes 81952 | tf_op jit(solution)/shard_map/ppermute | solution.py:649
  100.5 1.7 %collective-permute-start.36 = (bf16[80,384]{1,0:T(8,128)(2,1)S(1)}, bf16[80,384]{1,0:T(8,128)(2,1)S(1)}, u32[]{:S(2)}, u32[]{:S(2)}) collective-permute-start(bf16[80,384]{1,0:T(8,128)(2,1)S(1)} %add_convert_fusion.3), channel_id=1, source_target_pairs={{0,3},{1,2},{2,1},{3,0},{4,7},{5,6},{6,5},{7,4},{8,11},{9,10},{10,... | collective-permute-start | bytes 184328 | tf_op jit(solution)/shard_map/ppermute | solution.py:649
  102.3 2.6 %collective-permute-start.34 = (bf16[80,384]{1,0:T(8,128)(2,1)S(1)}, bf16[80,384]{1,0:T(8,128)(2,1)S(1)}, u32[]{:S(2)}, u32[]{:S(2)}) collective-permute-start(bf16[80,384]{1,0:T(8,128)(2,1)S(1)} %add_convert_fusion.3), channel_id=1, source_target_pairs={{0,1},{1,0},{2,3},{3,2},{4,5},{5,4},{6,7},{7,6},{8,9},{9,8},{10,11... | collective-permute-start | bytes 184328 | tf_op jit(solution)/shard_map/ppermute | solution.py:649
  105.0 2.0 %shard_map.234.refs_0_ = bf16[64,640]{1,0:T(8,128)(2,1)S(1)} custom-call(f32[144,384]{1,0:T(8,128)S(1)} %get-tuple-element.92.refs_0_, bf16[144,384]{1,0:T(8,128)(2,1)S(1)} %collective-permute-done.28.refs_1_, bf16[144,384]{1,0:T(8,128)(2,1)S(1)} %collective-permute-done.29.refs_2_, bf16[144,384]{1,0:T(8,128)(2,1)S(1)} %collective-permute-done.30.refs_3_, ...), custom_call_target="tpu_custom_call" | custom-call | flops 2300000000 | bytes 1048576 | tf_op jit(solution)/shard_map/pallas_call | solution.py:113
  107.3 1.5 %collective-permute-done.35 = bf16[80,384]{1,0:T(8,128)(2,1)S(1)} collective-permute-done((bf16[80,384]{1,0:T(8,128)(2,1)S(1)}, bf16[80,384]{1,0:T(8,128)(2,1)S(1)}, u32[]{:S(2)}, u32[]{:S(2)}) %collective-permute-start.35) | collective-permute-done | bytes 61472 | tf_op jit(solution)/shard_map/ppermute | solution.py:649
  108.8 1.5 %collective-permute-start.39 = (bf16[4,80,384]{2,1,0:T(8,128)(2,1)S(1)}, bf16[4,80,384]{2,1,0:T(8,128)(2,1)S(1)}, u32[]{:S(2)}, u32[]{:S(2)}) collective-permute-start(bf16[4,80,384]{2,1,0:T(8,128)(2,1)S(1)} %get-tuple-element.125.refs_1_), channel_id=1, source_target_pairs={{0,24},{4,28},{8,16},{12,20},{16,8},{20,12},{24,0},{28,4},{1,25},{... | collective-permute-start | bytes 737288 | tf_op jit(solution)/shard_map/ppermute | solution.py:649
  112.3 1.9 %collective-permute-start.33 = (bf16[64,640]{1,0:T(8,128)(2,1)S(1)}, bf16[64,640]{1,0:T(8,128)(2,1)S(1)}, u32[]{:S(2)}, u32[]{:S(2)}) collective-permute-start(bf16[64,640]{1,0:T(8,128)(2,1)S(1)} %shard_map.234.refs_0_), channel_id=1, source_target_pairs={{0,3},{1,2},{2,1},{3,0},{4,7},{5,6},{6,5},{7,4},{8,11},{9,10},{10,... | collective-permute-start | bytes 245768 | tf_op jit(solution)/shard_map/ppermute | solution.py:649
  114.2 1.7 %shard_map.236 = (f32[576,384]{1,0:T(8,128)}, f32[576,384]{1,0:T(8,128)}, f32[576,384]{1,0:T(8,128)}) custom-call(bf16[72,1152]{1,0:T(8,128)(2,1)S(1)} %add_convert_fusion, bf16[72,1152]{1,0:T(8,128)(2,1)S(1)} %collective-permute-done.24.refs_1_, bf16[72,1152]{1,0:T(8,128)(2,1)S(1)} %collective-permute-done.25.refs_2_, ...), custom_call_target="tpu_custom_call" | custom-call | flops 2300000000 | bytes 1048576 | tf_op jit(solution)/shard_map/pallas_call | solution.py:113
  116.0 2.7 %collective-permute-done.39.refs_4_ = bf16[4,80,384]{2,1,0:T(8,128)(2,1)S(1)} collective-permute-done((bf16[4,80,384]{2,1,0:T(8,128)(2,1)S(1)}, bf16[4,80,384]{2,1,0:T(8,128)(2,1)S(1)}, u32[]{:S(2)}, u32[]{:S(2)}) %collective-permute-start.39) | collective-permute-done | bytes 245792 | tf_op jit(solution)/shard_map/ppermute | solution.py:649
  119.1 3.7 %collective-permute-done.38.refs_3_ = bf16[4,80,384]{2,1,0:T(8,128)(2,1)S(1)} collective-permute-done((bf16[4,80,384]{2,1,0:T(8,128)(2,1)S(1)}, bf16[4,80,384]{2,1,0:T(8,128)(2,1)S(1)}, u32[]{:S(2)}, u32[]{:S(2)}) %collective-permute-start.38) | collective-permute-done | bytes 245792 | tf_op jit(solution)/shard_map/ppermute | solution.py:649
  125.6 2.9 %shard_map.237 = (f32[576,576]{1,0:T(8,128)}, f32[576,576]{1,0:T(8,128)}, f32[192,576]{1,0:T(8,128)}, f32[192,576]{1,0:T(8,128)}, f32[576]{0:T(1024)}, /*index=5*/f32[576]{0:T(1024)}) custom-call(bf16[576]{0:T(1024)(128)(2,1)S(1)} %copy-done.4, bf16[4,80,384]{2,1,0:T(8,128)(2,1)S(1)} %get-tuple-element.125.refs_1_, ...), custom_call_target="tpu_custom_call" | custom-call | flops 3449999872 | bytes 1048576 | tf_op jit(solution)/shard_map/pallas_call | solution.py:113
  (129 shorter events, 25.9 us)
Async XLA Ops:
  4.0 8.0 %collective-permute-start.5 = (bf16[144,256]{1,0:T(8,128)(2,1)}, bf16[144,256]{1,0:T(8,128)(2,1)S(1)}, u32[]{:S(2)}, u32[]{:S(2)}) collective-permute-start(bf16[144,256]{1,0:T(8,128)(2,1)} %get-tuple-element.66.refs_15_.refs_24_), channel_id=1, source_target_pairs={{0,24},{4,28},{8,16},{12,20},{16,8},{20,12},{24,0},{28,4},{1,25},{... | collective-permute-start | bytes 221192 | tf_op jit(solution)/shard_map/ppermute | solution.py:649
  8.0 9.1 %collective-permute-start.4 = (bf16[144,256]{1,0:T(8,128)(2,1)}, bf16[144,256]{1,0:T(8,128)(2,1)S(1)}, u32[]{:S(2)}, u32[]{:S(2)}) collective-permute-start(bf16[144,256]{1,0:T(8,128)(2,1)} %get-tuple-element.66.refs_15_.refs_24_), channel_id=1, source_target_pairs={{0,16},{4,20},{8,24},{12,28},{16,0},{20,4},{24,8},{28,12},{1,17},{... | collective-permute-start | bytes 221192 | tf_op jit(solution)/shard_map/ppermute | solution.py:649
  8.5 8.6 %collective-permute-start.3 = (bf16[144,256]{1,0:T(8,128)(2,1)}, bf16[144,256]{1,0:T(8,128)(2,1)S(1)}, u32[]{:S(2)}, u32[]{:S(2)}) collective-permute-start(bf16[144,256]{1,0:T(8,128)(2,1)} %get-tuple-element.66.refs_15_.refs_24_), channel_id=1, source_target_pairs={{0,8},{4,12},{8,0},{12,4},{16,24},{20,28},{24,16},{28,20},{1,9},{5... | collective-permute-start | bytes 221192 | tf_op jit(solution)/shard_map/ppermute | solution.py:649
  8.7 10.5 %collective-permute-start.2 = (bf16[256,384]{1,0:T(8,128)(2,1)}, bf16[256,384]{1,0:T(8,128)(2,1)S(1)}, u32[]{:S(2)}, u32[]{:S(2)}) collective-permute-start(bf16[256,384]{1,0:T(8,128)(2,1)} %get-tuple-element.67.refs_0_.refs_19_), channel_id=1, source_target_pairs={{0,24},{4,28},{8,16},{12,20},{16,8},{20,12},{24,0},{28,4},{1,25},{... | collective-permute-start | bytes 589832 | tf_op jit(solution)/shard_map/ppermute | solution.py:649
  11.5 9.5 %collective-permute-start.1 = (bf16[256,384]{1,0:T(8,128)(2,1)}, bf16[256,384]{1,0:T(8,128)(2,1)S(1)}, u32[]{:S(2)}, u32[]{:S(2)}) collective-permute-start(bf16[256,384]{1,0:T(8,128)(2,1)} %get-tuple-element.67.refs_0_.refs_19_), channel_id=1, source_target_pairs={{0,16},{4,20},{8,24},{12,28},{16,0},{20,4},{24,8},{28,12},{1,17},{... | collective-permute-start | bytes 589832 | tf_op jit(solution)/shard_map/ppermute | solution.py:649
  12.0 9.1 %collective-permute-start = (bf16[256,384]{1,0:T(8,128)(2,1)}, bf16[256,384]{1,0:T(8,128)(2,1)S(1)}, u32[]{:S(2)}, u32[]{:S(2)}) collective-permute-start(bf16[256,384]{1,0:T(8,128)(2,1)} %get-tuple-element.67.refs_0_.refs_19_), channel_id=1, source_target_pairs={{0,8},{4,12},{8,0},{12,4},{16,24},{20,28},{24,16},{28,20},{1,9},{5... | collective-permute-start | bytes 589832 | tf_op jit(solution)/shard_map/ppermute | solution.py:649
  39.5 28.6 %collective-permute-start.20 = (bf16[4,144,256]{2,1,0:T(8,128)(2,1)S(1)}, bf16[4,144,256]{2,1,0:T(8,128)(2,1)S(1)}, u32[]{:S(2)}, u32[]{:S(2)}) collective-permute-start(bf16[4,144,256]{2,1,0:T(8,128)(2,1)S(1)} %pad_maximum_fusion.3), channel_id=1, source_target_pairs={{0,4},{4,0},{8,12},{12,8},{16,20},{20,16},{24,28},{28,24},{1,5},{5... | collective-permute-start | bytes 884744 | tf_op jit(solution)/shard_map/ppermute | solution.py:649
  39.9 29.3 %collective-permute-start.7 = (bf16[64,640]{1,0:T(8,128)(2,1)}, bf16[64,640]{1,0:T(8,128)(2,1)S(1)}, u32[]{:S(2)}, u32[]{:S(2)}) collective-permute-start(bf16[64,640]{1,0:T(8,128)(2,1)} %get-tuple-element.73), channel_id=1, source_target_pairs={{0,1},{1,0},{2,3},{3,2},{4,5},{5,4},{6,7},{7,6},{8,9},{9,8},{10,11... | collective-permute-start | bytes 245768 | tf_op jit(solution)/shard_map/ppermute | solution.py:649
  41.5 6.6 %collective-permute-start.14 = (bf16[64,640]{1,0:T(8,128)(2,1)}, bf16[64,640]{1,0:T(8,128)(2,1)S(1)}, u32[]{:S(2)}, u32[]{:S(2)}) collective-permute-start(bf16[64,640]{1,0:T(8,128)(2,1)} %get-tuple-element.79), channel_id=1, source_target_pairs={{0,1},{1,0},{2,3},{3,2},{4,5},{5,4},{6,7},{7,6},{8,9},{9,8},{10,11... | collective-permute-start | bytes 245768 | tf_op jit(solution)/shard_map/ppermute | solution.py:649
  42.0 7.3 %collective-permute-start.15 = (bf16[64,640]{1,0:T(8,128)(2,1)}, bf16[64,640]{1,0:T(8,128)(2,1)S(1)}, u32[]{:S(2)}, u32[]{:S(2)}) collective-permute-start(bf16[64,640]{1,0:T(8,128)(2,1)} %get-tuple-element.80), channel_id=1, source_target_pairs={{0,2},{1,3},{2,0},{3,1},{4,6},{5,7},{6,4},{7,5},{8,10},{9,11},{10,... | collective-permute-start | bytes 245768 | tf_op jit(solution)/shard_map/ppermute | solution.py:649
  44.6 7.5 %collective-permute-start.16 = (bf16[64,640]{1,0:T(8,128)(2,1)}, bf16[64,640]{1,0:T(8,128)(2,1)S(1)}, u32[]{:S(2)}, u32[]{:S(2)}) collective-permute-start(bf16[64,640]{1,0:T(8,128)(2,1)} %get-tuple-element.81), channel_id=1, source_target_pairs={{0,3},{1,2},{2,1},{3,0},{4,7},{5,6},{6,5},{7,4},{8,11},{9,10},{10,... | collective-permute-start | bytes 245768 | tf_op jit(solution)/shard_map/ppermute | solution.py:649
  49.3 8.4 %collective-permute-start.23 = (bf16[72,1152]{1,0:T(8,128)(2,1)S(1)}, bf16[72,1152]{1,0:T(8,128)(2,1)S(1)}, u32[]{:S(2)}, u32[]{:S(2)}) collective-permute-start(bf16[72,1152]{1,0:T(8,128)(2,1)S(1)} %get-tuple-element.118), channel_id=1, source_target_pairs={{0,24},{4,28},{8,16},{12,20},{16,8},{20,12},{24,0},{28,4},{1,25},{... | collective-permute-start | bytes 497672 | tf_op jit(solution)/shard_map/ppermute | solution.py:649
  52.0 7.6 %collective-permute-start.22 = (bf16[72,1152]{1,0:T(8,128)(2,1)S(1)}, bf16[72,1152]{1,0:T(8,128)(2,1)S(1)}, u32[]{:S(2)}, u32[]{:S(2)}) collective-permute-start(bf16[72,1152]{1,0:T(8,128)(2,1)S(1)} %get-tuple-element.119), channel_id=1, source_target_pairs={{0,16},{4,20},{8,24},{12,28},{16,0},{20,4},{24,8},{28,12},{1,17},{... | collective-permute-start | bytes 497672 | tf_op jit(solution)/shard_map/ppermute | solution.py:649
  54.6 7.3 %collective-permute-start.19 = (bf16[64,640]{1,0:T(8,128)(2,1)S(1)}, bf16[64,640]{1,0:T(8,128)(2,1)S(1)}, u32[]{:S(2)}, u32[]{:S(2)}) collective-permute-start(bf16[64,640]{1,0:T(8,128)(2,1)S(1)} %add_convert_fusion.1.refs_0_), channel_id=1, source_target_pairs={{0,3},{1,2},{2,1},{3,0},{4,7},{5,6},{6,5},{7,4},{8,11},{9,10},{10,... | collective-permute-start | bytes 245768 | tf_op jit(solution)/shard_map/ppermute | solution.py:649
  57.7 6.7 %collective-permute-start.18 = (bf16[64,640]{1,0:T(8,128)(2,1)S(1)}, bf16[64,640]{1,0:T(8,128)(2,1)S(1)}, u32[]{:S(2)}, u32[]{:S(2)}) collective-permute-start(bf16[64,640]{1,0:T(8,128)(2,1)S(1)} %add_convert_fusion.1.refs_0_), channel_id=1, source_target_pairs={{0,2},{1,3},{2,0},{3,1},{4,6},{5,7},{6,4},{7,5},{8,10},{9,11},{10,... | collective-permute-start | bytes 245768 | tf_op jit(solution)/shard_map/ppermute | solution.py:649
  59.6 7.0 %collective-permute-start.17 = (bf16[64,640]{1,0:T(8,128)(2,1)S(1)}, bf16[64,640]{1,0:T(8,128)(2,1)S(1)}, u32[]{:S(2)}, u32[]{:S(2)}) collective-permute-start(bf16[64,640]{1,0:T(8,128)(2,1)S(1)} %add_convert_fusion.1.refs_0_), channel_id=1, source_target_pairs={{0,1},{1,0},{2,3},{3,2},{4,5},{5,4},{6,7},{7,6},{8,9},{9,8},{10,11... | collective-permute-start | bytes 245768 | tf_op jit(solution)/shard_map/ppermute | solution.py:649
  62.0 25.6 %collective-permute-start.8 = (bf16[64,640]{1,0:T(8,128)(2,1)S(1)}, bf16[64,640]{1,0:T(8,128)(2,1)S(1)}, u32[]{:S(2)}, u32[]{:S(2)}) collective-permute-start(bf16[64,640]{1,0:T(8,128)(2,1)S(1)} %copy-done.24), channel_id=1, source_target_pairs={{0,2},{1,3},{2,0},{3,1},{4,6},{5,7},{6,4},{7,5},{8,10},{9,11},{10,... | collective-permute-start | bytes 245768 | tf_op jit(solution)/shard_map/ppermute | solution.py:649
  64.4 23.2 %collective-permute-start.9 = (bf16[64,640]{1,0:T(8,128)(2,1)S(1)}, bf16[64,640]{1,0:T(8,128)(2,1)S(1)}, u32[]{:S(2)}, u32[]{:S(2)}) collective-permute-start(bf16[64,640]{1,0:T(8,128)(2,1)S(1)} %copy-done.23), channel_id=1, source_target_pairs={{0,3},{1,2},{2,1},{3,0},{4,7},{5,6},{6,5},{7,4},{8,11},{9,10},{10,... | collective-permute-start | bytes 245768 | tf_op jit(solution)/shard_map/ppermute | solution.py:649
  66.6 21.0 %collective-permute-start.26 = (bf16[72,1152]{1,0:T(8,128)(2,1)S(1)}, bf16[72,1152]{1,0:T(8,128)(2,1)S(1)}, u32[]{:S(2)}, u32[]{:S(2)}) collective-permute-start(bf16[72,1152]{1,0:T(8,128)(2,1)S(1)} %add_convert_fusion), channel_id=1, source_target_pairs={{0,24},{4,28},{8,16},{12,20},{16,8},{20,12},{24,0},{28,4},{1,25},{... | collective-permute-start | bytes 497672 | tf_op jit(solution)/shard_map/ppermute | solution.py:649
  68.1 19.6 %collective-permute-start.25 = (bf16[72,1152]{1,0:T(8,128)(2,1)S(1)}, bf16[72,1152]{1,0:T(8,128)(2,1)S(1)}, u32[]{:S(2)}, u32[]{:S(2)}) collective-permute-start(bf16[72,1152]{1,0:T(8,128)(2,1)S(1)} %add_convert_fusion), channel_id=1, source_target_pairs={{0,16},{4,20},{8,24},{12,28},{16,0},{20,4},{24,8},{28,12},{1,17},{... | collective-permute-start | bytes 497672 | tf_op jit(solution)/shard_map/ppermute | solution.py:649
  69.2 18.4 %collective-permute-start.24 = (bf16[72,1152]{1,0:T(8,128)(2,1)S(1)}, bf16[72,1152]{1,0:T(8,128)(2,1)S(1)}, u32[]{:S(2)}, u32[]{:S(2)}) collective-permute-start(bf16[72,1152]{1,0:T(8,128)(2,1)S(1)} %add_convert_fusion), channel_id=1, source_target_pairs={{0,8},{4,12},{8,0},{12,4},{16,24},{20,28},{24,16},{28,20},{1,9},{5... | collective-permute-start | bytes 497672 | tf_op jit(solution)/shard_map/ppermute | solution.py:649
  87.8 7.4 %collective-permute-start.12 = (bf16[64,640]{1,0:T(8,128)(2,1)S(1)}, bf16[64,640]{1,0:T(8,128)(2,1)S(1)}, u32[]{:S(2)}, u32[]{:S(2)}) collective-permute-start(bf16[64,640]{1,0:T(8,128)(2,1)S(1)} %add_convert_fusion.2.refs_4_), channel_id=1, source_target_pairs={{0,3},{1,2},{2,1},{3,0},{4,7},{5,6},{6,5},{7,4},{8,11},{9,10},{10,... | collective-permute-start | bytes 245768 | tf_op jit(solution)/shard_map/ppermute | solution.py:649
  89.5 8.5 %collective-permute-start.11 = (bf16[64,640]{1,0:T(8,128)(2,1)S(1)}, bf16[64,640]{1,0:T(8,128)(2,1)S(1)}, u32[]{:S(2)}, u32[]{:S(2)}) collective-permute-start(bf16[64,640]{1,0:T(8,128)(2,1)S(1)} %add_convert_fusion.2.refs_4_), channel_id=1, source_target_pairs={{0,2},{1,3},{2,0},{3,1},{4,6},{5,7},{6,4},{7,5},{8,10},{9,11},{10,... | collective-permute-start | bytes 245768 | tf_op jit(solution)/shard_map/ppermute | solution.py:649
  89.5 8.5 %collective-permute-start.10 = (bf16[64,640]{1,0:T(8,128)(2,1)S(1)}, bf16[64,640]{1,0:T(8,128)(2,1)S(1)}, u32[]{:S(2)}, u32[]{:S(2)}) collective-permute-start(bf16[64,640]{1,0:T(8,128)(2,1)S(1)} %add_convert_fusion.2.refs_4_), channel_id=1, source_target_pairs={{0,1},{1,0},{2,3},{3,2},{4,5},{5,4},{6,7},{7,6},{8,9},{9,8},{10,11... | collective-permute-start | bytes 245768 | tf_op jit(solution)/shard_map/ppermute | solution.py:649
  92.5 6.6 %collective-permute-start.30 = (bf16[144,384]{1,0:T(8,128)(2,1)S(1)}, bf16[144,384]{1,0:T(8,128)(2,1)S(1)}, u32[]{:S(2)}, u32[]{:S(2)}) collective-permute-start(bf16[144,384]{1,0:T(8,128)(2,1)S(1)} %get-tuple-element.120), channel_id=1, source_target_pairs={{0,24},{4,28},{8,16},{12,20},{16,8},{20,12},{24,0},{28,4},{1,25},{... | collective-permute-start | bytes 331784 | tf_op jit(solution)/shard_map/ppermute | solution.py:649
  98.0 16.2 %collective-permute-start.40 = (bf16[4,72,1152]{2,1,0:T(8,128)(2,1)S(1)}, bf16[4,72,1152]{2,1,0:T(8,128)(2,1)S(1)}, u32[]{:S(2)}, u32[]{:S(2)}) collective-permute-start(bf16[4,72,1152]{2,1,0:T(8,128)(2,1)S(1)} %pad_maximum_fusion.2), channel_id=1, source_target_pairs={{0,4},{4,0},{8,12},{12,8},{16,20},{20,16},{24,28},{28,24},{1,5},{5... | collective-permute-start | bytes 1990664 | tf_op jit(solution)/shard_map/ppermute | solution.py:649
  100.5 6.8 %collective-permute-start.36 = (bf16[80,384]{1,0:T(8,128)(2,1)S(1)}, bf16[80,384]{1,0:T(8,128)(2,1)S(1)}, u32[]{:S(2)}, u32[]{:S(2)}) collective-permute-start(bf16[80,384]{1,0:T(8,128)(2,1)S(1)} %add_convert_fusion.3), channel_id=1, source_target_pairs={{0,3},{1,2},{2,1},{3,0},{4,7},{5,6},{6,5},{7,4},{8,11},{9,10},{10,... | collective-permute-start | bytes 184328 | tf_op jit(solution)/shard_map/ppermute | solution.py:649
  108.8 9.8 %collective-permute-start.39 = (bf16[4,80,384]{2,1,0:T(8,128)(2,1)S(1)}, bf16[4,80,384]{2,1,0:T(8,128)(2,1)S(1)}, u32[]{:S(2)}, u32[]{:S(2)}) collective-permute-start(bf16[4,80,384]{2,1,0:T(8,128)(2,1)S(1)} %get-tuple-element.125.refs_1_), channel_id=1, source_target_pairs={{0,24},{4,28},{8,16},{12,20},{16,8},{20,12},{24,0},{28,4},{1,25},{... | collective-permute-start | bytes 737288 | tf_op jit(solution)/shard_map/ppermute | solution.py:649
  110.3 12.5 %collective-permute-start.38 = (bf16[4,80,384]{2,1,0:T(8,128)(2,1)S(1)}, bf16[4,80,384]{2,1,0:T(8,128)(2,1)S(1)}, u32[]{:S(2)}, u32[]{:S(2)}) collective-permute-start(bf16[4,80,384]{2,1,0:T(8,128)(2,1)S(1)} %get-tuple-element.125.refs_1_), channel_id=1, source_target_pairs={{0,16},{4,20},{8,24},{12,28},{16,0},{20,4},{24,8},{28,12},{1,17},{... | collective-permute-start | bytes 737288 | tf_op jit(solution)/shard_map/ppermute | solution.py:649
  111.3 11.5 %collective-permute-start.37 = (bf16[4,80,384]{2,1,0:T(8,128)(2,1)S(1)}, bf16[4,80,384]{2,1,0:T(8,128)(2,1)S(1)}, u32[]{:S(2)}, u32[]{:S(2)}) collective-permute-start(bf16[4,80,384]{2,1,0:T(8,128)(2,1)S(1)} %get-tuple-element.125.refs_1_), channel_id=1, source_target_pairs={{0,8},{4,12},{8,0},{12,4},{16,24},{20,28},{24,16},{28,20},{1,9},{5... | collective-permute-start | bytes 737288 | tf_op jit(solution)/shard_map/ppermute | solution.py:649
  112.3 10.6 %collective-permute-start.33 = (bf16[64,640]{1,0:T(8,128)(2,1)S(1)}, bf16[64,640]{1,0:T(8,128)(2,1)S(1)}, u32[]{:S(2)}, u32[]{:S(2)}) collective-permute-start(bf16[64,640]{1,0:T(8,128)(2,1)S(1)} %shard_map.234.refs_0_), channel_id=1, source_target_pairs={{0,3},{1,2},{2,1},{3,0},{4,7},{5,6},{6,5},{7,4},{8,11},{9,10},{10,... | collective-permute-start | bytes 245768 | tf_op jit(solution)/shard_map/ppermute | solution.py:649
  114.2 8.8 %collective-permute-start.32 = (bf16[64,640]{1,0:T(8,128)(2,1)S(1)}, bf16[64,640]{1,0:T(8,128)(2,1)S(1)}, u32[]{:S(2)}, u32[]{:S(2)}) collective-permute-start(bf16[64,640]{1,0:T(8,128)(2,1)S(1)} %shard_map.234.refs_0_), channel_id=1, source_target_pairs={{0,2},{1,3},{2,0},{3,1},{4,6},{5,7},{6,4},{7,5},{8,10},{9,11},{10,... | collective-permute-start | bytes 245768 | tf_op jit(solution)/shard_map/ppermute | solution.py:649
  (38 other events, 368.1 us)

commit v4 on v3

--- a/solution.py
+++ b/solution.py
@@ -104,11 +104,12 @@
         for item in given:
             if isinstance(item, Fetched):
                 item.get()
-        for item in results:
-            if isinstance(item, Stored):
-                if not item.sent:
-                    item.send()
-                item.copy.wait()
+        stored = [item for item in results if isinstance(item, Stored)]
+        for item in stored:
+            if not item.sent:
+                item.send()
+        for item in stored:
+            item.copy.wait()
 
     return pl.pallas_call(
         kernel,
@@ -729,15 +730,14 @@
     )
     evens = [kv] + [hop(kv, "ctx", n, k) for k in range(2, n, 2)]
     strips = [normed_q] + [hop(normed_q, "ctx", n, k) for k in range(2, n, 2)]
-    odds = hop(jnp.stack(after((q, strips), *evens)), "ctx", n, 1)
-    strip_odds = hop(jnp.stack(strips), "ctx", n, 1)
+    odds = hop(jnp.stack(after(q, *evens)), "ctx", n, 1)
 
     mlp_columns = 3 * hidden_width
     if small:
         block_shapes = [shape((n // 2, size, mlp_columns), BF)] * 2
     else:
         block_shapes = [shape((width, mlp_columns), BF), shape((8, 128), BF)]
-    att_t, lse, mixed, even, odd, mixed_q, *pieces = call(
+    results = call(
         functools.partial(forward_body, n, wt),
         [*evens, odds, None, stretch_order, q, tok, w_out, norm_mlp, w_gate, w_up, cot, w_down],
         "h" * (n // 2 + 1) + "msccc" + "c" + "cccc",
@@ -762,7 +762,9 @@
         early=functools.partial(forward_early, n),
         micros=14,
     )
+    att_t, lse, mixed, even, odd, mixed_q, *pieces = after(strips, *results)
     part_in, out_parts = pieces[:wt], pieces[wt:]
+    strip_odds = hop(jnp.stack(strips), "ctx", n, 1)
 
     terms = [part_in[0]] + [hop(part_in[k], "wt", wt, k) for k in range(1, wt)]
     quarter = summed(terms).astype(BF)

time: 129 us -> 126 us (0.977)
  waiting for transfers between devices: 25.4 us -> 23.6 us
    ppermute x42, waiting for transfers between devices: 25.4 us -> 23.6 us  [hop(): return lax.ppermute(x, axis, [(i, i ^ k) for i in range(size)])]
  transfers between devices with their start and end apart: 42 -> 42, of which waited for: 17 -> 16; matrix products, arithmetic and copies ran while one was open for 1% -> 1% of each run, Pallas kernels for 21% -> 32%
where the time goes in v4:
time: 126 us
  starting transfers between devices  52.2 us (41%)
  Pallas kernels  46.5 us (37%)
  waiting for transfers between devices  23.6 us (19%)
    ppermute x42, starting transfers between devices, hop(): return lax.ppermute(x, axis, [(i, i ^ k) for i in range(size)])  52.2 us
    pallas_call x8, Pallas kernels, call(): pl.pallas_call(kernel, out_shape=tuple(outs), in_specs=[SPEC[k] for _, k...  46.5 us
    ppermute x42, waiting for transfers between devices, hop(): return lax.ppermute(x, axis, [(i, i ^ k) for i in range(size)])  23.6 us
  transfers between devices with their start and end apart: 42, of which 16 were waited for; matrix products, arithmetic and copies ran while one was open for 1% of the time, Pallas kernels for 32%

profile of v4, /device:TPU:0, one launch (start us, length us, event | category | flops | bytes accessed | tf_op | source)
XLA Modules:
  0.0 125.5 jit_solution(4035901935486507469)
XLA Ops:
  0.6 3.4 %shard_map.230 = (bf16[576,256]{1,0:T(8,128)(2,1)}, bf16[256,384]{1,0:T(8,128)(2,1)}, f32[64,256]{1,0:T(8,128)}, bf16[144,256]{1,0:T(8,128)(2,1)}) custom-call(s32[1,16]{1,0:T(1,128)} %refs_4_.2, bf16[576]{0:T(1024)(128)(2,1)} %refs_0_.3, bf16[576,256]{1,0:T(8,128)(2,1)} %bitcast.55, bf16[192,576]{1,0:T(8,128)(2,1)} %bitcast.58, bf16[192,576]{1,0:T(8,128)(2,1)} %bitcast.61, ...), custom_call_target="tpu_custom_call" | custom-call | flops 3449999872 | bytes 1048576 | tf_op jit(solution)/shard_map/pallas_call | solution.py:114
  4.0 4.0 %collective-permute-start.5 = (bf16[256,384]{1,0:T(8,128)(2,1)}, bf16[256,384]{1,0:T(8,128)(2,1)S(1)}, u32[]{:S(2)}, u32[]{:S(2)}) collective-permute-start(bf16[256,384]{1,0:T(8,128)(2,1)} %get-tuple-element.81.refs_0_.refs_19_), channel_id=1, source_target_pairs={{0,24},{4,28},{8,16},{12,20},{16,8},{20,12},{24,0},{28,4},{1,25},{... | collective-permute-start | bytes 589832 | tf_op jit(solution)/shard_map/ppermute | solution.py:650
  8.7 4.0 %shard_map.231.refs_6_.refs_11_ = bf16[3,768,128]{2,1,0:T(8,128)(2,1)} custom-call(bf16[576,256]{1,0:T(8,128)(2,1)} %get-tuple-element.79.refs_0_, bf16[576,576]{1,0:T(8,128)(2,1)} %refs_8_.5, f32[64,256]{1,0:T(8,128)} %get-tuple-element.80.refs_2_.refs_12_), custom_call_target="tpu_custom_call" | custom-call | flops 3449999872 | bytes 1048576 | tf_op jit(solution)/shard_map/pallas_call | solution.py:114
  14.0 3.3 %collective-permute-done.4.refs_2_.refs_21_ = bf16[256,384]{1,0:T(8,128)(2,1)S(1)} collective-permute-done((bf16[256,384]{1,0:T(8,128)(2,1)}, bf16[256,384]{1,0:T(8,128)(2,1)S(1)}, u32[]{:S(2)}, u32[]{:S(2)}) %collective-permute-start.4) | collective-permute-done | bytes 196640 | tf_op jit(solution)/shard_map/ppermute | solution.py:650
  17.8 1.6 %collective-permute-start.2 = (bf16[144,256]{1,0:T(8,128)(2,1)S(1)}, bf16[144,256]{1,0:T(8,128)(2,1)S(1)}, u32[]{:S(2)}, u32[]{:S(2)}) collective-permute-start(bf16[144,256]{1,0:T(8,128)(2,1)S(1)} %copy-done.17), channel_id=1, source_target_pairs={{0,24},{4,28},{8,16},{12,20},{16,8},{20,12},{24,0},{28,4},{1,25},{... | collective-permute-start | bytes 221192 | tf_op jit(solution)/shard_map/ppermute | solution.py:650
  22.3 13.9 %shard_map.232 = (f32[576,256]{1,0:T(8,128)}, f32[6,1,384]{2,1,0:T(1,128)}, f32[256,640]{1,0:T(8,128)}, bf16[4,72,1152]{2,1,0:T(8,128)(2,1)}, bf16[4,72,1152]{2,...) custom-call(bf16[256,384]{1,0:T(8,128)(2,1)} %get-tuple-element.81.r, ...), custom_call_target="tpu_custom_call" | custom-call | flops 16099999744 | bytes 1048576 | tf_op jit(solution)/shard_map/pallas_call | solution.py:114
  36.9 1.6 %collective-permute-start.7 = (bf16[64,640]{1,0:T(8,128)(2,1)}, bf16[64,640]{1,0:T(8,128)(2,1)S(1)}, u32[]{:S(2)}, u32[]{:S(2)}) collective-permute-start(bf16[64,640]{1,0:T(8,128)(2,1)} %get-tuple-element.101), channel_id=1, source_target_pairs={{0,1},{1,0},{2,3},{3,2},{4,5},{5,4},{6,7},{7,6},{8,9},{9,8},{10,11... | collective-permute-start | bytes 245768 | tf_op jit(solution)/shard_map/ppermute | solution.py:650
  39.0 2.6 %collective-permute-start.15 = (bf16[64,640]{1,0:T(8,128)(2,1)}, bf16[64,640]{1,0:T(8,128)(2,1)S(1)}, u32[]{:S(2)}, u32[]{:S(2)}) collective-permute-start(bf16[64,640]{1,0:T(8,128)(2,1)} %get-tuple-element.108), channel_id=1, source_target_pairs={{0,2},{1,3},{2,0},{3,1},{4,6},{5,7},{6,4},{7,5},{8,10},{9,11},{10,... | collective-permute-start | bytes 245768 | tf_op jit(solution)/shard_map/ppermute | solution.py:650
  43.2 1.9 %collective-permute-done.14 = bf16[64,640]{1,0:T(8,128)(2,1)S(1)} collective-permute-done((bf16[64,640]{1,0:T(8,128)(2,1)}, bf16[64,640]{1,0:T(8,128)(2,1)S(1)}, u32[]{:S(2)}, u32[]{:S(2)}) %collective-permute-start.14) | collective-permute-done | bytes 81952 | tf_op jit(solution)/shard_map/ppermute | solution.py:650
  45.1 1.5 %collective-permute-start.21 = (bf16[72,1152]{1,0:T(8,128)(2,1)S(1)}, bf16[72,1152]{1,0:T(8,128)(2,1)S(1)}, u32[]{:S(2)}, u32[]{:S(2)}) collective-permute-start(bf16[72,1152]{1,0:T(8,128)(2,1)S(1)} %get-tuple-element.145), channel_id=1, source_target_pairs={{0,8},{4,12},{8,0},{12,4},{16,24},{20,28},{24,16},{28,20},{1,9},{5... | collective-permute-start | bytes 497672 | tf_op jit(solution)/shard_map/ppermute | solution.py:650
  49.0 1.4 %collective-permute-start.22 = (bf16[72,1152]{1,0:T(8,128)(2,1)S(1)}, bf16[72,1152]{1,0:T(8,128)(2,1)S(1)}, u32[]{:S(2)}, u32[]{:S(2)}) collective-permute-start(bf16[72,1152]{1,0:T(8,128)(2,1)S(1)} %get-tuple-element.147), channel_id=1, source_target_pairs={{0,16},{4,20},{8,24},{12,28},{16,0},{20,4},{24,8},{28,12},{1,17},{... | collective-permute-start | bytes 497672 | tf_op jit(solution)/shard_map/ppermute | solution.py:650
  51.6 3.4 %collective-permute-start.19 = (bf16[64,640]{1,0:T(8,128)(2,1)S(1)}, bf16[64,640]{1,0:T(8,128)(2,1)S(1)}, u32[]{:S(2)}, u32[]{:S(2)}) collective-permute-start(bf16[64,640]{1,0:T(8,128)(2,1)S(1)} %add_convert_fusion.1.refs_0_), channel_id=1, source_target_pairs={{0,3},{1,2},{2,1},{3,0},{4,7},{5,6},{6,5},{7,4},{8,11},{9,10},{10,... | collective-permute-start | bytes 245768 | tf_op jit(solution)/shard_map/ppermute | solution.py:650
  56.6 2.1 %collective-permute-start.17 = (bf16[64,640]{1,0:T(8,128)(2,1)S(1)}, bf16[64,640]{1,0:T(8,128)(2,1)S(1)}, u32[]{:S(2)}, u32[]{:S(2)}) collective-permute-start(bf16[64,640]{1,0:T(8,128)(2,1)S(1)} %add_convert_fusion.1.refs_0_), channel_id=1, source_target_pairs={{0,1},{1,0},{2,3},{3,2},{4,5},{5,4},{6,7},{7,6},{8,9},{9,8},{10,11... | collective-permute-start | bytes 245768 | tf_op jit(solution)/shard_map/ppermute | solution.py:650
  58.9 1.7 %collective-permute-start.8 = (bf16[64,640]{1,0:T(8,128)(2,1)S(1)}, bf16[64,640]{1,0:T(8,128)(2,1)S(1)}, u32[]{:S(2)}, u32[]{:S(2)}) collective-permute-start(bf16[64,640]{1,0:T(8,128)(2,1)S(1)} %copy-done.24), channel_id=1, source_target_pairs={{0,2},{1,3},{2,0},{3,1},{4,6},{5,7},{6,4},{7,5},{8,10},{9,11},{10,... | collective-permute-start | bytes 245768 | tf_op jit(solution)/shard_map/ppermute | solution.py:650
  61.3 2.4 %collective-permute-start.9 = (bf16[64,640]{1,0:T(8,128)(2,1)S(1)}, bf16[64,640]{1,0:T(8,128)(2,1)S(1)}, u32[]{:S(2)}, u32[]{:S(2)}) collective-permute-start(bf16[64,640]{1,0:T(8,128)(2,1)S(1)} %copy-done.23), channel_id=1, source_target_pairs={{0,3},{1,2},{2,1},{3,0},{4,7},{5,6},{6,5},{7,4},{8,11},{9,10},{10,... | collective-permute-start | bytes 245768 | tf_op jit(solution)/shard_map/ppermute | solution.py:650
  63.7 1.6 %collective-permute-start.26 = (bf16[72,1152]{1,0:T(8,128)(2,1)S(1)}, bf16[72,1152]{1,0:T(8,128)(2,1)S(1)}, u32[]{:S(2)}, u32[]{:S(2)}) collective-permute-start(bf16[72,1152]{1,0:T(8,128)(2,1)S(1)} %add_convert_fusion), channel_id=1, source_target_pairs={{0,24},{4,28},{8,16},{12,20},{16,8},{20,12},{24,0},{28,4},{1,25},{... | collective-permute-start | bytes 497672 | tf_op jit(solution)/shard_map/ppermute | solution.py:650
  67.2 17.3 %shard_map.233 = (f32[64,640]{1,0:T(8,128)}, bf16[64,640]{1,0:T(8,128)(2,1)}, bf16[4,144,384]{2,1,0:T(8,128)(2,1)}, bf16[4,144,384]{2,1,0:T(8,128)(2,1)}) custom-call(bf16[64,640]{1,0:T(8,128)(2,1)} %copy-done.15, bf16[64,640]{1,0:T(8,128)(2,1)} %copy-done.27, bf16[64,640]{1,0:T(8,128)(2,1)} %copy-done.26, bf16[64,640]{1,0:T(8,128)(2,1)} %copy-done.25, ...), custom_call_target="tpu_custom_call" | custom-call | flops 19549999104 | bytes 1048576 | tf_op jit(solution)/shard_map/pallas_call | solution.py:114
  84.7 1.5 %collective-permute-start.12 = (bf16[64,640]{1,0:T(8,128)(2,1)S(1)}, bf16[64,640]{1,0:T(8,128)(2,1)S(1)}, u32[]{:S(2)}, u32[]{:S(2)}) collective-permute-start(bf16[64,640]{1,0:T(8,128)(2,1)S(1)} %add_convert_fusion.2.refs_4_), channel_id=1, source_target_pairs={{0,3},{1,2},{2,1},{3,0},{4,7},{5,6},{6,5},{7,4},{8,11},{9,10},{10,... | collective-permute-start | bytes 245768 | tf_op jit(solution)/shard_map/ppermute | solution.py:650
  86.5 2.7 %collective-permute-start.10 = (bf16[64,640]{1,0:T(8,128)(2,1)S(1)}, bf16[64,640]{1,0:T(8,128)(2,1)S(1)}, u32[]{:S(2)}, u32[]{:S(2)}) collective-permute-start(bf16[64,640]{1,0:T(8,128)(2,1)S(1)} %add_convert_fusion.2.refs_4_), channel_id=1, source_target_pairs={{0,1},{1,0},{2,3},{3,2},{4,5},{5,4},{6,7},{7,6},{8,9},{9,8},{10,11... | collective-permute-start | bytes 245768 | tf_op jit(solution)/shard_map/ppermute | solution.py:650
  89.4 1.6 %collective-permute-start.30 = (bf16[144,384]{1,0:T(8,128)(2,1)S(1)}, bf16[144,384]{1,0:T(8,128)(2,1)S(1)}, u32[]{:S(2)}, u32[]{:S(2)}) collective-permute-start(bf16[144,384]{1,0:T(8,128)(2,1)S(1)} %get-tuple-element.148), channel_id=1, source_target_pairs={{0,24},{4,28},{8,16},{12,20},{16,8},{20,12},{24,0},{28,4},{1,25},{... | collective-permute-start | bytes 331784 | tf_op jit(solution)/shard_map/ppermute | solution.py:650
  93.4 1.5 %collective-permute-done.11.refs_6_ = bf16[64,640]{1,0:T(8,128)(2,1)S(1)} collective-permute-done((bf16[64,640]{1,0:T(8,128)(2,1)S(1)}, bf16[64,640]{1,0:T(8,128)(2,1)S(1)}, u32[]{:S(2)}, u32[]{:S(2)}) %collective-permute-start.11) | collective-permute-done | bytes 81952 | tf_op jit(solution)/shard_map/ppermute | solution.py:650
  95.9 1.5 %collective-permute-done.29.refs_2_ = bf16[144,384]{1,0:T(8,128)(2,1)S(1)} collective-permute-done((bf16[144,384]{1,0:T(8,128)(2,1)S(1)}, bf16[144,384]{1,0:T(8,128)(2,1)S(1)}, u32[]{:S(2)}, u32[]{:S(2)}) %collective-permute-start.29) | collective-permute-done | bytes 110624 | tf_op jit(solution)/shard_map/ppermute | solution.py:650
  97.4 1.5 %collective-permute-start.36 = (bf16[80,384]{1,0:T(8,128)(2,1)S(1)}, bf16[80,384]{1,0:T(8,128)(2,1)S(1)}, u32[]{:S(2)}, u32[]{:S(2)}) collective-permute-start(bf16[80,384]{1,0:T(8,128)(2,1)S(1)} %add_convert_fusion.3), channel_id=1, source_target_pairs={{0,3},{1,2},{2,1},{3,0},{4,7},{5,6},{6,5},{7,4},{8,11},{9,10},{10,... | collective-permute-start | bytes 184328 | tf_op jit(solution)/shard_map/ppermute | solution.py:650
  99.2 2.7 %collective-permute-start.34 = (bf16[80,384]{1,0:T(8,128)(2,1)S(1)}, bf16[80,384]{1,0:T(8,128)(2,1)S(1)}, u32[]{:S(2)}, u32[]{:S(2)}) collective-permute-start(bf16[80,384]{1,0:T(8,128)(2,1)S(1)} %add_convert_fusion.3), channel_id=1, source_target_pairs={{0,1},{1,0},{2,3},{3,2},{4,5},{5,4},{6,7},{7,6},{8,9},{9,8},{10,11... | collective-permute-start | bytes 184328 | tf_op jit(solution)/shard_map/ppermute | solution.py:650
  101.9 2.0 %shard_map.234.refs_0_ = bf16[64,640]{1,0:T(8,128)(2,1)S(1)} custom-call(f32[144,384]{1,0:T(8,128)S(1)} %get-tuple-element.120.refs_0_, bf16[144,384]{1,0:T(8,128)(2,1)S(1)} %collective-permute-done.28.refs_1_, bf16[144,384]{1,0:T(8,128)(2,1)S(1)} %collective-permute-done.29.refs_2_, bf16[144,384]{1,0:T(8,128)(2,1)S(1)} %collective-permute-done.30.refs_3_, ...), custom_call_target="tpu_custom_call" | custom-call | flops 2300000000 | bytes 1048576 | tf_op jit(solution)/shard_map/pallas_call | solution.py:114
  104.2 1.5 %collective-permute-done.35 = bf16[80,384]{1,0:T(8,128)(2,1)S(1)} collective-permute-done((bf16[80,384]{1,0:T(8,128)(2,1)S(1)}, bf16[80,384]{1,0:T(8,128)(2,1)S(1)}, u32[]{:S(2)}, u32[]{:S(2)}) %collective-permute-start.35) | collective-permute-done | bytes 61472 | tf_op jit(solution)/shard_map/ppermute | solution.py:650
  105.7 1.7 %collective-permute-start.39 = (bf16[4,80,384]{2,1,0:T(8,128)(2,1)S(1)}, bf16[4,80,384]{2,1,0:T(8,128)(2,1)S(1)}, u32[]{:S(2)}, u32[]{:S(2)}) collective-permute-start(bf16[4,80,384]{2,1,0:T(8,128)(2,1)S(1)} %get-tuple-element.153.refs_1_), channel_id=1, source_target_pairs={{0,24},{4,28},{8,16},{12,20},{16,8},{20,12},{24,0},{28,4},{1,25},{... | collective-permute-start | bytes 737288 | tf_op jit(solution)/shard_map/ppermute | solution.py:650
  109.3 1.5 %collective-permute-start.33 = (bf16[64,640]{1,0:T(8,128)(2,1)S(1)}, bf16[64,640]{1,0:T(8,128)(2,1)S(1)}, u32[]{:S(2)}, u32[]{:S(2)}) collective-permute-start(bf16[64,640]{1,0:T(8,128)(2,1)S(1)} %shard_map.234.refs_0_), channel_id=1, source_target_pairs={{0,3},{1,2},{2,1},{3,0},{4,7},{5,6},{6,5},{7,4},{8,11},{9,10},{10,... | collective-permute-start | bytes 245768 | tf_op jit(solution)/shard_map/ppermute | solution.py:650
  111.2 1.7 %shard_map.236 = (f32[576,384]{1,0:T(8,128)}, f32[576,384]{1,0:T(8,128)}, f32[576,384]{1,0:T(8,128)}) custom-call(bf16[72,1152]{1,0:T(8,128)(2,1)S(1)} %add_convert_fusion, bf16[72,1152]{1,0:T(8,128)(2,1)S(1)} %collective-permute-done.24.refs_1_, bf16[72,1152]{1,0:T(8,128)(2,1)S(1)} %collective-permute-done.25.refs_2_, ...), custom_call_target="tpu_custom_call" | custom-call | flops 2300000000 | bytes 1048576 | tf_op jit(solution)/shard_map/pallas_call | solution.py:114
  112.9 2.6 %collective-permute-done.39.refs_4_ = bf16[4,80,384]{2,1,0:T(8,128)(2,1)S(1)} collective-permute-done((bf16[4,80,384]{2,1,0:T(8,128)(2,1)S(1)}, bf16[4,80,384]{2,1,0:T(8,128)(2,1)S(1)}, u32[]{:S(2)}, u32[]{:S(2)}) %collective-permute-start.39) | collective-permute-done | bytes 245792 | tf_op jit(solution)/shard_map/ppermute | solution.py:650
  116.0 3.8 %collective-permute-done.38.refs_3_ = bf16[4,80,384]{2,1,0:T(8,128)(2,1)S(1)} collective-permute-done((bf16[4,80,384]{2,1,0:T(8,128)(2,1)S(1)}, bf16[4,80,384]{2,1,0:T(8,128)(2,1)S(1)}, u32[]{:S(2)}, u32[]{:S(2)}) %collective-permute-start.38) | collective-permute-done | bytes 245792 | tf_op jit(solution)/shard_map/ppermute | solution.py:650
  122.7 2.9 %shard_map.237 = (f32[576,576]{1,0:T(8,128)}, f32[576,576]{1,0:T(8,128)}, f32[192,576]{1,0:T(8,128)}, f32[192,576]{1,0:T(8,128)}, f32[576]{0:T(1024)}, /*index=5*/f32[576]{0:T(1024)}) custom-call(bf16[576]{0:T(1024)(128)(2,1)S(1)} %copy-done.4, bf16[4,80,384]{2,1,0:T(8,128)(2,1)S(1)} %get-tuple-element.153.refs_1_, ...), custom_call_target="tpu_custom_call" | custom-call | flops 3449999872 | bytes 1048576 | tf_op jit(solution)/shard_map/pallas_call | solution.py:114
  (129 shorter events, 25.9 us)
Async XLA Ops:
  4.0 9.9 %collective-permute-start.5 = (bf16[256,384]{1,0:T(8,128)(2,1)}, bf16[256,384]{1,0:T(8,128)(2,1)S(1)}, u32[]{:S(2)}, u32[]{:S(2)}) collective-permute-start(bf16[256,384]{1,0:T(8,128)(2,1)} %get-tuple-element.81.refs_0_.refs_19_), channel_id=1, source_target_pairs={{0,24},{4,28},{8,16},{12,20},{16,8},{20,12},{24,0},{28,4},{1,25},{... | collective-permute-start | bytes 589832 | tf_op jit(solution)/shard_map/ppermute | solution.py:650
  8.0 9.3 %collective-permute-start.4 = (bf16[256,384]{1,0:T(8,128)(2,1)}, bf16[256,384]{1,0:T(8,128)(2,1)S(1)}, u32[]{:S(2)}, u32[]{:S(2)}) collective-permute-start(bf16[256,384]{1,0:T(8,128)(2,1)} %get-tuple-element.81.refs_0_.refs_19_), channel_id=1, source_target_pairs={{0,16},{4,20},{8,24},{12,28},{16,0},{20,4},{24,8},{28,12},{1,17},{... | collective-permute-start | bytes 589832 | tf_op jit(solution)/shard_map/ppermute | solution.py:650
  8.5 9.1 %collective-permute-start.3 = (bf16[256,384]{1,0:T(8,128)(2,1)}, bf16[256,384]{1,0:T(8,128)(2,1)S(1)}, u32[]{:S(2)}, u32[]{:S(2)}) collective-permute-start(bf16[256,384]{1,0:T(8,128)(2,1)} %get-tuple-element.81.refs_0_.refs_19_), channel_id=1, source_target_pairs={{0,8},{4,12},{8,0},{12,4},{16,24},{20,28},{24,16},{28,20},{1,9},{5... | collective-permute-start | bytes 589832 | tf_op jit(solution)/shard_map/ppermute | solution.py:650
  17.8 18.4 %collective-permute-start.2 = (bf16[144,256]{1,0:T(8,128)(2,1)S(1)}, bf16[144,256]{1,0:T(8,128)(2,1)S(1)}, u32[]{:S(2)}, u32[]{:S(2)}) collective-permute-start(bf16[144,256]{1,0:T(8,128)(2,1)S(1)} %copy-done.17), channel_id=1, source_target_pairs={{0,24},{4,28},{8,16},{12,20},{16,8},{20,12},{24,0},{28,4},{1,25},{... | collective-permute-start | bytes 221192 | tf_op jit(solution)/shard_map/ppermute | solution.py:650
  19.5 16.8 %collective-permute-start.1 = (bf16[144,256]{1,0:T(8,128)(2,1)S(1)}, bf16[144,256]{1,0:T(8,128)(2,1)S(1)}, u32[]{:S(2)}, u32[]{:S(2)}) collective-permute-start(bf16[144,256]{1,0:T(8,128)(2,1)S(1)} %copy-done.17), channel_id=1, source_target_pairs={{0,16},{4,20},{8,24},{12,28},{16,0},{20,4},{24,8},{28,12},{1,17},{... | collective-permute-start | bytes 221192 | tf_op jit(solution)/shard_map/ppermute | solution.py:650
  20.9 15.4 %collective-permute-start = (bf16[144,256]{1,0:T(8,128)(2,1)S(1)}, bf16[144,256]{1,0:T(8,128)(2,1)S(1)}, u32[]{:S(2)}, u32[]{:S(2)}) collective-permute-start(bf16[144,256]{1,0:T(8,128)(2,1)S(1)} %copy-done.17), channel_id=1, source_target_pairs={{0,8},{4,12},{8,0},{12,4},{16,24},{20,28},{24,16},{28,20},{1,9},{5... | collective-permute-start | bytes 221192 | tf_op jit(solution)/shard_map/ppermute | solution.py:650
  36.4 28.8 %collective-permute-start.20 = (bf16[4,144,256]{2,1,0:T(8,128)(2,1)S(1)}, bf16[4,144,256]{2,1,0:T(8,128)(2,1)S(1)}, u32[]{:S(2)}, u32[]{:S(2)}) collective-permute-start(bf16[4,144,256]{2,1,0:T(8,128)(2,1)S(1)} %pad_maximum_fusion.3), channel_id=1, source_target_pairs={{0,4},{4,0},{8,12},{12,8},{16,20},{20,16},{24,28},{28,24},{1,5},{5... | collective-permute-start | bytes 884744 | tf_op jit(solution)/shard_map/ppermute | solution.py:650
  36.9 29.6 %collective-permute-start.7 = (bf16[64,640]{1,0:T(8,128)(2,1)}, bf16[64,640]{1,0:T(8,128)(2,1)S(1)}, u32[]{:S(2)}, u32[]{:S(2)}) collective-permute-start(bf16[64,640]{1,0:T(8,128)(2,1)} %get-tuple-element.101), channel_id=1, source_target_pairs={{0,1},{1,0},{2,3},{3,2},{4,5},{5,4},{6,7},{7,6},{8,9},{9,8},{10,11... | collective-permute-start | bytes 245768 | tf_op jit(solution)/shard_map/ppermute | solution.py:650
  38.5 6.6 %collective-permute-start.14 = (bf16[64,640]{1,0:T(8,128)(2,1)}, bf16[64,640]{1,0:T(8,128)(2,1)S(1)}, u32[]{:S(2)}, u32[]{:S(2)}) collective-permute-start(bf16[64,640]{1,0:T(8,128)(2,1)} %get-tuple-element.107), channel_id=1, source_target_pairs={{0,1},{1,0},{2,3},{3,2},{4,5},{5,4},{6,7},{7,6},{8,9},{9,8},{10,11... | collective-permute-start | bytes 245768 | tf_op jit(solution)/shard_map/ppermute | solution.py:650
  39.0 7.6 %collective-permute-start.15 = (bf16[64,640]{1,0:T(8,128)(2,1)}, bf16[64,640]{1,0:T(8,128)(2,1)S(1)}, u32[]{:S(2)}, u32[]{:S(2)}) collective-permute-start(bf16[64,640]{1,0:T(8,128)(2,1)} %get-tuple-element.108), channel_id=1, source_target_pairs={{0,2},{1,3},{2,0},{3,1},{4,6},{5,7},{6,4},{7,5},{8,10},{9,11},{10,... | collective-permute-start | bytes 245768 | tf_op jit(solution)/shard_map/ppermute | solution.py:650
  41.6 7.4 %collective-permute-start.16 = (bf16[64,640]{1,0:T(8,128)(2,1)}, bf16[64,640]{1,0:T(8,128)(2,1)S(1)}, u32[]{:S(2)}, u32[]{:S(2)}) collective-permute-start(bf16[64,640]{1,0:T(8,128)(2,1)} %get-tuple-element.109), channel_id=1, source_target_pairs={{0,3},{1,2},{2,1},{3,0},{4,7},{5,6},{6,5},{7,4},{8,11},{9,10},{10,... | collective-permute-start | bytes 245768 | tf_op jit(solution)/shard_map/ppermute | solution.py:650
  46.6 8.4 %collective-permute-start.23 = (bf16[72,1152]{1,0:T(8,128)(2,1)S(1)}, bf16[72,1152]{1,0:T(8,128)(2,1)S(1)}, u32[]{:S(2)}, u32[]{:S(2)}) collective-permute-start(bf16[72,1152]{1,0:T(8,128)(2,1)S(1)} %get-tuple-element.146), channel_id=1, source_target_pairs={{0,24},{4,28},{8,16},{12,20},{16,8},{20,12},{24,0},{28,4},{1,25},{... | collective-permute-start | bytes 497672 | tf_op jit(solution)/shard_map/ppermute | solution.py:650
  49.0 7.6 %collective-permute-start.22 = (bf16[72,1152]{1,0:T(8,128)(2,1)S(1)}, bf16[72,1152]{1,0:T(8,128)(2,1)S(1)}, u32[]{:S(2)}, u32[]{:S(2)}) collective-permute-start(bf16[72,1152]{1,0:T(8,128)(2,1)S(1)} %get-tuple-element.147), channel_id=1, source_target_pairs={{0,16},{4,20},{8,24},{12,28},{16,0},{20,4},{24,8},{28,12},{1,17},{... | collective-permute-start | bytes 497672 | tf_op jit(solution)/shard_map/ppermute | solution.py:650
  51.6 7.4 %collective-permute-start.19 = (bf16[64,640]{1,0:T(8,128)(2,1)S(1)}, bf16[64,640]{1,0:T(8,128)(2,1)S(1)}, u32[]{:S(2)}, u32[]{:S(2)}) collective-permute-start(bf16[64,640]{1,0:T(8,128)(2,1)S(1)} %add_convert_fusion.1.refs_0_), channel_id=1, source_target_pairs={{0,3},{1,2},{2,1},{3,0},{4,7},{5,6},{6,5},{7,4},{8,11},{9,10},{10,... | collective-permute-start | bytes 245768 | tf_op jit(solution)/shard_map/ppermute | solution.py:650
  56.6 7.0 %collective-permute-start.17 = (bf16[64,640]{1,0:T(8,128)(2,1)S(1)}, bf16[64,640]{1,0:T(8,128)(2,1)S(1)}, u32[]{:S(2)}, u32[]{:S(2)}) collective-permute-start(bf16[64,640]{1,0:T(8,128)(2,1)S(1)} %add_convert_fusion.1.refs_0_), channel_id=1, source_target_pairs={{0,1},{1,0},{2,3},{3,2},{4,5},{5,4},{6,7},{7,6},{8,9},{9,8},{10,11... | collective-permute-start | bytes 245768 | tf_op jit(solution)/shard_map/ppermute | solution.py:650
  58.9 25.6 %collective-permute-start.8 = (bf16[64,640]{1,0:T(8,128)(2,1)S(1)}, bf16[64,640]{1,0:T(8,128)(2,1)S(1)}, u32[]{:S(2)}, u32[]{:S(2)}) collective-permute-start(bf16[64,640]{1,0:T(8,128)(2,1)S(1)} %copy-done.24), channel_id=1, source_target_pairs={{0,2},{1,3},{2,0},{3,1},{4,6},{5,7},{6,4},{7,5},{8,10},{9,11},{10,... | collective-permute-start | bytes 245768 | tf_op jit(solution)/shard_map/ppermute | solution.py:650
  61.3 23.2 %collective-permute-start.9 = (bf16[64,640]{1,0:T(8,128)(2,1)S(1)}, bf16[64,640]{1,0:T(8,128)(2,1)S(1)}, u32[]{:S(2)}, u32[]{:S(2)}) collective-permute-start(bf16[64,640]{1,0:T(8,128)(2,1)S(1)} %copy-done.23), channel_id=1, source_target_pairs={{0,3},{1,2},{2,1},{3,0},{4,7},{5,6},{6,5},{7,4},{8,11},{9,10},{10,... | collective-permute-start | bytes 245768 | tf_op jit(solution)/shard_map/ppermute | solution.py:650
  63.7 20.8 %collective-permute-start.26 = (bf16[72,1152]{1,0:T(8,128)(2,1)S(1)}, bf16[72,1152]{1,0:T(8,128)(2,1)S(1)}, u32[]{:S(2)}, u32[]{:S(2)}) collective-permute-start(bf16[72,1152]{1,0:T(8,128)(2,1)S(1)} %add_convert_fusion), channel_id=1, source_target_pairs={{0,24},{4,28},{8,16},{12,20},{16,8},{20,12},{24,0},{28,4},{1,25},{... | collective-permute-start | bytes 497672 | tf_op jit(solution)/shard_map/ppermute | solution.py:650
  65.2 19.3 %collective-permute-start.25 = (bf16[72,1152]{1,0:T(8,128)(2,1)S(1)}, bf16[72,1152]{1,0:T(8,128)(2,1)S(1)}, u32[]{:S(2)}, u32[]{:S(2)}) collective-permute-start(bf16[72,1152]{1,0:T(8,128)(2,1)S(1)} %add_convert_fusion), channel_id=1, source_target_pairs={{0,16},{4,20},{8,24},{12,28},{16,0},{20,4},{24,8},{28,12},{1,17},{... | collective-permute-start | bytes 497672 | tf_op jit(solution)/shard_map/ppermute | solution.py:650
  66.5 18.0 %collective-permute-start.24 = (bf16[72,1152]{1,0:T(8,128)(2,1)S(1)}, bf16[72,1152]{1,0:T(8,128)(2,1)S(1)}, u32[]{:S(2)}, u32[]{:S(2)}) collective-permute-start(bf16[72,1152]{1,0:T(8,128)(2,1)S(1)} %add_convert_fusion), channel_id=1, source_target_pairs={{0,8},{4,12},{8,0},{12,4},{16,24},{20,28},{24,16},{28,20},{1,9},{5... | collective-permute-start | bytes 497672 | tf_op jit(solution)/shard_map/ppermute | solution.py:650
  84.7 7.6 %collective-permute-start.12 = (bf16[64,640]{1,0:T(8,128)(2,1)S(1)}, bf16[64,640]{1,0:T(8,128)(2,1)S(1)}, u32[]{:S(2)}, u32[]{:S(2)}) collective-permute-start(bf16[64,640]{1,0:T(8,128)(2,1)S(1)} %add_convert_fusion.2.refs_4_), channel_id=1, source_target_pairs={{0,3},{1,2},{2,1},{3,0},{4,7},{5,6},{6,5},{7,4},{8,11},{9,10},{10,... | collective-permute-start | bytes 245768 | tf_op jit(solution)/shard_map/ppermute | solution.py:650
  86.2 8.7 %collective-permute-start.11 = (bf16[64,640]{1,0:T(8,128)(2,1)S(1)}, bf16[64,640]{1,0:T(8,128)(2,1)S(1)}, u32[]{:S(2)}, u32[]{:S(2)}) collective-permute-start(bf16[64,640]{1,0:T(8,128)(2,1)S(1)} %add_convert_fusion.2.refs_4_), channel_id=1, source_target_pairs={{0,2},{1,3},{2,0},{3,1},{4,6},{5,7},{6,4},{7,5},{8,10},{9,11},{10,... | collective-permute-start | bytes 245768 | tf_op jit(solution)/shard_map/ppermute | solution.py:650
  86.5 8.5 %collective-permute-start.10 = (bf16[64,640]{1,0:T(8,128)(2,1)S(1)}, bf16[64,640]{1,0:T(8,128)(2,1)S(1)}, u32[]{:S(2)}, u32[]{:S(2)}) collective-permute-start(bf16[64,640]{1,0:T(8,128)(2,1)S(1)} %add_convert_fusion.2.refs_4_), channel_id=1, source_target_pairs={{0,1},{1,0},{2,3},{3,2},{4,5},{5,4},{6,7},{7,6},{8,9},{9,8},{10,11... | collective-permute-start | bytes 245768 | tf_op jit(solution)/shard_map/ppermute | solution.py:650
  89.4 6.5 %collective-permute-start.30 = (bf16[144,384]{1,0:T(8,128)(2,1)S(1)}, bf16[144,384]{1,0:T(8,128)(2,1)S(1)}, u32[]{:S(2)}, u32[]{:S(2)}) collective-permute-start(bf16[144,384]{1,0:T(8,128)(2,1)S(1)} %get-tuple-element.148), channel_id=1, source_target_pairs={{0,24},{4,28},{8,16},{12,20},{16,8},{20,12},{24,0},{28,4},{1,25},{... | collective-permute-start | bytes 331784 | tf_op jit(solution)/shard_map/ppermute | solution.py:650
  94.9 15.9 %collective-permute-start.40 = (bf16[4,72,1152]{2,1,0:T(8,128)(2,1)S(1)}, bf16[4,72,1152]{2,1,0:T(8,128)(2,1)S(1)}, u32[]{:S(2)}, u32[]{:S(2)}) collective-permute-start(bf16[4,72,1152]{2,1,0:T(8,128)(2,1)S(1)} %pad_maximum_fusion.2), channel_id=1, source_target_pairs={{0,4},{4,0},{8,12},{12,8},{16,20},{20,16},{24,28},{28,24},{1,5},{5... | collective-permute-start | bytes 1990664 | tf_op jit(solution)/shard_map/ppermute | solution.py:650
  97.4 6.8 %collective-permute-start.36 = (bf16[80,384]{1,0:T(8,128)(2,1)S(1)}, bf16[80,384]{1,0:T(8,128)(2,1)S(1)}, u32[]{:S(2)}, u32[]{:S(2)}) collective-permute-start(bf16[80,384]{1,0:T(8,128)(2,1)S(1)} %add_convert_fusion.3), channel_id=1, source_target_pairs={{0,3},{1,2},{2,1},{3,0},{4,7},{5,6},{6,5},{7,4},{8,11},{9,10},{10,... | collective-permute-start | bytes 184328 | tf_op jit(solution)/shard_map/ppermute | solution.py:650
  98.9 6.7 %collective-permute-start.35 = (bf16[80,384]{1,0:T(8,128)(2,1)S(1)}, bf16[80,384]{1,0:T(8,128)(2,1)S(1)}, u32[]{:S(2)}, u32[]{:S(2)}) collective-permute-start(bf16[80,384]{1,0:T(8,128)(2,1)S(1)} %add_convert_fusion.3), channel_id=1, source_target_pairs={{0,2},{1,3},{2,0},{3,1},{4,6},{5,7},{6,4},{7,5},{8,10},{9,11},{10,... | collective-permute-start | bytes 184328 | tf_op jit(solution)/shard_map/ppermute | solution.py:650
  105.7 9.8 %collective-permute-start.39 = (bf16[4,80,384]{2,1,0:T(8,128)(2,1)S(1)}, bf16[4,80,384]{2,1,0:T(8,128)(2,1)S(1)}, u32[]{:S(2)}, u32[]{:S(2)}) collective-permute-start(bf16[4,80,384]{2,1,0:T(8,128)(2,1)S(1)} %get-tuple-element.153.refs_1_), channel_id=1, source_target_pairs={{0,24},{4,28},{8,16},{12,20},{16,8},{20,12},{24,0},{28,4},{1,25},{... | collective-permute-start | bytes 737288 | tf_op jit(solution)/shard_map/ppermute | solution.py:650
  107.4 12.4 %collective-permute-start.38 = (bf16[4,80,384]{2,1,0:T(8,128)(2,1)S(1)}, bf16[4,80,384]{2,1,0:T(8,128)(2,1)S(1)}, u32[]{:S(2)}, u32[]{:S(2)}) collective-permute-start(bf16[4,80,384]{2,1,0:T(8,128)(2,1)S(1)} %get-tuple-element.153.refs_1_), channel_id=1, source_target_pairs={{0,16},{4,20},{8,24},{12,28},{16,0},{20,4},{24,8},{28,12},{1,17},{... | collective-permute-start | bytes 737288 | tf_op jit(solution)/shard_map/ppermute | solution.py:650
  108.5 11.4 %collective-permute-start.37 = (bf16[4,80,384]{2,1,0:T(8,128)(2,1)S(1)}, bf16[4,80,384]{2,1,0:T(8,128)(2,1)S(1)}, u32[]{:S(2)}, u32[]{:S(2)}) collective-permute-start(bf16[4,80,384]{2,1,0:T(8,128)(2,1)S(1)} %get-tuple-element.153.refs_1_), channel_id=1, source_target_pairs={{0,8},{4,12},{8,0},{12,4},{16,24},{20,28},{24,16},{28,20},{1,9},{5... | collective-permute-start | bytes 737288 | tf_op jit(solution)/shard_map/ppermute | solution.py:650
  109.3 10.7 %collective-permute-start.33 = (bf16[64,640]{1,0:T(8,128)(2,1)S(1)}, bf16[64,640]{1,0:T(8,128)(2,1)S(1)}, u32[]{:S(2)}, u32[]{:S(2)}) collective-permute-start(bf16[64,640]{1,0:T(8,128)(2,1)S(1)} %shard_map.234.refs_0_), channel_id=1, source_target_pairs={{0,3},{1,2},{2,1},{3,0},{4,7},{5,6},{6,5},{7,4},{8,11},{9,10},{10,... | collective-permute-start | bytes 245768 | tf_op jit(solution)/shard_map/ppermute | solution.py:650
  110.8 9.2 %collective-permute-start.32 = (bf16[64,640]{1,0:T(8,128)(2,1)S(1)}, bf16[64,640]{1,0:T(8,128)(2,1)S(1)}, u32[]{:S(2)}, u32[]{:S(2)}) collective-permute-start(bf16[64,640]{1,0:T(8,128)(2,1)S(1)} %shard_map.234.refs_0_), channel_id=1, source_target_pairs={{0,2},{1,3},{2,0},{3,1},{4,6},{5,7},{6,4},{7,5},{8,10},{9,11},{10,... | collective-permute-start | bytes 245768 | tf_op jit(solution)/shard_map/ppermute | solution.py:650
  (38 other events, 331.0 us)

commit v5 on v4

--- a/solution.py
+++ b/solution.py
@@ -426,7 +426,7 @@
         delta = jnp.sum(prod[h * HEAD : (h + 1) * HEAD, :], axis=0, keepdims=True)
         do = jnp.concatenate([zero, ga[:, h * HEAD : (h + 1) * HEAD]], axis=1).astype(BF)
         for sel in range(2):
-            at = (sel * GROUP + hh) * stretch
+            at = (sel * 2 * GROUP + GROUP + hh) * stretch
             half = slice(sel * stretch, (sel + 1) * stretch)
             dl_s[2 * g + sel, :, hh * stretch : (hh + 1) * stretch] = delta[:, half]
             do_s[g, at : at + stretch, :] = do[half]
@@ -434,6 +434,9 @@
     mine = span(meta[1], strip)
     grads[:, width : 2 * width] = dot(att_t.get()[mine, :].astype(BF), branch)
     lse, q_ref, angle = lse.get(), q_in.get(), angle.get()
+    for g in range(KV_HEADS):
+        for sel in range(2):
+            do_s[g, 2 * sel * wide : (2 * sel + 1) * wide, :] = q_ref[g, sel * wide : (sel + 1) * wide, :]
     for copy in kv_copies:
         copy.wait()
     first, inner = first.get(), inner.get()
@@ -453,11 +456,11 @@
         def low_step(i):
             at = span(i, low_group * stretch)
             keys = kv[at, lanes]
-            q = q_ref[g, wide : 2 * wide, :]
-            do = do_s[g, wide : 2 * wide, :]
-            p = jnp.exp(dot_nt(keys, q) - lse[2 * g + 1])
-            ds = (p * (dot_nt(keys, do) - dl_s[2 * g + 1])).astype(BF)
-            dkv[at, :] = dot(ds, q) + dot(p.astype(BF), do)
+            both = do_s[g, 2 * wide :, :]
+            s = dot_nt(keys, both)
+            p = jnp.exp(s[:, :wide] - lse[2 * g + 1])
+            ds = (p * (s[:, wide:] - dl_s[2 * g + 1])).astype(BF)
+            dkv[at, :] = dot(jnp.concatenate([ds, p.astype(BF)], axis=1), both)
             dq_s[1] += dot_tn(keys, ds)
 
         loop(low_steps, low_step)
@@ -468,13 +471,13 @@
             low_key = jnp.where(is_low, u, u - low_chunks - 1 + n // chunk) * (chunk * stretch)
             at = pl.ds(pl.multiple_of(low_key, chunk * stretch), chunk * stretch)
             keys = kv[at, lanes]
-            q = q_ref[g, span(sel, wide), :]
-            do = do_s[g, span(sel, wide), :]
-            p = jnp.exp(dot_nt(keys, q) - lse[2 * g + sel])
+            both = do_s[g, span(sel, 2 * wide), :]
+            s = dot_nt(keys, both)
+            p = jnp.exp(s[:, :wide] - lse[2 * g + sel])
             ahead = low_key - jnp.where(is_low, c, 2 * n - 1 - c) * stretch
             p = jnp.where(key_ids + ahead <= query_ids, p, 0.0)
-            ds = (p * (dot_nt(keys, do) - dl_s[2 * g + sel])).astype(BF)
-            dkv[at, :] += dot(ds, q) + dot(p.astype(BF), do)
+            ds = (p * (s[:, wide:] - dl_s[2 * g + sel])).astype(BF)
+            dkv[at, :] += dot(jnp.concatenate([ds, p.astype(BF)], axis=1), both)
             dq_s[sel] += dot_tn(keys, ds)
 
         if n <= 8:
@@ -795,7 +798,7 @@
         "cc" + "v" * len(out_blocks),
         scratch=[
             pltpu.VMEM((rows, padded), F32),
-            pltpu.VMEM((KV_HEADS, 2 * wide, PAIR), BF),
+            pltpu.VMEM((KV_HEADS, 4 * wide, PAIR), BF),
             pltpu.VMEM((2 * KV_HEADS, 1, wide), F32),
             pltpu.VMEM((n * rows, PAIR), F32),
             pltpu.VMEM((2, PAIR, wide), F32),
@@ -812,6 +815,7 @@
         early_at=wt + 10,
         micros=17,
     )
+    out_parts = after(mlp_own, *out_parts) if small else out_parts
     out_terms = [out_parts[0]] + [hop(out_parts[k], "wt", wt, k) for k in range(1, wt)]
     out_q = (mixed_q + summed(out_terms)).astype(BF)
     out_qs = [out_q] + [hop(out_q, "wt", wt, k) for k in range(1, wt)]

time: 126 us -> 122 us (0.968)
  starting transfers between devices: 52.2 us -> 47.2 us
    ppermute x42, starting transfers between devices: 52.2 us -> 47.2 us  [hop(): return lax.ppermute(x, axis, [(i, i ^ k) for i in range(size)])]
  transfers between devices with their start and end apart: 42 -> 42, of which waited for: 16 -> 14; matrix products, arithmetic and copies ran while one was open for 1% -> 1% of each run, Pallas kernels for 32% -> 33%
where the time goes in v5:
time: 122 us; the launch traced here: 121 us
  starting transfers between devices  47.2 us (39%)
  Pallas kernels  46.2 us (38%)
  waiting for transfers between devices  24.8 us (20%)
    ppermute x42, starting transfers between devices, hop(): return lax.ppermute(x, axis, [(i, i ^ k) for i in range(size)])  47.2 us
    pallas_call x8, Pallas kernels, call(): pl.pallas_call(kernel, out_shape=tuple(outs), in_specs=[SPEC[k] for _, k...  46.2 us
    ppermute x42, waiting for transfers between devices, hop(): return lax.ppermute(x, axis, [(i, i ^ k) for i in range(size)])  24.8 us
  transfers between devices with their start and end apart: 42, of which 14 were waited for; matrix products, arithmetic and copies ran while one was open for 1% of the time, Pallas kernels for 33%

profile of v5, /device:TPU:0, one launch (start us, length us, event | category | flops | bytes accessed | tf_op | source)
XLA Modules:
  0.0 121.4 jit_solution(10314018303333100712)
XLA Ops:
  0.6 3.4 %shard_map.230 = (bf16[576,256]{1,0:T(8,128)(2,1)}, bf16[256,384]{1,0:T(8,128)(2,1)}, f32[64,256]{1,0:T(8,128)}, bf16[144,256]{1,0:T(8,128)(2,1)}) custom-call(s32[1,16]{1,0:T(1,128)} %refs_4_.2, bf16[576]{0:T(1024)(128)(2,1)} %refs_0_.3, bf16[576,256]{1,0:T(8,128)(2,1)} %bitcast.55, bf16[192,576]{1,0:T(8,128)(2,1)} %bitcast.58, bf16[192,576]{1,0:T(8,128)(2,1)} %bitcast.61, ...), custom_call_target="tpu_custom_call" | custom-call | flops 3449999872 | bytes 1048576 | tf_op jit(solution)/shard_map/pallas_call | solution.py:114
  4.0 4.0 %collective-permute-start.5 = (bf16[256,384]{1,0:T(8,128)(2,1)}, bf16[256,384]{1,0:T(8,128)(2,1)S(1)}, u32[]{:S(2)}, u32[]{:S(2)}) collective-permute-start(bf16[256,384]{1,0:T(8,128)(2,1)} %get-tuple-element.85.refs_0_.refs_19_), channel_id=1, source_target_pairs={{0,24},{4,28},{8,16},{12,20},{16,8},{20,12},{24,0},{28,4},{1,25},{... | collective-permute-start | bytes 589832 | tf_op jit(solution)/shard_map/ppermute | solution.py:653
  8.7 4.0 %shard_map.231.refs_6_.refs_11_ = bf16[3,768,128]{2,1,0:T(8,128)(2,1)} custom-call(bf16[576,256]{1,0:T(8,128)(2,1)} %get-tuple-element.83.refs_0_, bf16[576,576]{1,0:T(8,128)(2,1)} %refs_8_.5, f32[64,256]{1,0:T(8,128)} %get-tuple-element.84.refs_2_.refs_12_), custom_call_target="tpu_custom_call" | custom-call | flops 3449999872 | bytes 1048576 | tf_op jit(solution)/shard_map/pallas_call | solution.py:114
  14.0 3.3 %collective-permute-done.4.refs_2_.refs_21_ = bf16[256,384]{1,0:T(8,128)(2,1)S(1)} collective-permute-done((bf16[256,384]{1,0:T(8,128)(2,1)}, bf16[256,384]{1,0:T(8,128)(2,1)S(1)}, u32[]{:S(2)}, u32[]{:S(2)}) %collective-permute-start.4) | collective-permute-done | bytes 196640 | tf_op jit(solution)/shard_map/ppermute | solution.py:653
  17.8 1.6 %collective-permute-start.2 = (bf16[144,256]{1,0:T(8,128)(2,1)S(1)}, bf16[144,256]{1,0:T(8,128)(2,1)S(1)}, u32[]{:S(2)}, u32[]{:S(2)}) collective-permute-start(bf16[144,256]{1,0:T(8,128)(2,1)S(1)} %copy-done.17), channel_id=1, source_target_pairs={{0,24},{4,28},{8,16},{12,20},{16,8},{20,12},{24,0},{28,4},{1,25},{... | collective-permute-start | bytes 221192 | tf_op jit(solution)/shard_map/ppermute | solution.py:653
  19.4 1.4 %collective-permute-start.1 = (bf16[144,256]{1,0:T(8,128)(2,1)S(1)}, bf16[144,256]{1,0:T(8,128)(2,1)S(1)}, u32[]{:S(2)}, u32[]{:S(2)}) collective-permute-start(bf16[144,256]{1,0:T(8,128)(2,1)S(1)} %copy-done.17), channel_id=1, source_target_pairs={{0,16},{4,20},{8,24},{12,28},{16,0},{20,4},{24,8},{28,12},{1,17},{... | collective-permute-start | bytes 221192 | tf_op jit(solution)/shard_map/ppermute | solution.py:653
  22.3 13.9 %shard_map.232 = (f32[576,256]{1,0:T(8,128)}, f32[6,1,384]{2,1,0:T(1,128)}, f32[256,640]{1,0:T(8,128)}, bf16[4,72,1152]{2,1,0:T(8,128)(2,1)}, bf16[4,72,1152]{2,...) custom-call(bf16[256,384]{1,0:T(8,128)(2,1)} %get-tuple-element.85.r, ...), custom_call_target="tpu_custom_call" | custom-call | flops 16099999744 | bytes 1048576 | tf_op jit(solution)/shard_map/pallas_call | solution.py:114
  36.9 1.6 %collective-permute-start.17 = (bf16[64,640]{1,0:T(8,128)(2,1)}, bf16[64,640]{1,0:T(8,128)(2,1)S(1)}, u32[]{:S(2)}, u32[]{:S(2)}) collective-permute-start(bf16[64,640]{1,0:T(8,128)(2,1)} %get-tuple-element.115), channel_id=1, source_target_pairs={{0,1},{1,0},{2,3},{3,2},{4,5},{5,4},{6,7},{7,6},{8,9},{9,8},{10,11... | collective-permute-start | bytes 245768 | tf_op jit(solution)/shard_map/ppermute | solution.py:653
  38.5 2.6 %collective-permute-start.18 = (bf16[64,640]{1,0:T(8,128)(2,1)}, bf16[64,640]{1,0:T(8,128)(2,1)S(1)}, u32[]{:S(2)}, u32[]{:S(2)}) collective-permute-start(bf16[64,640]{1,0:T(8,128)(2,1)} %get-tuple-element.116), channel_id=1, source_target_pairs={{0,2},{1,3},{2,0},{3,1},{4,6},{5,7},{6,4},{7,5},{8,10},{9,11},{10,... | collective-permute-start | bytes 245768 | tf_op jit(solution)/shard_map/ppermute | solution.py:653
  41.6 1.6 %collective-permute-start.8 = (bf16[72,1152]{1,0:T(8,128)(2,1)S(1)}, bf16[72,1152]{1,0:T(8,128)(2,1)S(1)}, u32[]{:S(2)}, u32[]{:S(2)}) collective-permute-start(bf16[72,1152]{1,0:T(8,128)(2,1)S(1)} %get-tuple-element.153), channel_id=1, source_target_pairs={{0,8},{4,12},{8,0},{12,4},{16,24},{20,28},{24,16},{28,20},{1,9},{5... | collective-permute-start | bytes 497672 | tf_op jit(solution)/shard_map/ppermute | solution.py:653
  43.2 1.4 %collective-permute-start.10 = (bf16[72,1152]{1,0:T(8,128)(2,1)S(1)}, bf16[72,1152]{1,0:T(8,128)(2,1)S(1)}, u32[]{:S(2)}, u32[]{:S(2)}) collective-permute-start(bf16[72,1152]{1,0:T(8,128)(2,1)S(1)} %get-tuple-element.154), channel_id=1, source_target_pairs={{0,24},{4,28},{8,16},{12,20},{16,8},{20,12},{24,0},{28,4},{1,25},{... | collective-permute-start | bytes 497672 | tf_op jit(solution)/shard_map/ppermute | solution.py:653
  44.6 3.6 %collective-permute-done.18 = bf16[64,640]{1,0:T(8,128)(2,1)S(1)} collective-permute-done((bf16[64,640]{1,0:T(8,128)(2,1)}, bf16[64,640]{1,0:T(8,128)(2,1)S(1)}, u32[]{:S(2)}, u32[]{:S(2)}) %collective-permute-start.18) | collective-permute-done | bytes 81952 | tf_op jit(solution)/shard_map/ppermute | solution.py:653
  48.2 1.4 %collective-permute-start.9 = (bf16[72,1152]{1,0:T(8,128)(2,1)S(1)}, bf16[72,1152]{1,0:T(8,128)(2,1)S(1)}, u32[]{:S(2)}, u32[]{:S(2)}) collective-permute-start(bf16[72,1152]{1,0:T(8,128)(2,1)S(1)} %get-tuple-element.155), channel_id=1, source_target_pairs={{0,16},{4,20},{8,24},{12,28},{16,0},{20,4},{24,8},{28,12},{1,17},{... | collective-permute-start | bytes 497672 | tf_op jit(solution)/shard_map/ppermute | solution.py:653
  49.7 2.5 %collective-permute-start.22 = (bf16[64,640]{1,0:T(8,128)(2,1)S(1)}, bf16[64,640]{1,0:T(8,128)(2,1)S(1)}, u32[]{:S(2)}, u32[]{:S(2)}) collective-permute-start(bf16[64,640]{1,0:T(8,128)(2,1)S(1)} %add_convert_fusion.1.refs_0_), channel_id=1, source_target_pairs={{0,3},{1,2},{2,1},{3,0},{4,7},{5,6},{6,5},{7,4},{8,11},{9,10},{10,... | collective-permute-start | bytes 245768 | tf_op jit(solution)/shard_map/ppermute | solution.py:653
  52.2 1.9 %collective-permute-start.20 = (bf16[64,640]{1,0:T(8,128)(2,1)S(1)}, bf16[64,640]{1,0:T(8,128)(2,1)S(1)}, u32[]{:S(2)}, u32[]{:S(2)}) collective-permute-start(bf16[64,640]{1,0:T(8,128)(2,1)S(1)} %add_convert_fusion.1.refs_0_), channel_id=1, source_target_pairs={{0,1},{1,0},{2,3},{3,2},{4,5},{5,4},{6,7},{7,6},{8,9},{9,8},{10,11... | collective-permute-start | bytes 245768 | tf_op jit(solution)/shard_map/ppermute | solution.py:653
  54.5 1.8 %collective-permute-done.22.refs_3_ = bf16[64,640]{1,0:T(8,128)(2,1)S(1)} collective-permute-done((bf16[64,640]{1,0:T(8,128)(2,1)S(1)}, bf16[64,640]{1,0:T(8,128)(2,1)S(1)}, u32[]{:S(2)}, u32[]{:S(2)}) %collective-permute-start.22) | collective-permute-done | bytes 81952 | tf_op jit(solution)/shard_map/ppermute | solution.py:653
  56.3 1.5 %collective-permute-start.26 = (bf16[72,1152]{1,0:T(8,128)(2,1)S(1)}, bf16[72,1152]{1,0:T(8,128)(2,1)S(1)}, u32[]{:S(2)}, u32[]{:S(2)}) collective-permute-start(bf16[72,1152]{1,0:T(8,128)(2,1)S(1)} %add_convert_fusion), channel_id=1, source_target_pairs={{0,24},{4,28},{8,16},{12,20},{16,8},{20,12},{24,0},{28,4},{1,25},{... | collective-permute-start | bytes 497672 | tf_op jit(solution)/shard_map/ppermute | solution.py:653
  61.5 1.4 %collective-permute-start.13 = (bf16[64,640]{1,0:T(8,128)(2,1)S(1)}, bf16[64,640]{1,0:T(8,128)(2,1)S(1)}, u32[]{:S(2)}, u32[]{:S(2)}) collective-permute-start(bf16[64,640]{1,0:T(8,128)(2,1)S(1)} %copy-done.23), channel_id=1, source_target_pairs={{0,3},{1,2},{2,1},{3,0},{4,7},{5,6},{6,5},{7,4},{8,11},{9,10},{10,... | collective-permute-start | bytes 245768 | tf_op jit(solution)/shard_map/ppermute | solution.py:653
  62.9 17.0 %shard_map.233 = (f32[64,640]{1,0:T(8,128)}, bf16[64,640]{1,0:T(8,128)(2,1)}, bf16[4,144,384]{2,1,0:T(8,128)(2,1)}, bf16[4,144,384]{2,1,0:T(8,128)(2,1)}) custom-call(bf16[64,640]{1,0:T(8,128)(2,1)} %copy-done.15, bf16[64,640]{1,0:T(8,128)(2,1)} %copy-done.28, bf16[64,640]{1,0:T(8,128)(2,1)} %copy-done.27, bf16[64,640]{1,0:T(8,128)(2,1)} %copy-done.26, ...), custom_call_target="tpu_custom_call" | custom-call | flops 19549999104 | bytes 1048576 | tf_op jit(solution)/shard_map/pallas_call | solution.py:114
  80.2 2.5 %collective-permute-start.16 = (bf16[64,640]{1,0:T(8,128)(2,1)S(1)}, bf16[64,640]{1,0:T(8,128)(2,1)S(1)}, u32[]{:S(2)}, u32[]{:S(2)}) collective-permute-start(bf16[64,640]{1,0:T(8,128)(2,1)S(1)} %add_convert_fusion.2.refs_4_), channel_id=1, source_target_pairs={{0,3},{1,2},{2,1},{3,0},{4,7},{5,6},{6,5},{7,4},{8,11},{9,10},{10,... | collective-permute-start | bytes 245768 | tf_op jit(solution)/shard_map/ppermute | solution.py:653
  82.7 1.9 %collective-permute-start.14 = (bf16[64,640]{1,0:T(8,128)(2,1)S(1)}, bf16[64,640]{1,0:T(8,128)(2,1)S(1)}, u32[]{:S(2)}, u32[]{:S(2)}) collective-permute-start(bf16[64,640]{1,0:T(8,128)(2,1)S(1)} %add_convert_fusion.2.refs_4_), channel_id=1, source_target_pairs={{0,1},{1,0},{2,3},{3,2},{4,5},{5,4},{6,7},{7,6},{8,9},{9,8},{10,11... | collective-permute-start | bytes 245768 | tf_op jit(solution)/shard_map/ppermute | solution.py:653
  84.9 1.7 %collective-permute-start.30 = (bf16[144,384]{1,0:T(8,128)(2,1)S(1)}, bf16[144,384]{1,0:T(8,128)(2,1)S(1)}, u32[]{:S(2)}, u32[]{:S(2)}) collective-permute-start(bf16[144,384]{1,0:T(8,128)(2,1)S(1)} %get-tuple-element.156), channel_id=1, source_target_pairs={{0,24},{4,28},{8,16},{12,20},{16,8},{20,12},{24,0},{28,4},{1,25},{... | collective-permute-start | bytes 331784 | tf_op jit(solution)/shard_map/ppermute | solution.py:653
  88.7 2.1 %collective-permute-done.15.refs_6_ = bf16[64,640]{1,0:T(8,128)(2,1)S(1)} collective-permute-done((bf16[64,640]{1,0:T(8,128)(2,1)S(1)}, bf16[64,640]{1,0:T(8,128)(2,1)S(1)}, u32[]{:S(2)}, u32[]{:S(2)}) %collective-permute-start.15) | collective-permute-done | bytes 81952 | tf_op jit(solution)/shard_map/ppermute | solution.py:653
  92.9 2.5 %collective-permute-start.36 = (bf16[80,384]{1,0:T(8,128)(2,1)S(1)}, bf16[80,384]{1,0:T(8,128)(2,1)S(1)}, u32[]{:S(2)}, u32[]{:S(2)}) collective-permute-start(bf16[80,384]{1,0:T(8,128)(2,1)S(1)} %add_convert_fusion.3), channel_id=1, source_target_pairs={{0,3},{1,2},{2,1},{3,0},{4,7},{5,6},{6,5},{7,4},{8,11},{9,10},{10,... | collective-permute-start | bytes 184328 | tf_op jit(solution)/shard_map/ppermute | solution.py:653
  97.4 2.0 %shard_map.234.refs_0_ = bf16[64,640]{1,0:T(8,128)(2,1)S(1)} custom-call(f32[144,384]{1,0:T(8,128)S(1)} %get-tuple-element.128.refs_0_, bf16[144,384]{1,0:T(8,128)(2,1)S(1)} %collective-permute-done.28.refs_1_, bf16[144,384]{1,0:T(8,128)(2,1)S(1)} %collective-permute-done.29.refs_2_, bf16[144,384]{1,0:T(8,128)(2,1)S(1)} %collective-permute-done.30.refs_3_, ...), custom_call_target="tpu_custom_call" | custom-call | flops 2300000000 | bytes 1048576 | tf_op jit(solution)/shard_map/pallas_call | solution.py:114
  99.4 2.1 %collective-permute-done.35 = bf16[80,384]{1,0:T(8,128)(2,1)S(1)} collective-permute-done((bf16[80,384]{1,0:T(8,128)(2,1)S(1)}, bf16[80,384]{1,0:T(8,128)(2,1)S(1)}, u32[]{:S(2)}, u32[]{:S(2)}) %collective-permute-start.35) | collective-permute-done | bytes 61472 | tf_op jit(solution)/shard_map/ppermute | solution.py:653
  101.6 2.0 %collective-permute-start.39 = (bf16[4,80,384]{2,1,0:T(8,128)(2,1)S(1)}, bf16[4,80,384]{2,1,0:T(8,128)(2,1)S(1)}, u32[]{:S(2)}, u32[]{:S(2)}) collective-permute-start(bf16[4,80,384]{2,1,0:T(8,128)(2,1)S(1)} %get-tuple-element.161.refs_1_), channel_id=1, source_target_pairs={{0,24},{4,28},{8,16},{12,20},{16,8},{20,12},{24,0},{28,4},{1,25},{... | collective-permute-start | bytes 737288 | tf_op jit(solution)/shard_map/ppermute | solution.py:653
  105.2 2.5 %collective-permute-start.33 = (bf16[64,640]{1,0:T(8,128)(2,1)S(1)}, bf16[64,640]{1,0:T(8,128)(2,1)S(1)}, u32[]{:S(2)}, u32[]{:S(2)}) collective-permute-start(bf16[64,640]{1,0:T(8,128)(2,1)S(1)} %shard_map.234.refs_0_), channel_id=1, source_target_pairs={{0,3},{1,2},{2,1},{3,0},{4,7},{5,6},{6,5},{7,4},{8,11},{9,10},{10,... | collective-permute-start | bytes 245768 | tf_op jit(solution)/shard_map/ppermute | solution.py:653
  107.7 1.7 %shard_map.236 = (f32[576,384]{1,0:T(8,128)}, f32[576,384]{1,0:T(8,128)}, f32[576,384]{1,0:T(8,128)}) custom-call(bf16[72,1152]{1,0:T(8,128)(2,1)S(1)} %add_convert_fusion, bf16[72,1152]{1,0:T(8,128)(2,1)S(1)} %collective-permute-done.24.refs_1_, bf16[72,1152]{1,0:T(8,128)(2,1)S(1)} %collective-permute-done.25.refs_2_, ...), custom_call_target="tpu_custom_call" | custom-call | flops 2300000000 | bytes 1048576 | tf_op jit(solution)/shard_map/pallas_call | solution.py:114
  109.5 2.0 %collective-permute-done.39.refs_4_ = bf16[4,80,384]{2,1,0:T(8,128)(2,1)S(1)} collective-permute-done((bf16[4,80,384]{2,1,0:T(8,128)(2,1)S(1)}, bf16[4,80,384]{2,1,0:T(8,128)(2,1)S(1)}, u32[]{:S(2)}, u32[]{:S(2)}) %collective-permute-start.39) | collective-permute-done | bytes 245792 | tf_op jit(solution)/shard_map/ppermute | solution.py:653
  111.6 3.6 %collective-permute-done.38.refs_3_ = bf16[4,80,384]{2,1,0:T(8,128)(2,1)S(1)} collective-permute-done((bf16[4,80,384]{2,1,0:T(8,128)(2,1)S(1)}, bf16[4,80,384]{2,1,0:T(8,128)(2,1)S(1)}, u32[]{:S(2)}, u32[]{:S(2)}) %collective-permute-start.38) | collective-permute-done | bytes 245792 | tf_op jit(solution)/shard_map/ppermute | solution.py:653
  118.5 2.9 %shard_map.237 = (f32[576,576]{1,0:T(8,128)}, f32[576,576]{1,0:T(8,128)}, f32[192,576]{1,0:T(8,128)}, f32[192,576]{1,0:T(8,128)}, f32[576]{0:T(1024)}, /*index=5*/f32[576]{0:T(1024)}) custom-call(bf16[576]{0:T(1024)(128)(2,1)S(1)} %copy-done.4, bf16[4,80,384]{2,1,0:T(8,128)(2,1)S(1)} %get-tuple-element.161.refs_1_, ...), custom_call_target="tpu_custom_call" | custom-call | flops 3449999872 | bytes 1048576 | tf_op jit(solution)/shard_map/pallas_call | solution.py:114
  (131 shorter events, 20.6 us)
Async XLA Ops:
  4.0 9.9 %collective-permute-start.5 = (bf16[256,384]{1,0:T(8,128)(2,1)}, bf16[256,384]{1,0:T(8,128)(2,1)S(1)}, u32[]{:S(2)}, u32[]{:S(2)}) collective-permute-start(bf16[256,384]{1,0:T(8,128)(2,1)} %get-tuple-element.85.refs_0_.refs_19_), channel_id=1, source_target_pairs={{0,24},{4,28},{8,16},{12,20},{16,8},{20,12},{24,0},{28,4},{1,25},{... | collective-permute-start | bytes 589832 | tf_op jit(solution)/shard_map/ppermute | solution.py:653
  8.0 9.3 %collective-permute-start.4 = (bf16[256,384]{1,0:T(8,128)(2,1)}, bf16[256,384]{1,0:T(8,128)(2,1)S(1)}, u32[]{:S(2)}, u32[]{:S(2)}) collective-permute-start(bf16[256,384]{1,0:T(8,128)(2,1)} %get-tuple-element.85.refs_0_.refs_19_), channel_id=1, source_target_pairs={{0,16},{4,20},{8,24},{12,28},{16,0},{20,4},{24,8},{28,12},{1,17},{... | collective-permute-start | bytes 589832 | tf_op jit(solution)/shard_map/ppermute | solution.py:653
  8.5 9.1 %collective-permute-start.3 = (bf16[256,384]{1,0:T(8,128)(2,1)}, bf16[256,384]{1,0:T(8,128)(2,1)S(1)}, u32[]{:S(2)}, u32[]{:S(2)}) collective-permute-start(bf16[256,384]{1,0:T(8,128)(2,1)} %get-tuple-element.85.refs_0_.refs_19_), channel_id=1, source_target_pairs={{0,8},{4,12},{8,0},{12,4},{16,24},{20,28},{24,16},{28,20},{1,9},{5... | collective-permute-start | bytes 589832 | tf_op jit(solution)/shard_map/ppermute | solution.py:653
  17.8 18.4 %collective-permute-start.2 = (bf16[144,256]{1,0:T(8,128)(2,1)S(1)}, bf16[144,256]{1,0:T(8,128)(2,1)S(1)}, u32[]{:S(2)}, u32[]{:S(2)}) collective-permute-start(bf16[144,256]{1,0:T(8,128)(2,1)S(1)} %copy-done.17), channel_id=1, source_target_pairs={{0,24},{4,28},{8,16},{12,20},{16,8},{20,12},{24,0},{28,4},{1,25},{... | collective-permute-start | bytes 221192 | tf_op jit(solution)/shard_map/ppermute | solution.py:653
  19.4 16.8 %collective-permute-start.1 = (bf16[144,256]{1,0:T(8,128)(2,1)S(1)}, bf16[144,256]{1,0:T(8,128)(2,1)S(1)}, u32[]{:S(2)}, u32[]{:S(2)}) collective-permute-start(bf16[144,256]{1,0:T(8,128)(2,1)S(1)} %copy-done.17), channel_id=1, source_target_pairs={{0,16},{4,20},{8,24},{12,28},{16,0},{20,4},{24,8},{28,12},{1,17},{... | collective-permute-start | bytes 221192 | tf_op jit(solution)/shard_map/ppermute | solution.py:653
  20.9 15.4 %collective-permute-start = (bf16[144,256]{1,0:T(8,128)(2,1)S(1)}, bf16[144,256]{1,0:T(8,128)(2,1)S(1)}, u32[]{:S(2)}, u32[]{:S(2)}) collective-permute-start(bf16[144,256]{1,0:T(8,128)(2,1)S(1)} %copy-done.17), channel_id=1, source_target_pairs={{0,8},{4,12},{8,0},{12,4},{16,24},{20,28},{24,16},{28,20},{1,9},{5... | collective-permute-start | bytes 221192 | tf_op jit(solution)/shard_map/ppermute | solution.py:653
  36.4 23.9 %collective-permute-start.23 = (bf16[4,144,256]{2,1,0:T(8,128)(2,1)S(1)}, bf16[4,144,256]{2,1,0:T(8,128)(2,1)S(1)}, u32[]{:S(2)}, u32[]{:S(2)}) collective-permute-start(bf16[4,144,256]{2,1,0:T(8,128)(2,1)S(1)} %pad_maximum_fusion.3), channel_id=1, source_target_pairs={{0,4},{4,0},{8,12},{12,8},{16,20},{20,16},{24,28},{28,24},{1,5},{5... | collective-permute-start | bytes 884744 | tf_op jit(solution)/shard_map/ppermute | solution.py:653
  36.9 6.2 %collective-permute-start.17 = (bf16[64,640]{1,0:T(8,128)(2,1)}, bf16[64,640]{1,0:T(8,128)(2,1)S(1)}, u32[]{:S(2)}, u32[]{:S(2)}) collective-permute-start(bf16[64,640]{1,0:T(8,128)(2,1)} %get-tuple-element.115), channel_id=1, source_target_pairs={{0,1},{1,0},{2,3},{3,2},{4,5},{5,4},{6,7},{7,6},{8,9},{9,8},{10,11... | collective-permute-start | bytes 245768 | tf_op jit(solution)/shard_map/ppermute | solution.py:653
  38.5 9.6 %collective-permute-start.18 = (bf16[64,640]{1,0:T(8,128)(2,1)}, bf16[64,640]{1,0:T(8,128)(2,1)S(1)}, u32[]{:S(2)}, u32[]{:S(2)}) collective-permute-start(bf16[64,640]{1,0:T(8,128)(2,1)} %get-tuple-element.116), channel_id=1, source_target_pairs={{0,2},{1,3},{2,0},{3,1},{4,6},{5,7},{6,4},{7,5},{8,10},{9,11},{10,... | collective-permute-start | bytes 245768 | tf_op jit(solution)/shard_map/ppermute | solution.py:653
  41.1 8.5 %collective-permute-start.19 = (bf16[64,640]{1,0:T(8,128)(2,1)}, bf16[64,640]{1,0:T(8,128)(2,1)S(1)}, u32[]{:S(2)}, u32[]{:S(2)}) collective-permute-start(bf16[64,640]{1,0:T(8,128)(2,1)} %get-tuple-element.117), channel_id=1, source_target_pairs={{0,3},{1,2},{2,1},{3,0},{4,7},{5,6},{6,5},{7,4},{8,11},{9,10},{10,... | collective-permute-start | bytes 245768 | tf_op jit(solution)/shard_map/ppermute | solution.py:653
  41.6 10.6 %collective-permute-start.8 = (bf16[72,1152]{1,0:T(8,128)(2,1)S(1)}, bf16[72,1152]{1,0:T(8,128)(2,1)S(1)}, u32[]{:S(2)}, u32[]{:S(2)}) collective-permute-start(bf16[72,1152]{1,0:T(8,128)(2,1)S(1)} %get-tuple-element.153), channel_id=1, source_target_pairs={{0,8},{4,12},{8,0},{12,4},{16,24},{20,28},{24,16},{28,20},{1,9},{5... | collective-permute-start | bytes 497672 | tf_op jit(solution)/shard_map/ppermute | solution.py:653
  43.2 9.1 %collective-permute-start.10 = (bf16[72,1152]{1,0:T(8,128)(2,1)S(1)}, bf16[72,1152]{1,0:T(8,128)(2,1)S(1)}, u32[]{:S(2)}, u32[]{:S(2)}) collective-permute-start(bf16[72,1152]{1,0:T(8,128)(2,1)S(1)} %get-tuple-element.154), channel_id=1, source_target_pairs={{0,24},{4,28},{8,16},{12,20},{16,8},{20,12},{24,0},{28,4},{1,25},{... | collective-permute-start | bytes 497672 | tf_op jit(solution)/shard_map/ppermute | solution.py:653
  49.7 6.6 %collective-permute-start.22 = (bf16[64,640]{1,0:T(8,128)(2,1)S(1)}, bf16[64,640]{1,0:T(8,128)(2,1)S(1)}, u32[]{:S(2)}, u32[]{:S(2)}) collective-permute-start(bf16[64,640]{1,0:T(8,128)(2,1)S(1)} %add_convert_fusion.1.refs_0_), channel_id=1, source_target_pairs={{0,3},{1,2},{2,1},{3,0},{4,7},{5,6},{6,5},{7,4},{8,11},{9,10},{10,... | collective-permute-start | bytes 245768 | tf_op jit(solution)/shard_map/ppermute | solution.py:653
  52.2 6.9 %collective-permute-start.20 = (bf16[64,640]{1,0:T(8,128)(2,1)S(1)}, bf16[64,640]{1,0:T(8,128)(2,1)S(1)}, u32[]{:S(2)}, u32[]{:S(2)}) collective-permute-start(bf16[64,640]{1,0:T(8,128)(2,1)S(1)} %add_convert_fusion.1.refs_0_), channel_id=1, source_target_pairs={{0,1},{1,0},{2,3},{3,2},{4,5},{5,4},{6,7},{7,6},{8,9},{9,8},{10,11... | collective-permute-start | bytes 245768 | tf_op jit(solution)/shard_map/ppermute | solution.py:653
  54.3 7.2 %collective-permute-start.11 = (bf16[64,640]{1,0:T(8,128)(2,1)S(1)}, bf16[64,640]{1,0:T(8,128)(2,1)S(1)}, u32[]{:S(2)}, u32[]{:S(2)}) collective-permute-start(bf16[64,640]{1,0:T(8,128)(2,1)S(1)} %copy-done.25), channel_id=1, source_target_pairs={{0,1},{1,0},{2,3},{3,2},{4,5},{5,4},{6,7},{7,6},{8,9},{9,8},{10,11... | collective-permute-start | bytes 245768 | tf_op jit(solution)/shard_map/ppermute | solution.py:653
  56.3 23.7 %collective-permute-start.26 = (bf16[72,1152]{1,0:T(8,128)(2,1)S(1)}, bf16[72,1152]{1,0:T(8,128)(2,1)S(1)}, u32[]{:S(2)}, u32[]{:S(2)}) collective-permute-start(bf16[72,1152]{1,0:T(8,128)(2,1)S(1)} %add_convert_fusion), channel_id=1, source_target_pairs={{0,24},{4,28},{8,16},{12,20},{16,8},{20,12},{24,0},{28,4},{1,25},{... | collective-permute-start | bytes 497672 | tf_op jit(solution)/shard_map/ppermute | solution.py:653
  58.3 21.7 %collective-permute-start.25 = (bf16[72,1152]{1,0:T(8,128)(2,1)S(1)}, bf16[72,1152]{1,0:T(8,128)(2,1)S(1)}, u32[]{:S(2)}, u32[]{:S(2)}) collective-permute-start(bf16[72,1152]{1,0:T(8,128)(2,1)S(1)} %add_convert_fusion), channel_id=1, source_target_pairs={{0,16},{4,20},{8,24},{12,28},{16,0},{20,4},{24,8},{28,12},{1,17},{... | collective-permute-start | bytes 497672 | tf_op jit(solution)/shard_map/ppermute | solution.py:653
  59.2 20.8 %collective-permute-start.24 = (bf16[72,1152]{1,0:T(8,128)(2,1)S(1)}, bf16[72,1152]{1,0:T(8,128)(2,1)S(1)}, u32[]{:S(2)}, u32[]{:S(2)}) collective-permute-start(bf16[72,1152]{1,0:T(8,128)(2,1)S(1)} %add_convert_fusion), channel_id=1, source_target_pairs={{0,8},{4,12},{8,0},{12,4},{16,24},{20,28},{24,16},{28,20},{1,9},{5... | collective-permute-start | bytes 497672 | tf_op jit(solution)/shard_map/ppermute | solution.py:653
  60.3 19.6 %collective-permute-start.12 = (bf16[64,640]{1,0:T(8,128)(2,1)S(1)}, bf16[64,640]{1,0:T(8,128)(2,1)S(1)}, u32[]{:S(2)}, u32[]{:S(2)}) collective-permute-start(bf16[64,640]{1,0:T(8,128)(2,1)S(1)} %copy-done.24), channel_id=1, source_target_pairs={{0,2},{1,3},{2,0},{3,1},{4,6},{5,7},{6,4},{7,5},{8,10},{9,11},{10,... | collective-permute-start | bytes 245768 | tf_op jit(solution)/shard_map/ppermute | solution.py:653
  61.5 18.5 %collective-permute-start.13 = (bf16[64,640]{1,0:T(8,128)(2,1)S(1)}, bf16[64,640]{1,0:T(8,128)(2,1)S(1)}, u32[]{:S(2)}, u32[]{:S(2)}) collective-permute-start(bf16[64,640]{1,0:T(8,128)(2,1)S(1)} %copy-done.23), channel_id=1, source_target_pairs={{0,3},{1,2},{2,1},{3,0},{4,7},{5,6},{6,5},{7,4},{8,11},{9,10},{10,... | collective-permute-start | bytes 245768 | tf_op jit(solution)/shard_map/ppermute | solution.py:653
  80.2 7.4 %collective-permute-start.16 = (bf16[64,640]{1,0:T(8,128)(2,1)S(1)}, bf16[64,640]{1,0:T(8,128)(2,1)S(1)}, u32[]{:S(2)}, u32[]{:S(2)}) collective-permute-start(bf16[64,640]{1,0:T(8,128)(2,1)S(1)} %add_convert_fusion.2.refs_4_), channel_id=1, source_target_pairs={{0,3},{1,2},{2,1},{3,0},{4,7},{5,6},{6,5},{7,4},{8,11},{9,10},{10,... | collective-permute-start | bytes 245768 | tf_op jit(solution)/shard_map/ppermute | solution.py:653
  82.6 8.1 %collective-permute-start.15 = (bf16[64,640]{1,0:T(8,128)(2,1)S(1)}, bf16[64,640]{1,0:T(8,128)(2,1)S(1)}, u32[]{:S(2)}, u32[]{:S(2)}) collective-permute-start(bf16[64,640]{1,0:T(8,128)(2,1)S(1)} %add_convert_fusion.2.refs_4_), channel_id=1, source_target_pairs={{0,2},{1,3},{2,0},{3,1},{4,6},{5,7},{6,4},{7,5},{8,10},{9,11},{10,... | collective-permute-start | bytes 245768 | tf_op jit(solution)/shard_map/ppermute | solution.py:653
  82.7 8.1 %collective-permute-start.14 = (bf16[64,640]{1,0:T(8,128)(2,1)S(1)}, bf16[64,640]{1,0:T(8,128)(2,1)S(1)}, u32[]{:S(2)}, u32[]{:S(2)}) collective-permute-start(bf16[64,640]{1,0:T(8,128)(2,1)S(1)} %add_convert_fusion.2.refs_4_), channel_id=1, source_target_pairs={{0,1},{1,0},{2,3},{3,2},{4,5},{5,4},{6,7},{7,6},{8,9},{9,8},{10,11... | collective-permute-start | bytes 245768 | tf_op jit(solution)/shard_map/ppermute | solution.py:653
  84.9 6.6 %collective-permute-start.30 = (bf16[144,384]{1,0:T(8,128)(2,1)S(1)}, bf16[144,384]{1,0:T(8,128)(2,1)S(1)}, u32[]{:S(2)}, u32[]{:S(2)}) collective-permute-start(bf16[144,384]{1,0:T(8,128)(2,1)S(1)} %get-tuple-element.156), channel_id=1, source_target_pairs={{0,24},{4,28},{8,16},{12,20},{16,8},{20,12},{24,0},{28,4},{1,25},{... | collective-permute-start | bytes 331784 | tf_op jit(solution)/shard_map/ppermute | solution.py:653
  90.8 17.0 %collective-permute-start.40 = (bf16[4,72,1152]{2,1,0:T(8,128)(2,1)S(1)}, bf16[4,72,1152]{2,1,0:T(8,128)(2,1)S(1)}, u32[]{:S(2)}, u32[]{:S(2)}) collective-permute-start(bf16[4,72,1152]{2,1,0:T(8,128)(2,1)S(1)} %pad_maximum_fusion.2), channel_id=1, source_target_pairs={{0,4},{4,0},{8,12},{12,8},{16,20},{20,16},{24,28},{28,24},{1,5},{5... | collective-permute-start | bytes 1990664 | tf_op jit(solution)/shard_map/ppermute | solution.py:653
  92.9 6.5 %collective-permute-start.36 = (bf16[80,384]{1,0:T(8,128)(2,1)S(1)}, bf16[80,384]{1,0:T(8,128)(2,1)S(1)}, u32[]{:S(2)}, u32[]{:S(2)}) collective-permute-start(bf16[80,384]{1,0:T(8,128)(2,1)S(1)} %add_convert_fusion.3), channel_id=1, source_target_pairs={{0,3},{1,2},{2,1},{3,0},{4,7},{5,6},{6,5},{7,4},{8,11},{9,10},{10,... | collective-permute-start | bytes 184328 | tf_op jit(solution)/shard_map/ppermute | solution.py:653
  95.3 6.2 %collective-permute-start.35 = (bf16[80,384]{1,0:T(8,128)(2,1)S(1)}, bf16[80,384]{1,0:T(8,128)(2,1)S(1)}, u32[]{:S(2)}, u32[]{:S(2)}) collective-permute-start(bf16[80,384]{1,0:T(8,128)(2,1)S(1)} %add_convert_fusion.3), channel_id=1, source_target_pairs={{0,2},{1,3},{2,0},{3,1},{4,6},{5,7},{6,4},{7,5},{8,10},{9,11},{10,... | collective-permute-start | bytes 184328 | tf_op jit(solution)/shard_map/ppermute | solution.py:653
  101.6 9.9 %collective-permute-start.39 = (bf16[4,80,384]{2,1,0:T(8,128)(2,1)S(1)}, bf16[4,80,384]{2,1,0:T(8,128)(2,1)S(1)}, u32[]{:S(2)}, u32[]{:S(2)}) collective-permute-start(bf16[4,80,384]{2,1,0:T(8,128)(2,1)S(1)} %get-tuple-element.161.refs_1_), channel_id=1, source_target_pairs={{0,24},{4,28},{8,16},{12,20},{16,8},{20,12},{24,0},{28,4},{1,25},{... | collective-permute-start | bytes 737288 | tf_op jit(solution)/shard_map/ppermute | solution.py:653
  103.6 11.6 %collective-permute-start.38 = (bf16[4,80,384]{2,1,0:T(8,128)(2,1)S(1)}, bf16[4,80,384]{2,1,0:T(8,128)(2,1)S(1)}, u32[]{:S(2)}, u32[]{:S(2)}) collective-permute-start(bf16[4,80,384]{2,1,0:T(8,128)(2,1)S(1)} %get-tuple-element.161.refs_1_), channel_id=1, source_target_pairs={{0,16},{4,20},{8,24},{12,28},{16,0},{20,4},{24,8},{28,12},{1,17},{... | collective-permute-start | bytes 737288 | tf_op jit(solution)/shard_map/ppermute | solution.py:653
  103.9 11.3 %collective-permute-start.37 = (bf16[4,80,384]{2,1,0:T(8,128)(2,1)S(1)}, bf16[4,80,384]{2,1,0:T(8,128)(2,1)S(1)}, u32[]{:S(2)}, u32[]{:S(2)}) collective-permute-start(bf16[4,80,384]{2,1,0:T(8,128)(2,1)S(1)} %get-tuple-element.161.refs_1_), channel_id=1, source_target_pairs={{0,8},{4,12},{8,0},{12,4},{16,24},{20,28},{24,16},{28,20},{1,9},{5... | collective-permute-start | bytes 737288 | tf_op jit(solution)/shard_map/ppermute | solution.py:653
  105.2 10.2 %collective-permute-start.33 = (bf16[64,640]{1,0:T(8,128)(2,1)S(1)}, bf16[64,640]{1,0:T(8,128)(2,1)S(1)}, u32[]{:S(2)}, u32[]{:S(2)}) collective-permute-start(bf16[64,640]{1,0:T(8,128)(2,1)S(1)} %shard_map.234.refs_0_), channel_id=1, source_target_pairs={{0,3},{1,2},{2,1},{3,0},{4,7},{5,6},{6,5},{7,4},{8,11},{9,10},{10,... | collective-permute-start | bytes 245768 | tf_op jit(solution)/shard_map/ppermute | solution.py:653
  107.7 7.7 %collective-permute-start.32 = (bf16[64,640]{1,0:T(8,128)(2,1)S(1)}, bf16[64,640]{1,0:T(8,128)(2,1)S(1)}, u32[]{:S(2)}, u32[]{:S(2)}) collective-permute-start(bf16[64,640]{1,0:T(8,128)(2,1)S(1)} %shard_map.234.refs_0_), channel_id=1, source_target_pairs={{0,2},{1,3},{2,0},{3,1},{4,6},{5,7},{6,4},{7,5},{8,10},{9,11},{10,... | collective-permute-start | bytes 245768 | tf_op jit(solution)/shard_map/ppermute | solution.py:653
  (39 other events, 335.5 us)

commit v6 on v5

--- a/solution.py
+++ b/solution.py
@@ -153,21 +153,19 @@
     copies = []
     for half in range(2):
         src = turned.at[order[0, 2 * meta[0] + half]]
-        copies.append(pltpu.make_async_copy(src, scratch[1].at[half], scratch[2].at[half]))
+        copies.append(pltpu.make_async_copy(src, scratch[0].at[half], scratch[1].at[half]))
         copies[-1].start()
     return copies
 
 
 def key_body(ins, outs, scratch, copies):
     meta, order, gain, tok, wk, wv, turned = ins
-    normed_out, kv_out, angle_out, normed_q = outs
-    normed_s, angle_s, sems = scratch
+    normed_out, kv_out, angle_out = outs
+    angle_s, sems = scratch
     x = tok.get()[...].astype(F32)
     gain = jnp.broadcast_to(row_of(gain.get()), (8, x.shape[0])).T[:, 0:1]
     normed = (x * norm_scale(x, 0) * gain).astype(BF)
     normed_out[...] = normed
-    normed_s[...] = normed.astype(F32)
-    normed_q[...] = normed_s[span(meta[1], normed_q.shape[0]), :].astype(BF)
     for copy in copies:
         copy.wait()
     angle = jnp.concatenate([angle_s[0], angle_s[1]], axis=1)
@@ -183,8 +181,11 @@
 
 
 def query_body(ins, outs, scratch):
-    normed, wq, angle = ins
-    q_out = outs[0].ref
+    meta, normed, wq, angle = ins
+    q_out, normed_q = outs[0].ref, outs[1]
+    (normed_s,) = scratch
+    normed_s[...] = normed[...].astype(F32)
+    normed_q[...] = normed_s[span(meta[1], normed_q.shape[0]), :].astype(BF)
     rows = normed.shape[1]
     stretch = rows // 2
     q = dot(normed[...].astype(F32).T.astype(BF), wq.get()[...])
@@ -710,26 +711,25 @@
     turned, first, inner = (jnp.asarray(t) for t in angle_tables(n, stretch))
     tok, cot, wk, wv, w_down = tokens.T, cotangent.T, w_key.T, w_value.T, w_down.T
 
-    normed, kv, angle, normed_q = call(
+    normed, kv, angle = call(
         key_body,
         [None, stretch_order, norm_attn, tok, wk, wv, turned],
         "mscccch",
-        [shape((width, rows), BF), shape((rows, kv_width), BF), shape((HEAD, rows), F32)]
-        + [shape((strip, rows), BF)],
-        "vvvv",
+        [shape((width, rows), BF), shape((rows, kv_width), BF), shape((HEAD, rows), F32)],
+        "vvv",
         scratch=[
-            pltpu.VMEM((width, rows), F32),
             pltpu.VMEM((2, HEAD, stretch), F32),
             pltpu.SemaphoreType.DMA((2,)),
         ],
         early=key_early,
     )
-    (q,) = call(
+    q, normed_q = call(
         query_body,
-        [normed, w_query, angle],
-        "vcv",
-        [shape((KV_HEADS, 2 * wide, PAIR), BF)],
-        "c",
+        [None, normed, w_query, angle],
+        "mvcv",
+        [shape((KV_HEADS, 2 * wide, PAIR), BF), shape((strip, rows), BF)],
+        "cv",
+        scratch=[pltpu.VMEM((width, rows), F32)],
     )
     evens = [kv] + [hop(kv, "ctx", n, k) for k in range(2, n, 2)]
     strips = [normed_q] + [hop(normed_q, "ctx", n, k) for k in range(2, n, 2)]

time: 122 us -> 122 us (level)
  no operation moved by 1% of the time
where the time goes in v6:
time: 122 us; the launch traced here: 121 us
  starting transfers between devices  47.1 us (39%)
  Pallas kernels  46.8 us (38%)
  waiting for transfers between devices  24.3 us (20%)
    ppermute x42, starting transfers between devices, hop(): return lax.ppermute(x, axis, [(i, i ^ k) for i in range(size)])  47.1 us
    pallas_call x8, Pallas kernels, call(): pl.pallas_call(kernel, out_shape=tuple(outs), in_specs=[SPEC[k] for _, k...  46.8 us
    ppermute x42, waiting for transfers between devices, hop(): return lax.ppermute(x, axis, [(i, i ^ k) for i in range(size)])  24.3 us
  transfers between devices with their start and end apart: 42, of which 14 were waited for; matrix products, arithmetic and copies ran while one was open for 1% of the time, Pallas kernels for 33%

profile of v6, /device:TPU:0, one launch (start us, length us, event | category | flops | bytes accessed | tf_op | source)
XLA Modules:
  0.0 121.4 jit_solution(17696490202876289654)
XLA Ops:
  0.6 3.4 %shard_map.230 = (bf16[576,256]{1,0:T(8,128)(2,1)}, bf16[256,384]{1,0:T(8,128)(2,1)}, f32[64,256]{1,0:T(8,128)}) custom-call(s32[1,16]{1,0:T(1,128)} %refs_4_.2, bf16[576]{0:T(1024)(128)(2,1)} %refs_0_.3, bf16[576,256]{1,0:T(8,128)(2,1)} %bitcast.55, bf16[192,576]{1,0:T(8,128)(2,1)} %bitcast.58, bf16[192,576]{1,0:T(8,128)(2,1)} %bitcast.61, ...), custom_call_target="tpu_custom_call" | custom-call | flops 3449999872 | bytes 1048576 | tf_op jit(solution)/shard_map/pallas_call | solution.py:114
  4.0 4.0 %collective-permute-start.5 = (bf16[256,384]{1,0:T(8,128)(2,1)}, bf16[256,384]{1,0:T(8,128)(2,1)S(1)}, u32[]{:S(2)}, u32[]{:S(2)}) collective-permute-start(bf16[256,384]{1,0:T(8,128)(2,1)} %get-tuple-element.87.refs_0_.refs_19_), channel_id=1, source_target_pairs={{0,24},{4,28},{8,16},{12,20},{16,8},{20,12},{24,0},{28,4},{1,25},{... | collective-permute-start | bytes 589832 | tf_op jit(solution)/shard_map/ppermute | solution.py:654
  8.6 4.6 %shard_map.231 = (bf16[3,768,128]{2,1,0:T(8,128)(2,1)}, bf16[144,256]{1,0:T(8,128)(2,1)}) custom-call(bf16[576,256]{1,0:T(8,128)(2,1)} %get-tuple-element.82.refs_0_, bf16[576,576]{1,0:T(8,128)(2,1)} %refs_8_.5, f32[64,256]{1,0:T(8,128)} %get-tuple-element.83.refs_2_.refs_12_), custom_call_target="tpu_custom_call" | custom-call | flops 3449999872 | bytes 1048576 | tf_op jit(solution)/shard_map/pallas_call | solution.py:114
  14.0 3.3 %collective-permute-done.4.refs_2_.refs_21_ = bf16[256,384]{1,0:T(8,128)(2,1)S(1)} collective-permute-done((bf16[256,384]{1,0:T(8,128)(2,1)}, bf16[256,384]{1,0:T(8,128)(2,1)S(1)}, u32[]{:S(2)}, u32[]{:S(2)}) %collective-permute-start.4) | collective-permute-done | bytes 196640 | tf_op jit(solution)/shard_map/ppermute | solution.py:654
  17.8 1.6 %collective-permute-start.2 = (bf16[144,256]{1,0:T(8,128)(2,1)S(1)}, bf16[144,256]{1,0:T(8,128)(2,1)S(1)}, u32[]{:S(2)}, u32[]{:S(2)}) collective-permute-start(bf16[144,256]{1,0:T(8,128)(2,1)S(1)} %copy-done.17), channel_id=1, source_target_pairs={{0,24},{4,28},{8,16},{12,20},{16,8},{20,12},{24,0},{28,4},{1,25},{... | collective-permute-start | bytes 221192 | tf_op jit(solution)/shard_map/ppermute | solution.py:654
  19.4 1.4 %collective-permute-start.1 = (bf16[144,256]{1,0:T(8,128)(2,1)S(1)}, bf16[144,256]{1,0:T(8,128)(2,1)S(1)}, u32[]{:S(2)}, u32[]{:S(2)}) collective-permute-start(bf16[144,256]{1,0:T(8,128)(2,1)S(1)} %copy-done.17), channel_id=1, source_target_pairs={{0,16},{4,20},{8,24},{12,28},{16,0},{20,4},{24,8},{28,12},{1,17},{... | collective-permute-start | bytes 221192 | tf_op jit(solution)/shard_map/ppermute | solution.py:654
  22.3 13.9 %shard_map.232 = (f32[576,256]{1,0:T(8,128)}, f32[6,1,384]{2,1,0:T(1,128)}, f32[256,640]{1,0:T(8,128)}, bf16[4,72,1152]{2,1,0:T(8,128)(2,1)}, bf16[4,72,1152]{2,...) custom-call(bf16[256,384]{1,0:T(8,128)(2,1)} %get-tuple-element.87.r, ...), custom_call_target="tpu_custom_call" | custom-call | flops 16099999744 | bytes 1048576 | tf_op jit(solution)/shard_map/pallas_call | solution.py:114
  36.9 1.6 %collective-permute-start.17 = (bf16[64,640]{1,0:T(8,128)(2,1)}, bf16[64,640]{1,0:T(8,128)(2,1)S(1)}, u32[]{:S(2)}, u32[]{:S(2)}) collective-permute-start(bf16[64,640]{1,0:T(8,128)(2,1)} %get-tuple-element.117), channel_id=1, source_target_pairs={{0,1},{1,0},{2,3},{3,2},{4,5},{5,4},{6,7},{7,6},{8,9},{9,8},{10,11... | collective-permute-start | bytes 245768 | tf_op jit(solution)/shard_map/ppermute | solution.py:654
  38.5 2.6 %collective-permute-start.18 = (bf16[64,640]{1,0:T(8,128)(2,1)}, bf16[64,640]{1,0:T(8,128)(2,1)S(1)}, u32[]{:S(2)}, u32[]{:S(2)}) collective-permute-start(bf16[64,640]{1,0:T(8,128)(2,1)} %get-tuple-element.118), channel_id=1, source_target_pairs={{0,2},{1,3},{2,0},{3,1},{4,6},{5,7},{6,4},{7,5},{8,10},{9,11},{10,... | collective-permute-start | bytes 245768 | tf_op jit(solution)/shard_map/ppermute | solution.py:654
  41.6 1.6 %collective-permute-start.8 = (bf16[72,1152]{1,0:T(8,128)(2,1)S(1)}, bf16[72,1152]{1,0:T(8,128)(2,1)S(1)}, u32[]{:S(2)}, u32[]{:S(2)}) collective-permute-start(bf16[72,1152]{1,0:T(8,128)(2,1)S(1)} %get-tuple-element.155), channel_id=1, source_target_pairs={{0,8},{4,12},{8,0},{12,4},{16,24},{20,28},{24,16},{28,20},{1,9},{5... | collective-permute-start | bytes 497672 | tf_op jit(solution)/shard_map/ppermute | solution.py:654
  43.1 1.4 %collective-permute-start.10 = (bf16[72,1152]{1,0:T(8,128)(2,1)S(1)}, bf16[72,1152]{1,0:T(8,128)(2,1)S(1)}, u32[]{:S(2)}, u32[]{:S(2)}) collective-permute-start(bf16[72,1152]{1,0:T(8,128)(2,1)S(1)} %get-tuple-element.156), channel_id=1, source_target_pairs={{0,24},{4,28},{8,16},{12,20},{16,8},{20,12},{24,0},{28,4},{1,25},{... | collective-permute-start | bytes 497672 | tf_op jit(solution)/shard_map/ppermute | solution.py:654
  44.6 3.6 %collective-permute-done.18 = bf16[64,640]{1,0:T(8,128)(2,1)S(1)} collective-permute-done((bf16[64,640]{1,0:T(8,128)(2,1)}, bf16[64,640]{1,0:T(8,128)(2,1)S(1)}, u32[]{:S(2)}, u32[]{:S(2)}) %collective-permute-start.18) | collective-permute-done | bytes 81952 | tf_op jit(solution)/shard_map/ppermute | solution.py:654
  48.1 1.4 %collective-permute-start.9 = (bf16[72,1152]{1,0:T(8,128)(2,1)S(1)}, bf16[72,1152]{1,0:T(8,128)(2,1)S(1)}, u32[]{:S(2)}, u32[]{:S(2)}) collective-permute-start(bf16[72,1152]{1,0:T(8,128)(2,1)S(1)} %get-tuple-element.157), channel_id=1, source_target_pairs={{0,16},{4,20},{8,24},{12,28},{16,0},{20,4},{24,8},{28,12},{1,17},{... | collective-permute-start | bytes 497672 | tf_op jit(solution)/shard_map/ppermute | solution.py:654
  49.6 2.5 %collective-permute-start.22 = (bf16[64,640]{1,0:T(8,128)(2,1)S(1)}, bf16[64,640]{1,0:T(8,128)(2,1)S(1)}, u32[]{:S(2)}, u32[]{:S(2)}) collective-permute-start(bf16[64,640]{1,0:T(8,128)(2,1)S(1)} %add_convert_fusion.1.refs_0_), channel_id=1, source_target_pairs={{0,3},{1,2},{2,1},{3,0},{4,7},{5,6},{6,5},{7,4},{8,11},{9,10},{10,... | collective-permute-start | bytes 245768 | tf_op jit(solution)/shard_map/ppermute | solution.py:654
  52.2 1.9 %collective-permute-start.20 = (bf16[64,640]{1,0:T(8,128)(2,1)S(1)}, bf16[64,640]{1,0:T(8,128)(2,1)S(1)}, u32[]{:S(2)}, u32[]{:S(2)}) collective-permute-start(bf16[64,640]{1,0:T(8,128)(2,1)S(1)} %add_convert_fusion.1.refs_0_), channel_id=1, source_target_pairs={{0,1},{1,0},{2,3},{3,2},{4,5},{5,4},{6,7},{7,6},{8,9},{9,8},{10,11... | collective-permute-start | bytes 245768 | tf_op jit(solution)/shard_map/ppermute | solution.py:654
  54.5 1.8 %collective-permute-done.22.refs_3_ = bf16[64,640]{1,0:T(8,128)(2,1)S(1)} collective-permute-done((bf16[64,640]{1,0:T(8,128)(2,1)S(1)}, bf16[64,640]{1,0:T(8,128)(2,1)S(1)}, u32[]{:S(2)}, u32[]{:S(2)}) %collective-permute-start.22) | collective-permute-done | bytes 81952 | tf_op jit(solution)/shard_map/ppermute | solution.py:654
  56.3 1.4 %collective-permute-start.26 = (bf16[72,1152]{1,0:T(8,128)(2,1)S(1)}, bf16[72,1152]{1,0:T(8,128)(2,1)S(1)}, u32[]{:S(2)}, u32[]{:S(2)}) collective-permute-start(bf16[72,1152]{1,0:T(8,128)(2,1)S(1)} %add_convert_fusion), channel_id=1, source_target_pairs={{0,24},{4,28},{8,16},{12,20},{16,8},{20,12},{24,0},{28,4},{1,25},{... | collective-permute-start | bytes 497672 | tf_op jit(solution)/shard_map/ppermute | solution.py:654
  61.4 1.4 %collective-permute-start.13 = (bf16[64,640]{1,0:T(8,128)(2,1)S(1)}, bf16[64,640]{1,0:T(8,128)(2,1)S(1)}, u32[]{:S(2)}, u32[]{:S(2)}) collective-permute-start(bf16[64,640]{1,0:T(8,128)(2,1)S(1)} %copy-done.23), channel_id=1, source_target_pairs={{0,3},{1,2},{2,1},{3,0},{4,7},{5,6},{6,5},{7,4},{8,11},{9,10},{10,... | collective-permute-start | bytes 245768 | tf_op jit(solution)/shard_map/ppermute | solution.py:654
  62.9 17.0 %shard_map.233 = (f32[64,640]{1,0:T(8,128)}, bf16[64,640]{1,0:T(8,128)(2,1)}, bf16[4,144,384]{2,1,0:T(8,128)(2,1)}, bf16[4,144,384]{2,1,0:T(8,128)(2,1)}) custom-call(bf16[64,640]{1,0:T(8,128)(2,1)} %copy-done.15, bf16[64,640]{1,0:T(8,128)(2,1)} %copy-done.28, bf16[64,640]{1,0:T(8,128)(2,1)} %copy-done.27, bf16[64,640]{1,0:T(8,128)(2,1)} %copy-done.26, ...), custom_call_target="tpu_custom_call" | custom-call | flops 19549999104 | bytes 1048576 | tf_op jit(solution)/shard_map/pallas_call | solution.py:114
  80.2 2.5 %collective-permute-start.16 = (bf16[64,640]{1,0:T(8,128)(2,1)S(1)}, bf16[64,640]{1,0:T(8,128)(2,1)S(1)}, u32[]{:S(2)}, u32[]{:S(2)}) collective-permute-start(bf16[64,640]{1,0:T(8,128)(2,1)S(1)} %add_convert_fusion.2.refs_4_), channel_id=1, source_target_pairs={{0,3},{1,2},{2,1},{3,0},{4,7},{5,6},{6,5},{7,4},{8,11},{9,10},{10,... | collective-permute-start | bytes 245768 | tf_op jit(solution)/shard_map/ppermute | solution.py:654
  82.7 1.9 %collective-permute-start.14 = (bf16[64,640]{1,0:T(8,128)(2,1)S(1)}, bf16[64,640]{1,0:T(8,128)(2,1)S(1)}, u32[]{:S(2)}, u32[]{:S(2)}) collective-permute-start(bf16[64,640]{1,0:T(8,128)(2,1)S(1)} %add_convert_fusion.2.refs_4_), channel_id=1, source_target_pairs={{0,1},{1,0},{2,3},{3,2},{4,5},{5,4},{6,7},{7,6},{8,9},{9,8},{10,11... | collective-permute-start | bytes 245768 | tf_op jit(solution)/shard_map/ppermute | solution.py:654
  84.9 1.7 %collective-permute-start.30 = (bf16[144,384]{1,0:T(8,128)(2,1)S(1)}, bf16[144,384]{1,0:T(8,128)(2,1)S(1)}, u32[]{:S(2)}, u32[]{:S(2)}) collective-permute-start(bf16[144,384]{1,0:T(8,128)(2,1)S(1)} %get-tuple-element.158), channel_id=1, source_target_pairs={{0,24},{4,28},{8,16},{12,20},{16,8},{20,12},{24,0},{28,4},{1,25},{... | collective-permute-start | bytes 331784 | tf_op jit(solution)/shard_map/ppermute | solution.py:654
  88.6 2.1 %collective-permute-done.15.refs_6_ = bf16[64,640]{1,0:T(8,128)(2,1)S(1)} collective-permute-done((bf16[64,640]{1,0:T(8,128)(2,1)S(1)}, bf16[64,640]{1,0:T(8,128)(2,1)S(1)}, u32[]{:S(2)}, u32[]{:S(2)}) %collective-permute-start.15) | collective-permute-done | bytes 81952 | tf_op jit(solution)/shard_map/ppermute | solution.py:654
  92.8 2.5 %collective-permute-start.36 = (bf16[80,384]{1,0:T(8,128)(2,1)S(1)}, bf16[80,384]{1,0:T(8,128)(2,1)S(1)}, u32[]{:S(2)}, u32[]{:S(2)}) collective-permute-start(bf16[80,384]{1,0:T(8,128)(2,1)S(1)} %add_convert_fusion.3), channel_id=1, source_target_pairs={{0,3},{1,2},{2,1},{3,0},{4,7},{5,6},{6,5},{7,4},{8,11},{9,10},{10,... | collective-permute-start | bytes 184328 | tf_op jit(solution)/shard_map/ppermute | solution.py:654
  97.3 2.0 %shard_map.234.refs_0_ = bf16[64,640]{1,0:T(8,128)(2,1)S(1)} custom-call(f32[144,384]{1,0:T(8,128)S(1)} %get-tuple-element.130.refs_0_, bf16[144,384]{1,0:T(8,128)(2,1)S(1)} %collective-permute-done.28.refs_1_, bf16[144,384]{1,0:T(8,128)(2,1)S(1)} %collective-permute-done.29.refs_2_, bf16[144,384]{1,0:T(8,128)(2,1)S(1)} %collective-permute-done.30.refs_3_, ...), custom_call_target="tpu_custom_call" | custom-call | flops 2300000000 | bytes 1048576 | tf_op jit(solution)/shard_map/pallas_call | solution.py:114
  99.4 2.2 %collective-permute-done.35 = bf16[80,384]{1,0:T(8,128)(2,1)S(1)} collective-permute-done((bf16[80,384]{1,0:T(8,128)(2,1)S(1)}, bf16[80,384]{1,0:T(8,128)(2,1)S(1)}, u32[]{:S(2)}, u32[]{:S(2)}) %collective-permute-start.35) | collective-permute-done | bytes 61472 | tf_op jit(solution)/shard_map/ppermute | solution.py:654
  101.7 1.9 %collective-permute-start.39 = (bf16[4,80,384]{2,1,0:T(8,128)(2,1)S(1)}, bf16[4,80,384]{2,1,0:T(8,128)(2,1)S(1)}, u32[]{:S(2)}, u32[]{:S(2)}) collective-permute-start(bf16[4,80,384]{2,1,0:T(8,128)(2,1)S(1)} %get-tuple-element.163.refs_1_), channel_id=1, source_target_pairs={{0,24},{4,28},{8,16},{12,20},{16,8},{20,12},{24,0},{28,4},{1,25},{... | collective-permute-start | bytes 737288 | tf_op jit(solution)/shard_map/ppermute | solution.py:654
  105.2 2.5 %collective-permute-start.33 = (bf16[64,640]{1,0:T(8,128)(2,1)S(1)}, bf16[64,640]{1,0:T(8,128)(2,1)S(1)}, u32[]{:S(2)}, u32[]{:S(2)}) collective-permute-start(bf16[64,640]{1,0:T(8,128)(2,1)S(1)} %shard_map.234.refs_0_), channel_id=1, source_target_pairs={{0,3},{1,2},{2,1},{3,0},{4,7},{5,6},{6,5},{7,4},{8,11},{9,10},{10,... | collective-permute-start | bytes 245768 | tf_op jit(solution)/shard_map/ppermute | solution.py:654
  107.7 1.7 %shard_map.236 = (f32[576,384]{1,0:T(8,128)}, f32[576,384]{1,0:T(8,128)}, f32[576,384]{1,0:T(8,128)}) custom-call(bf16[72,1152]{1,0:T(8,128)(2,1)S(1)} %add_convert_fusion, bf16[72,1152]{1,0:T(8,128)(2,1)S(1)} %collective-permute-done.24.refs_1_, bf16[72,1152]{1,0:T(8,128)(2,1)S(1)} %collective-permute-done.25.refs_2_, ...), custom_call_target="tpu_custom_call" | custom-call | flops 2300000000 | bytes 1048576 | tf_op jit(solution)/shard_map/pallas_call | solution.py:114
  109.5 2.1 %collective-permute-done.39.refs_4_ = bf16[4,80,384]{2,1,0:T(8,128)(2,1)S(1)} collective-permute-done((bf16[4,80,384]{2,1,0:T(8,128)(2,1)S(1)}, bf16[4,80,384]{2,1,0:T(8,128)(2,1)S(1)}, u32[]{:S(2)}, u32[]{:S(2)}) %collective-permute-start.39) | collective-permute-done | bytes 245792 | tf_op jit(solution)/shard_map/ppermute | solution.py:654
  111.6 3.7 %collective-permute-done.38.refs_3_ = bf16[4,80,384]{2,1,0:T(8,128)(2,1)S(1)} collective-permute-done((bf16[4,80,384]{2,1,0:T(8,128)(2,1)S(1)}, bf16[4,80,384]{2,1,0:T(8,128)(2,1)S(1)}, u32[]{:S(2)}, u32[]{:S(2)}) %collective-permute-start.38) | collective-permute-done | bytes 245792 | tf_op jit(solution)/shard_map/ppermute | solution.py:654
  118.6 2.9 %shard_map.237 = (f32[576,576]{1,0:T(8,128)}, f32[576,576]{1,0:T(8,128)}, f32[192,576]{1,0:T(8,128)}, f32[192,576]{1,0:T(8,128)}, f32[576]{0:T(1024)}, /*index=5*/f32[576]{0:T(1024)}) custom-call(bf16[576]{0:T(1024)(128)(2,1)S(1)} %copy-done.4, bf16[4,80,384]{2,1,0:T(8,128)(2,1)S(1)} %get-tuple-element.163.refs_1_, ...), custom_call_target="tpu_custom_call" | custom-call | flops 3449999872 | bytes 1048576 | tf_op jit(solution)/shard_map/pallas_call | solution.py:114
  (131 shorter events, 20.0 us)
Async XLA Ops:
  4.0 9.9 %collective-permute-start.5 = (bf16[256,384]{1,0:T(8,128)(2,1)}, bf16[256,384]{1,0:T(8,128)(2,1)S(1)}, u32[]{:S(2)}, u32[]{:S(2)}) collective-permute-start(bf16[256,384]{1,0:T(8,128)(2,1)} %get-tuple-element.87.refs_0_.refs_19_), channel_id=1, source_target_pairs={{0,24},{4,28},{8,16},{12,20},{16,8},{20,12},{24,0},{28,4},{1,25},{... | collective-permute-start | bytes 589832 | tf_op jit(solution)/shard_map/ppermute | solution.py:654
  8.0 9.3 %collective-permute-start.4 = (bf16[256,384]{1,0:T(8,128)(2,1)}, bf16[256,384]{1,0:T(8,128)(2,1)S(1)}, u32[]{:S(2)}, u32[]{:S(2)}) collective-permute-start(bf16[256,384]{1,0:T(8,128)(2,1)} %get-tuple-element.87.refs_0_.refs_19_), channel_id=1, source_target_pairs={{0,16},{4,20},{8,24},{12,28},{16,0},{20,4},{24,8},{28,12},{1,17},{... | collective-permute-start | bytes 589832 | tf_op jit(solution)/shard_map/ppermute | solution.py:654
  8.5 9.1 %collective-permute-start.3 = (bf16[256,384]{1,0:T(8,128)(2,1)}, bf16[256,384]{1,0:T(8,128)(2,1)S(1)}, u32[]{:S(2)}, u32[]{:S(2)}) collective-permute-start(bf16[256,384]{1,0:T(8,128)(2,1)} %get-tuple-element.87.refs_0_.refs_19_), channel_id=1, source_target_pairs={{0,8},{4,12},{8,0},{12,4},{16,24},{20,28},{24,16},{28,20},{1,9},{5... | collective-permute-start | bytes 589832 | tf_op jit(solution)/shard_map/ppermute | solution.py:654
  17.8 18.4 %collective-permute-start.2 = (bf16[144,256]{1,0:T(8,128)(2,1)S(1)}, bf16[144,256]{1,0:T(8,128)(2,1)S(1)}, u32[]{:S(2)}, u32[]{:S(2)}) collective-permute-start(bf16[144,256]{1,0:T(8,128)(2,1)S(1)} %copy-done.17), channel_id=1, source_target_pairs={{0,24},{4,28},{8,16},{12,20},{16,8},{20,12},{24,0},{28,4},{1,25},{... | collective-permute-start | bytes 221192 | tf_op jit(solution)/shard_map/ppermute | solution.py:654
  19.4 16.8 %collective-permute-start.1 = (bf16[144,256]{1,0:T(8,128)(2,1)S(1)}, bf16[144,256]{1,0:T(8,128)(2,1)S(1)}, u32[]{:S(2)}, u32[]{:S(2)}) collective-permute-start(bf16[144,256]{1,0:T(8,128)(2,1)S(1)} %copy-done.17), channel_id=1, source_target_pairs={{0,16},{4,20},{8,24},{12,28},{16,0},{20,4},{24,8},{28,12},{1,17},{... | collective-permute-start | bytes 221192 | tf_op jit(solution)/shard_map/ppermute | solution.py:654
  20.9 15.4 %collective-permute-start = (bf16[144,256]{1,0:T(8,128)(2,1)S(1)}, bf16[144,256]{1,0:T(8,128)(2,1)S(1)}, u32[]{:S(2)}, u32[]{:S(2)}) collective-permute-start(bf16[144,256]{1,0:T(8,128)(2,1)S(1)} %copy-done.17), channel_id=1, source_target_pairs={{0,8},{4,12},{8,0},{12,4},{16,24},{20,28},{24,16},{28,20},{1,9},{5... | collective-permute-start | bytes 221192 | tf_op jit(solution)/shard_map/ppermute | solution.py:654
  36.4 23.9 %collective-permute-start.23 = (bf16[4,144,256]{2,1,0:T(8,128)(2,1)S(1)}, bf16[4,144,256]{2,1,0:T(8,128)(2,1)S(1)}, u32[]{:S(2)}, u32[]{:S(2)}) collective-permute-start(bf16[4,144,256]{2,1,0:T(8,128)(2,1)S(1)} %pad_maximum_fusion.3), channel_id=1, source_target_pairs={{0,4},{4,0},{8,12},{12,8},{16,20},{20,16},{24,28},{28,24},{1,5},{5... | collective-permute-start | bytes 884744 | tf_op jit(solution)/shard_map/ppermute | solution.py:654
  36.9 6.2 %collective-permute-start.17 = (bf16[64,640]{1,0:T(8,128)(2,1)}, bf16[64,640]{1,0:T(8,128)(2,1)S(1)}, u32[]{:S(2)}, u32[]{:S(2)}) collective-permute-start(bf16[64,640]{1,0:T(8,128)(2,1)} %get-tuple-element.117), channel_id=1, source_target_pairs={{0,1},{1,0},{2,3},{3,2},{4,5},{5,4},{6,7},{7,6},{8,9},{9,8},{10,11... | collective-permute-start | bytes 245768 | tf_op jit(solution)/shard_map/ppermute | solution.py:654
  38.5 9.6 %collective-permute-start.18 = (bf16[64,640]{1,0:T(8,128)(2,1)}, bf16[64,640]{1,0:T(8,128)(2,1)S(1)}, u32[]{:S(2)}, u32[]{:S(2)}) collective-permute-start(bf16[64,640]{1,0:T(8,128)(2,1)} %get-tuple-element.118), channel_id=1, source_target_pairs={{0,2},{1,3},{2,0},{3,1},{4,6},{5,7},{6,4},{7,5},{8,10},{9,11},{10,... | collective-permute-start | bytes 245768 | tf_op jit(solution)/shard_map/ppermute | solution.py:654
  41.1 8.5 %collective-permute-start.19 = (bf16[64,640]{1,0:T(8,128)(2,1)}, bf16[64,640]{1,0:T(8,128)(2,1)S(1)}, u32[]{:S(2)}, u32[]{:S(2)}) collective-permute-start(bf16[64,640]{1,0:T(8,128)(2,1)} %get-tuple-element.119), channel_id=1, source_target_pairs={{0,3},{1,2},{2,1},{3,0},{4,7},{5,6},{6,5},{7,4},{8,11},{9,10},{10,... | collective-permute-start | bytes 245768 | tf_op jit(solution)/shard_map/ppermute | solution.py:654
  41.6 10.6 %collective-permute-start.8 = (bf16[72,1152]{1,0:T(8,128)(2,1)S(1)}, bf16[72,1152]{1,0:T(8,128)(2,1)S(1)}, u32[]{:S(2)}, u32[]{:S(2)}) collective-permute-start(bf16[72,1152]{1,0:T(8,128)(2,1)S(1)} %get-tuple-element.155), channel_id=1, source_target_pairs={{0,8},{4,12},{8,0},{12,4},{16,24},{20,28},{24,16},{28,20},{1,9},{5... | collective-permute-start | bytes 497672 | tf_op jit(solution)/shard_map/ppermute | solution.py:654
  43.1 9.1 %collective-permute-start.10 = (bf16[72,1152]{1,0:T(8,128)(2,1)S(1)}, bf16[72,1152]{1,0:T(8,128)(2,1)S(1)}, u32[]{:S(2)}, u32[]{:S(2)}) collective-permute-start(bf16[72,1152]{1,0:T(8,128)(2,1)S(1)} %get-tuple-element.156), channel_id=1, source_target_pairs={{0,24},{4,28},{8,16},{12,20},{16,8},{20,12},{24,0},{28,4},{1,25},{... | collective-permute-start | bytes 497672 | tf_op jit(solution)/shard_map/ppermute | solution.py:654
  49.6 6.6 %collective-permute-start.22 = (bf16[64,640]{1,0:T(8,128)(2,1)S(1)}, bf16[64,640]{1,0:T(8,128)(2,1)S(1)}, u32[]{:S(2)}, u32[]{:S(2)}) collective-permute-start(bf16[64,640]{1,0:T(8,128)(2,1)S(1)} %add_convert_fusion.1.refs_0_), channel_id=1, source_target_pairs={{0,3},{1,2},{2,1},{3,0},{4,7},{5,6},{6,5},{7,4},{8,11},{9,10},{10,... | collective-permute-start | bytes 245768 | tf_op jit(solution)/shard_map/ppermute | solution.py:654
  52.2 6.9 %collective-permute-start.20 = (bf16[64,640]{1,0:T(8,128)(2,1)S(1)}, bf16[64,640]{1,0:T(8,128)(2,1)S(1)}, u32[]{:S(2)}, u32[]{:S(2)}) collective-permute-start(bf16[64,640]{1,0:T(8,128)(2,1)S(1)} %add_convert_fusion.1.refs_0_), channel_id=1, source_target_pairs={{0,1},{1,0},{2,3},{3,2},{4,5},{5,4},{6,7},{7,6},{8,9},{9,8},{10,11... | collective-permute-start | bytes 245768 | tf_op jit(solution)/shard_map/ppermute | solution.py:654
  54.2 7.2 %collective-permute-start.11 = (bf16[64,640]{1,0:T(8,128)(2,1)S(1)}, bf16[64,640]{1,0:T(8,128)(2,1)S(1)}, u32[]{:S(2)}, u32[]{:S(2)}) collective-permute-start(bf16[64,640]{1,0:T(8,128)(2,1)S(1)} %copy-done.25), channel_id=1, source_target_pairs={{0,1},{1,0},{2,3},{3,2},{4,5},{5,4},{6,7},{7,6},{8,9},{9,8},{10,11... | collective-permute-start | bytes 245768 | tf_op jit(solution)/shard_map/ppermute | solution.py:654
  56.3 23.7 %collective-permute-start.26 = (bf16[72,1152]{1,0:T(8,128)(2,1)S(1)}, bf16[72,1152]{1,0:T(8,128)(2,1)S(1)}, u32[]{:S(2)}, u32[]{:S(2)}) collective-permute-start(bf16[72,1152]{1,0:T(8,128)(2,1)S(1)} %add_convert_fusion), channel_id=1, source_target_pairs={{0,24},{4,28},{8,16},{12,20},{16,8},{20,12},{24,0},{28,4},{1,25},{... | collective-permute-start | bytes 497672 | tf_op jit(solution)/shard_map/ppermute | solution.py:654
  58.3 21.7 %collective-permute-start.25 = (bf16[72,1152]{1,0:T(8,128)(2,1)S(1)}, bf16[72,1152]{1,0:T(8,128)(2,1)S(1)}, u32[]{:S(2)}, u32[]{:S(2)}) collective-permute-start(bf16[72,1152]{1,0:T(8,128)(2,1)S(1)} %add_convert_fusion), channel_id=1, source_target_pairs={{0,16},{4,20},{8,24},{12,28},{16,0},{20,4},{24,8},{28,12},{1,17},{... | collective-permute-start | bytes 497672 | tf_op jit(solution)/shard_map/ppermute | solution.py:654
  59.1 20.9 %collective-permute-start.24 = (bf16[72,1152]{1,0:T(8,128)(2,1)S(1)}, bf16[72,1152]{1,0:T(8,128)(2,1)S(1)}, u32[]{:S(2)}, u32[]{:S(2)}) collective-permute-start(bf16[72,1152]{1,0:T(8,128)(2,1)S(1)} %add_convert_fusion), channel_id=1, source_target_pairs={{0,8},{4,12},{8,0},{12,4},{16,24},{20,28},{24,16},{28,20},{1,9},{5... | collective-permute-start | bytes 497672 | tf_op jit(solution)/shard_map/ppermute | solution.py:654
  60.3 19.6 %collective-permute-start.12 = (bf16[64,640]{1,0:T(8,128)(2,1)S(1)}, bf16[64,640]{1,0:T(8,128)(2,1)S(1)}, u32[]{:S(2)}, u32[]{:S(2)}) collective-permute-start(bf16[64,640]{1,0:T(8,128)(2,1)S(1)} %copy-done.24), channel_id=1, source_target_pairs={{0,2},{1,3},{2,0},{3,1},{4,6},{5,7},{6,4},{7,5},{8,10},{9,11},{10,... | collective-permute-start | bytes 245768 | tf_op jit(solution)/shard_map/ppermute | solution.py:654
  61.4 18.5 %collective-permute-start.13 = (bf16[64,640]{1,0:T(8,128)(2,1)S(1)}, bf16[64,640]{1,0:T(8,128)(2,1)S(1)}, u32[]{:S(2)}, u32[]{:S(2)}) collective-permute-start(bf16[64,640]{1,0:T(8,128)(2,1)S(1)} %copy-done.23), channel_id=1, source_target_pairs={{0,3},{1,2},{2,1},{3,0},{4,7},{5,6},{6,5},{7,4},{8,11},{9,10},{10,... | collective-permute-start | bytes 245768 | tf_op jit(solution)/shard_map/ppermute | solution.py:654
  80.2 7.4 %collective-permute-start.16 = (bf16[64,640]{1,0:T(8,128)(2,1)S(1)}, bf16[64,640]{1,0:T(8,128)(2,1)S(1)}, u32[]{:S(2)}, u32[]{:S(2)}) collective-permute-start(bf16[64,640]{1,0:T(8,128)(2,1)S(1)} %add_convert_fusion.2.refs_4_), channel_id=1, source_target_pairs={{0,3},{1,2},{2,1},{3,0},{4,7},{5,6},{6,5},{7,4},{8,11},{9,10},{10,... | collective-permute-start | bytes 245768 | tf_op jit(solution)/shard_map/ppermute | solution.py:654
  82.6 8.1 %collective-permute-start.15 = (bf16[64,640]{1,0:T(8,128)(2,1)S(1)}, bf16[64,640]{1,0:T(8,128)(2,1)S(1)}, u32[]{:S(2)}, u32[]{:S(2)}) collective-permute-start(bf16[64,640]{1,0:T(8,128)(2,1)S(1)} %add_convert_fusion.2.refs_4_), channel_id=1, source_target_pairs={{0,2},{1,3},{2,0},{3,1},{4,6},{5,7},{6,4},{7,5},{8,10},{9,11},{10,... | collective-permute-start | bytes 245768 | tf_op jit(solution)/shard_map/ppermute | solution.py:654
  82.7 8.1 %collective-permute-start.14 = (bf16[64,640]{1,0:T(8,128)(2,1)S(1)}, bf16[64,640]{1,0:T(8,128)(2,1)S(1)}, u32[]{:S(2)}, u32[]{:S(2)}) collective-permute-start(bf16[64,640]{1,0:T(8,128)(2,1)S(1)} %add_convert_fusion.2.refs_4_), channel_id=1, source_target_pairs={{0,1},{1,0},{2,3},{3,2},{4,5},{5,4},{6,7},{7,6},{8,9},{9,8},{10,11... | collective-permute-start | bytes 245768 | tf_op jit(solution)/shard_map/ppermute | solution.py:654
  84.9 6.6 %collective-permute-start.30 = (bf16[144,384]{1,0:T(8,128)(2,1)S(1)}, bf16[144,384]{1,0:T(8,128)(2,1)S(1)}, u32[]{:S(2)}, u32[]{:S(2)}) collective-permute-start(bf16[144,384]{1,0:T(8,128)(2,1)S(1)} %get-tuple-element.158), channel_id=1, source_target_pairs={{0,24},{4,28},{8,16},{12,20},{16,8},{20,12},{24,0},{28,4},{1,25},{... | collective-permute-start | bytes 331784 | tf_op jit(solution)/shard_map/ppermute | solution.py:654
  90.7 17.0 %collective-permute-start.40 = (bf16[4,72,1152]{2,1,0:T(8,128)(2,1)S(1)}, bf16[4,72,1152]{2,1,0:T(8,128)(2,1)S(1)}, u32[]{:S(2)}, u32[]{:S(2)}) collective-permute-start(bf16[4,72,1152]{2,1,0:T(8,128)(2,1)S(1)} %pad_maximum_fusion.2), channel_id=1, source_target_pairs={{0,4},{4,0},{8,12},{12,8},{16,20},{20,16},{24,28},{28,24},{1,5},{5... | collective-permute-start | bytes 1990664 | tf_op jit(solution)/shard_map/ppermute | solution.py:654
  92.8 6.5 %collective-permute-start.36 = (bf16[80,384]{1,0:T(8,128)(2,1)S(1)}, bf16[80,384]{1,0:T(8,128)(2,1)S(1)}, u32[]{:S(2)}, u32[]{:S(2)}) collective-permute-start(bf16[80,384]{1,0:T(8,128)(2,1)S(1)} %add_convert_fusion.3), channel_id=1, source_target_pairs={{0,3},{1,2},{2,1},{3,0},{4,7},{5,6},{6,5},{7,4},{8,11},{9,10},{10,... | collective-permute-start | bytes 184328 | tf_op jit(solution)/shard_map/ppermute | solution.py:654
  95.3 6.3 %collective-permute-start.35 = (bf16[80,384]{1,0:T(8,128)(2,1)S(1)}, bf16[80,384]{1,0:T(8,128)(2,1)S(1)}, u32[]{:S(2)}, u32[]{:S(2)}) collective-permute-start(bf16[80,384]{1,0:T(8,128)(2,1)S(1)} %add_convert_fusion.3), channel_id=1, source_target_pairs={{0,2},{1,3},{2,0},{3,1},{4,6},{5,7},{6,4},{7,5},{8,10},{9,11},{10,... | collective-permute-start | bytes 184328 | tf_op jit(solution)/shard_map/ppermute | solution.py:654
  101.7 9.9 %collective-permute-start.39 = (bf16[4,80,384]{2,1,0:T(8,128)(2,1)S(1)}, bf16[4,80,384]{2,1,0:T(8,128)(2,1)S(1)}, u32[]{:S(2)}, u32[]{:S(2)}) collective-permute-start(bf16[4,80,384]{2,1,0:T(8,128)(2,1)S(1)} %get-tuple-element.163.refs_1_), channel_id=1, source_target_pairs={{0,24},{4,28},{8,16},{12,20},{16,8},{20,12},{24,0},{28,4},{1,25},{... | collective-permute-start | bytes 737288 | tf_op jit(solution)/shard_map/ppermute | solution.py:654
  103.6 11.7 %collective-permute-start.38 = (bf16[4,80,384]{2,1,0:T(8,128)(2,1)S(1)}, bf16[4,80,384]{2,1,0:T(8,128)(2,1)S(1)}, u32[]{:S(2)}, u32[]{:S(2)}) collective-permute-start(bf16[4,80,384]{2,1,0:T(8,128)(2,1)S(1)} %get-tuple-element.163.refs_1_), channel_id=1, source_target_pairs={{0,16},{4,20},{8,24},{12,28},{16,0},{20,4},{24,8},{28,12},{1,17},{... | collective-permute-start | bytes 737288 | tf_op jit(solution)/shard_map/ppermute | solution.py:654
  103.9 11.4 %collective-permute-start.37 = (bf16[4,80,384]{2,1,0:T(8,128)(2,1)S(1)}, bf16[4,80,384]{2,1,0:T(8,128)(2,1)S(1)}, u32[]{:S(2)}, u32[]{:S(2)}) collective-permute-start(bf16[4,80,384]{2,1,0:T(8,128)(2,1)S(1)} %get-tuple-element.163.refs_1_), channel_id=1, source_target_pairs={{0,8},{4,12},{8,0},{12,4},{16,24},{20,28},{24,16},{28,20},{1,9},{5... | collective-permute-start | bytes 737288 | tf_op jit(solution)/shard_map/ppermute | solution.py:654
  105.2 10.2 %collective-permute-start.33 = (bf16[64,640]{1,0:T(8,128)(2,1)S(1)}, bf16[64,640]{1,0:T(8,128)(2,1)S(1)}, u32[]{:S(2)}, u32[]{:S(2)}) collective-permute-start(bf16[64,640]{1,0:T(8,128)(2,1)S(1)} %shard_map.234.refs_0_), channel_id=1, source_target_pairs={{0,3},{1,2},{2,1},{3,0},{4,7},{5,6},{6,5},{7,4},{8,11},{9,10},{10,... | collective-permute-start | bytes 245768 | tf_op jit(solution)/shard_map/ppermute | solution.py:654
  107.7 7.7 %collective-permute-start.32 = (bf16[64,640]{1,0:T(8,128)(2,1)S(1)}, bf16[64,640]{1,0:T(8,128)(2,1)S(1)}, u32[]{:S(2)}, u32[]{:S(2)}) collective-permute-start(bf16[64,640]{1,0:T(8,128)(2,1)S(1)} %shard_map.234.refs_0_), channel_id=1, source_target_pairs={{0,2},{1,3},{2,0},{3,1},{4,6},{5,7},{6,4},{7,5},{8,10},{9,11},{10,... | collective-permute-start | bytes 245768 | tf_op jit(solution)/shard_map/ppermute | solution.py:654
  (39 other events, 335.0 us)
